TPU v7x, 128 devices: a whole 4x4x4 slice. The times are simulated.
128 devices in a mesh: path: 8 (over z, x_lo), trade: 16 (over x_hi, y, core).
Axes of the slice: x: 4 (x_hi: 2, x_lo: 2; x = x_hi * 2 + x_lo), y: 4, z: 4, core: 2. Of those that a mesh axis runs over, the one named last changes fastest.
Arguments:
- factors: bfloat16 [32, 8, 1024], P(None, None, 'path'), may hold values from -5 to 5
- loadings: bfloat16 [32, 8, 65536], P(None, None, 'trade'), may hold values from -0.5 to 0.5
- notional: float32 [65536], P('trade'), may hold values from -1 to 1
- strike: float32 [65536], P('trade'), may hold values from 0.5 to 1.5
- date_weight: float32 [32], replicated, may hold values from 0.3 to 3
- loss_spanning: float32 [256], replicated, may hold values from 0.2 to 0.9
- loss_local: float32 [2048], P('trade'), may hold values from 0.2 to 0.9
- trade_slot: int32 [65536], P('trade'), may hold values from 0 to 255
- span_list: int32 [2048], P('trade'), may hold values from 0 to 255, as said below
Outputs:
- loading_grad: float32 [32, 8, 65536], P('path', None, 'trade')
- factor_grad: float32 [32, 8, 1024], P('trade', None, 'path')
Inputs may be any that keep to these rules, and one draw needn't show every extreme that they name: `trade_slot`: slot s < 128 of a trade shard holds that shard's spanning set from span_list; slot 128 + i holds the shard's i-th local set. `span_list`: the 128 entries of one trade shard are distinct spanning set ids.
All inputs are finite; a program needn't handle non-finite values.
Results may differ from a plain program's by a relative error of at most 0.0021.
Values may be sent and summed in bfloat16 or wider, within the bound.
No kernel may reach another device: no remote copies, remote signals or barrier semaphores. Data moves between devices by JAX's collectives and lax.ppermute only.
A program may use at most 64 MiB of HBM per device.

v0:
```python
import math

import jax
import jax.numpy as jnp
from jax import lax
from jax.sharding import PartitionSpec as P

smoothing = 0.5


def price(factor_block, loading_block):
    exponent = jnp.einsum(
        "bfp,bfk->bpk", factor_block, loading_block, preferred_element_type=jnp.float32
    )
    return jnp.exp(exponent)


def on_device(
    factors,
    loadings,
    notional,
    strike,
    date_weight,
    loss_spanning,
    loss_local,
    trade_slot,
    span_list,
):
    path_total = lax.axis_size("path") * factors.shape[2]
    date_count = factors.shape[0]
    factor_count = factors.shape[1]
    path_local = factors.shape[2]
    trade_local = loadings.shape[2]
    span_local = span_list.shape[0]
    span_count = loss_spanning.shape[0]
    slot_count = span_local + loss_local.shape[0]
    dates_per_step = math.gcd(date_count, max(1, 512 // path_local))
    block_count = date_count // dates_per_step
    slot_table = (trade_slot[:, None] == jnp.arange(slot_count, dtype=jnp.int32)[None, :]).astype(
        jnp.bfloat16
    )
    set_match = span_list[:, None] == jnp.arange(span_count, dtype=jnp.int32)[None, :]
    set_table = set_match.astype(jnp.float32)
    set_select = set_match.astype(jnp.bfloat16)
    factor_blocks = factors.reshape(block_count, dates_per_step, factor_count, path_local)
    loading_blocks = loadings.reshape(block_count, dates_per_step, factor_count, trade_local)
    weight_blocks = date_weight.reshape(block_count, dates_per_step)

    def forward(operands):
        factor_block, loading_block, weight_block = operands
        growth = price(factor_block, loading_block)
        values = (notional * (growth - strike)).astype(jnp.bfloat16)
        partial_sums = jnp.einsum(
            "bpk,ks->bps", values, slot_table, preferred_element_type=jnp.float32
        )
        span_part = jnp.einsum(
            "bps,sn->bpn",
            partial_sums[:, :, :span_local],
            set_table,
            precision=lax.Precision.HIGHEST,
            preferred_element_type=jnp.float32,
        )
        local_weight = (
            weight_block[:, None, None]
            * loss_local
            * jax.nn.sigmoid(partial_sums[:, :, span_local:] / smoothing)
        ).astype(jnp.bfloat16)
        return (span_part, local_weight)

    span_parts, local_weights = lax.map(forward, (factor_blocks, loading_blocks, weight_blocks))
    span_parts = span_parts.reshape(date_count, path_local, span_count)
    span_total = lax.psum(span_parts, "trade")
    span_weight = (
        date_weight[:, None, None] * loss_spanning * jax.nn.sigmoid(span_total / smoothing)
    ).astype(jnp.bfloat16)
    span_blocks = span_weight.reshape(block_count, dates_per_step, path_local, span_count)

    def adjoint(operands):
        factor_block, loading_block, span_block, local_block = operands
        growth = price(factor_block, loading_block)
        span_slots = jnp.einsum(
            "bpn,sn->bps", span_block, set_select, preferred_element_type=jnp.float32
        ).astype(jnp.bfloat16)
        slot_weight = jnp.concatenate([span_slots, local_block], axis=2)
        trade_weight = jnp.einsum(
            "bps,ks->bpk", slot_weight, slot_table, preferred_element_type=jnp.float32
        )
        sensitivity = (trade_weight * notional * growth).astype(jnp.bfloat16)
        loading_term = jnp.einsum(
            "bfp,bpk->bfk", factor_block, sensitivity, preferred_element_type=jnp.float32
        )
        factor_term = jnp.einsum(
            "bfk,bpk->bfp", loading_block, sensitivity, preferred_element_type=jnp.float32
        )
        return (loading_term, factor_term)

    loading_terms, factor_terms = lax.map(
        adjoint, (factor_blocks, loading_blocks, span_blocks, local_weights)
    )
    loading_terms = loading_terms.reshape(date_count, factor_count, trade_local)
    factor_terms = factor_terms.reshape(date_count, factor_count, path_local)
    loading_grad = (
        lax.psum_scatter(loading_terms, "path", scatter_dimension=0, tiled=True) / path_total
    )
    factor_grad = lax.psum_scatter(factor_terms, "trade", scatter_dimension=0, tiled=True)
    return (loading_grad, factor_grad)


def solution(mesh):
    return jax.shard_map(
        on_device,
        mesh=mesh,
        in_specs=(
            P(None, None, "path"),
            P(None, None, "trade"),
            P("trade"),
            P("trade"),
            P(),
            P(),
            P("trade"),
            P("trade"),
            P("trade"),
        ),
        out_specs=(P("path", None, "trade"), P("trade", None, "path")),
        check_vma=False,
    )
```

profile of v0, /device:TPU:1, one launch (start us, length us, event | category | flops | bytes accessed | tf_op | source)
XLA Modules:
  0.0 445.8 jit_solution(448649677609125940)
XLA Ops:
  8.0 40.7 %while.26 = (s32[]{:T(128)}, f32[8,4,128,256]{3,2,1,0:T(8,128)}, bf16[8,4,128,128]{3,2,1,0:T(8,128)(2,1)S(1)}, f32[4096]{0:T(1024)}, bf16[8,4,8,128]{3,2,1,0:T(8...) while((s32[]{:T(128)}, f32[8,4,128,256]{3,2,1,0:T(8,128)}, ...), condition=%wide.region_1.2_spmd.clone, body=%wide.region_0.1_spmd.clone.sunk | while | flops 1317470720 | bytes 2034405 | solution.py:70
  8.0 3.4 fusion.92
  11.6 1.5 fusion.93
  13.1 3.4 fusion.92
  16.7 1.5 fusion.93
  18.2 3.4 fusion.92
  21.8 1.4 fusion.93
  23.3 3.4 fusion.92
  26.9 1.4 fusion.93
  28.4 3.4 fusion.92
  32.0 1.5 fusion.93
  33.5 3.4 fusion.92
  37.1 1.4 fusion.93
  38.5 3.4 fusion.92
  42.2 1.4 fusion.93
  43.6 3.4 fusion.92
  47.2 1.4 fusion.93
  49.5 152.6 %all-reduce.2.cloned.1.call-done = f32[32,128,256]{2,1,0:T(8,128)} async-done(((f32[32,128,256]{2,1,0:T(8,128)}), f32[32,128,256]{2,1,0:T(8,128)}) %all-reduce.2.cloned.1.call-update) | async-done | bytes 4194320 | tf_op jit(solution)/shard_map/psum | solution.py:72
  202.0 3.3 multiply_convert_fusion.2
  205.4 73.7 %while.27 = (s32[]{:T(128)}, f32[8,4,8,4096]{3,2,1,0:T(8,128)}, f32[8,4,8,128]{3,2,1,0:T(8,128)}, bf16[8,4,8,128]{3,2,1,0:T(8,128)(2,1)}, bf16[8,4,128,256]{3,2,...) while((s32[]{:T(128)}, f32[8,4,8,4096]{3,2,1,0:T(8,128)}, ...), condition=%wide.region_4.5_spmd.clone, body=%wide.region_3.4_spmd.clone.sunk | while | flops 1217003520 | bytes 31395444 | solution.py:97
  207.1 2.6 multiply_convert_fusion.4
  209.7 2.2 fusion.106
  211.8 2.8 fusion.107
  216.3 2.6 multiply_convert_fusion.4
  218.9 2.1 fusion.106
  221.1 2.7 fusion.107
  225.5 2.6 multiply_convert_fusion.4
  228.1 2.2 fusion.106
  230.3 2.7 fusion.107
  234.7 2.6 multiply_convert_fusion.4
  237.3 2.1 fusion.106
  239.5 2.7 fusion.107
  243.9 2.6 multiply_convert_fusion.4
  246.5 2.2 fusion.106
  248.7 2.7 fusion.107
  253.2 2.6 multiply_convert_fusion.4
  255.8 2.2 fusion.106
  257.9 2.7 fusion.107
  261.0 1.4 fusion.105
  262.4 2.6 multiply_convert_fusion.4
  265.0 2.2 fusion.106
  267.2 2.7 fusion.107
  271.6 2.6 multiply_convert_fusion.4
  274.2 2.1 fusion.106
  276.4 2.7 fusion.107
  279.9 92.2 %reduce-scatter.3.cloned.1.call-done = f32[4,8,4096]{2,1,0:T(8,128)} async-done(((f32[32,8,4096]{2,1,0:T(8,128)}), f32[4,8,4096]{2,1,0:T(8,128)}) %reduce-scatter.3.cloned.1.call-update) | async-done | bytes 524304 | tf_op jit(solution)/shard_map/reduce_scatter | solution.py:103
  372.0 1.9 broadcast_multiply_fusion.1
  373.9 65.3 %reduce-scatter.5.cloned.1.call-done = f32[2,8,128]{2,1,0:T(8,128)} async-done(((f32[32,8,128]{2,1,0:T(8,128)}), f32[2,8,128]{2,1,0:T(8,128)}) %reduce-scatter.5.cloned.1.call-update) | async-done | bytes 8208 | tf_op jit(solution)/shard_map/reduce_scatter | solution.py:105
  (101 shorter events, 15.8 us)
Async XLA Ops:
  7.2 194.9 %all-reduce.2.cloned.1.call-start = ((), (), s32[]{:S(2)}) async-start(), calls=%async_computation.2 | async-start | bytes 8388608 | tf_op jit(solution)/shard_map/psum | solution.py:72
  8.0 3.5 copy-start.4
  8.0 3.6 copy-start.2
  13.1 3.4 copy-start.4
  13.1 3.6 copy-start.2
  18.2 3.4 copy-start.4
  18.2 3.6 copy-start.2
  23.3 3.4 copy-start.4
  23.3 3.6 copy-start.2
  28.4 3.5 copy-start.4
  28.4 3.6 copy-start.2
  33.5 3.4 copy-start.4
  33.5 3.6 copy-start.2
  38.5 3.4 copy-start.4
  38.5 3.6 copy-start.2
  43.6 3.5 copy-start.4
  43.6 3.6 copy-start.2
  48.7 0.7 copy-start.5
  48.7 0.7 copy-start.6
  48.7 156.6 %copy-start = (f32[4096]{0:T(1024)S(1)}, f32[4096]{0:T(1024)}, u32[]{:S(2)}) copy-start(f32[4096]{0:T(1024)} %get-tuple-element.416) | copy-start | bytes 49156
  48.7 156.6 %copy-start.1 = (s32[4096]{0:T(1024)S(1)}, s32[4096]{0:T(1024)}, u32[]{:S(2)}) copy-start(s32[4096]{0:T(1024)} %get-tuple-element.417) | copy-start | bytes 49156
  48.7 156.6 %copy-start.3 = (s32[128]{0:T(128)S(1)}, s32[128]{0:T(128)}, u32[]{:S(2)}) copy-start(s32[128]{0:T(128)} %get-tuple-element.421) | copy-start | bytes 1540
  48.7 323.3 %reduce-scatter.3.cloned.1.call-start = ((), (), s32[]{:S(2)}) async-start(), calls=%async_computation.3 | async-start | bytes 4718592 | tf_op jit(solution)/shard_map/reduce_scatter | solution.py:103
  279.1 160.1 %reduce-scatter.5.cloned.1.call-start = ((), (), s32[]{:S(2)}) async-start(), calls=%async_computation.4 | async-start | bytes 139264 | tf_op jit(solution)/shard_map/reduce_scatter | solution.py:105
Sparse Core Ops, SparseCore 0:
  48.8 153.1 all-reduce.1
  279.3 92.7 reduce-scatter.2
  376.3 62.9 reduce-scatter.4
where the time goes:
time: 448 us; the launch traced here: 446 us
  waiting for transfers between devices  311 us (69%)
  matrix products  112 us (25%)
  between operations  13.8 us (3%)
  other arithmetic  6.62 us (1%)
    psum x1, waiting for transfers between devices, on_device(): span_total = lax.psum(span_parts, 'trade')  153 us
    reduce_scatter x1, waiting for transfers between devices, on_device(): lax.psum_scatter(loading_terms, 'path', scatter_dimension=0, tiled=True)  92.2 us
    reduce_scatter x1, waiting for transfers between devices, on_device(): lax.psum_scatter(factor_terms, 'trade', scatter_dimension=0, tiled=True)  65.3 us
    dot_general x8, matrix products, forward(): jnp.einsum('bpk,ks->bps', values, slot_table, preferred_element_type=jnp....  27.3 us
    dot_general x8, matrix products, adjoint(): jnp.einsum('bfk,bpk->bfp', loading_block, sensitivity, preferred_element_...  21.9 us
    dot_general x8, matrix products, price(): jnp.einsum('bfp,bfk->bpk', factor_block, loading_block, preferred_element...  20.9 us
    dot_general x8, matrix products, adjoint(): jnp.einsum('bfp,bpk->bfk', factor_block, sensitivity, preferred_element_t...  17.3 us
    dot_general x8, matrix products, forward(): jnp.einsum('bps,sn->bpn', partial_sums[:, :, :span_local], set_table, pre...  11.6 us
  transfers between devices with their start and end apart: 3, of which 3 were waited for; matrix products, arithmetic and copies ran while one was open for 0% of the time, Pallas kernels for 0%

commit v1 on v0

v1 whole, which is shorter than its diff:
```python
import functools
import math

import jax
import jax.numpy as jnp
from jax import lax
from jax.experimental import pallas as pl
from jax.experimental.pallas import tpu as pltpu
from jax.sharding import PartitionSpec as P

smoothing = 0.5
log2e = math.log2(math.e)
f32 = jnp.float32
bf16 = jnp.bfloat16
nt = (((1,), (1,)), ((), ()))


def pieces(x, count):
    parts = []
    for _ in range(count):
        part = lax.reduce_precision(x, 8, 7)
        parts.append(part.astype(bf16))
        x = x - part
    return parts


def split(x):
    high = x.astype(bf16)
    return high, (x - high.astype(f32)).astype(bf16)


def kernel(
    block,
    weight_ref,
    trade_ref,
    column_ref,
    row_ref,
    loss_ref,
    loading_out,
    factor_out,
    values_ref,
    slot_weight_ref,
):
    shards, _, trades = trade_ref.shape
    paths = column_ref.shape[0]
    factors = row_ref.shape[0]
    slots = slot_weight_ref.shape[2]
    span_local = slots // 2
    span_count = loss_ref.shape[1]
    steps = trades // block
    weight = weight_ref[0, 0]
    column = column_ref[...]
    row = row_ref[...]

    def trade_block(shard, step):
        start = pl.multiple_of(step * block, block)
        return trade_ref[shard, :, pl.ds(start, block)].astype(f32)

    def table_of(slot):
        ids = lax.broadcasted_iota(jnp.int32, (slots, block), 0).astype(f32)
        return jnp.where(ids == slot, 1.0, 0.0).astype(bf16)

    def set_table(shard):
        names = trade_ref[shard, :, pl.ds(0, span_local)].astype(f32)[13:14]
        ids = lax.broadcasted_iota(jnp.int32, (span_count, span_local), 0).astype(f32)
        return jnp.where(ids == names, 1.0, 0.0).astype(bf16)

    def forward(shard, span_total):
        def step_of(step, partial):
            data = trade_block(shard, step)
            both = jnp.concatenate(split(data[:8] * log2e), axis=0)
            exponent = jnp.dot(column, both, preferred_element_type=f32)
            notional = data[9:10] + data[10:11]
            strike = data[11:12] + data[12:13]
            values = (notional * (jnp.exp2(exponent) - strike)).astype(bf16)
            start = pl.multiple_of(shard * trades + step * block, block)
            values_ref[:, pl.ds(start, block)] = values
            return partial + lax.dot_general(
                values, table_of(data[8:9]), nt, preferred_element_type=f32
            )

        partial = lax.fori_loop(0, steps, step_of, jnp.zeros((paths, slots), f32))
        loss = trade_ref[shard, :, pl.ds(span_local, 3 * span_local)].astype(f32)[13:14]
        loss = (
            loss[:, :span_local]
            + loss[:, span_local : 2 * span_local]
            + loss[:, 2 * span_local :]
        )
        local = weight * loss * jax.nn.sigmoid(partial[:, span_local:] / smoothing)
        slot_weight_ref[shard, :, span_local:] = local.astype(bf16)
        table = set_table(shard)
        for part in split(partial[:, :span_local]):
            span_total = span_total + lax.dot_general(
                part, table, nt, preferred_element_type=f32
            )
        return span_total

    span_total = lax.fori_loop(0, shards, forward, jnp.zeros((paths, span_count), f32))
    span_weight = (weight * loss_ref[...] * jax.nn.sigmoid(span_total / smoothing)).astype(bf16)

    def backward(shard, total):
        slot_weight_ref[shard, :, :span_local] = jnp.dot(
            span_weight, set_table(shard), preferred_element_type=f32
        ).astype(bf16)

        def step_of(step, total):
            data = trade_block(shard, step)
            table = table_of(data[8:9])
            trade_weight = jnp.dot(slot_weight_ref[shard], table, preferred_element_type=f32)
            notional = data[9:10] + data[10:11]
            strike = data[11:12] + data[12:13]
            start = pl.multiple_of(shard * trades + step * block, block)
            scaled = values_ref[:, pl.ds(start, block)].astype(f32) + notional * strike
            sensitivity = (trade_weight * scaled).astype(bf16)
            start = pl.multiple_of(step * block, block)
            loading_out[shard, :, pl.ds(start, block)] = jnp.dot(
                row, sensitivity, preferred_element_type=f32
            ).astype(bf16)
            return total + lax.dot_general(
                data[:8].astype(bf16), sensitivity, nt, preferred_element_type=f32
            )

        return lax.fori_loop(0, steps, step_of, total)

    factor_out[...] = lax.fori_loop(0, shards, backward, jnp.zeros((factors, paths), f32))


def price_and_adjoint(weight, trade_data, factor_rows, loss_spanning, block=1024):
    shards, _, trades = trade_data.shape
    factors, paths = factor_rows.shape
    slots = 256
    column = jnp.concatenate([factor_rows, factor_rows], axis=0).T
    vmem = pl.BlockSpec(memory_space=pltpu.VMEM)
    return pl.pallas_call(
        functools.partial(kernel, block),
        out_shape=(
            jax.ShapeDtypeStruct((shards, factors, trades), bf16),
            jax.ShapeDtypeStruct((factors, paths), f32),
        ),
        in_specs=[pl.BlockSpec(memory_space=pltpu.SMEM), vmem, vmem, vmem, vmem],
        out_specs=(vmem, vmem),
        scratch_shapes=[
            pltpu.VMEM((paths, shards * trades), bf16),
            pltpu.VMEM((shards, paths, slots), bf16),
        ],
        compiler_params=pltpu.CompilerParams(vmem_limit_bytes=58 * 2**20),
    )(weight, trade_data, column, factor_rows, loss_spanning)


def on_device(
    factors,
    loadings,
    notional,
    strike,
    date_weight,
    loss_spanning,
    loss_local,
    trade_slot,
    span_list,
):
    path_devices = lax.axis_size("path")
    trade_devices = lax.axis_size("trade")
    path_at = lax.axis_index("path")
    trade_at = lax.axis_index("trade")
    dates, factor_count, chunk = factors.shape
    trades = loadings.shape[2]
    group_dates = dates // path_devices
    quarters = trade_devices // group_dates
    span_local = span_list.shape[0]

    own = lax.dynamic_slice_in_dim(loadings, path_at * group_dates, group_dates, 0)
    lists = jnp.concatenate([span_list.astype(bf16)] + pieces(loss_local, 3))
    lists = jnp.concatenate([lists, jnp.zeros((trades - lists.shape[0],), bf16)])
    zero = jnp.zeros((trades,), bf16)
    extra = jnp.stack(
        [trade_slot.astype(bf16)] + pieces(notional, 2) + pieces(strike, 2) + [lists, zero, zero]
    )
    sent = jnp.concatenate(
        [
            jnp.repeat(own, quarters, axis=0),
            jnp.broadcast_to(extra[None], (trade_devices,) + extra.shape),
        ],
        axis=1,
    )
    trade_data = lax.all_to_all(sent, "trade", 0, 0, tiled=True)

    routes = []
    for turn in range(2):
        route = []
        for a in range(path_devices):
            for b in range(trade_devices):
                date = 2 * b + (a + turn) % 2
                to = (date // group_dates) * trade_devices + (date % group_dates) * quarters + a // 2
                route.append((a * trade_devices + b, to))
        routes.append(route)
    mine = lax.dynamic_slice_in_dim(factors, 2 * trade_at, 2, 0)
    odd_path = path_at % 2 == 1
    odd_date = (trade_at // quarters) % 2 == 1
    first = jnp.where(odd_path, mine[1], mine[0])
    second = jnp.where(odd_path, mine[0], mine[1])
    first = lax.ppermute(first, ("path", "trade"), routes[0])
    second = lax.ppermute(second, ("path", "trade"), routes[1])
    factor_rows = jnp.where(
        odd_date,
        jnp.concatenate([second, first], axis=1),
        jnp.concatenate([first, second], axis=1),
    )

    date_at = path_at * group_dates + trade_at // quarters
    weight = lax.dynamic_slice_in_dim(date_weight, date_at, 1).reshape(1, 1)
    loading_part, factor_part = price_and_adjoint(
        weight, trade_data, factor_rows, loss_spanning[None, :]
    )

    back = [[(to, origin) for origin, to in route] for route in routes]
    left, right = factor_part[:, :chunk], factor_part[:, chunk:]
    first = lax.ppermute(jnp.where(odd_date, right, left), ("path", "trade"), back[0])
    second = lax.ppermute(jnp.where(odd_date, left, right), ("path", "trade"), back[1])
    factor_grad = jnp.where(odd_path, jnp.stack([second, first]), jnp.stack([first, second]))

    loading_part = lax.all_to_all(loading_part, "trade", 0, 0, tiled=True)
    loading_part = loading_part.reshape(group_dates, quarters, factor_count, trades)
    loading_grad = loading_part.astype(f32).sum(axis=1) / (path_devices * chunk)
    return (loading_grad, factor_grad)


def solution(mesh):
    return jax.shard_map(
        on_device,
        mesh=mesh,
        in_specs=(
            P(None, None, "path"),
            P(None, None, "trade"),
            P("trade"),
            P("trade"),
            P(),
            P(),
            P("trade"),
            P("trade"),
            P("trade"),
        ),
        out_specs=(P("path", None, "trade"), P("trade", None, "path")),
        check_vma=False,
    )
```

time: 448 us -> 155 us (0.35)
  waiting for transfers between devices: 311 us -> 25.9 us
  matrix products: 112 us -> 0 us
  Pallas kernels: 0 us -> 82.3 us
  starting transfers between devices: 0.12 us -> 34.6 us
  between operations: 13.8 us -> 0.78 us
    reduce_scatter x2 -> x0, waiting for transfers between devices: 157 us -> none  [the longest x1 92.2 us: on_device(): lax.psum_scatter(loading_terms, 'path', scatter_dimension=0, tiled=True)]
    psum x1 -> x0, waiting for transfers between devices: 153 us -> none  [on_device(): span_total = lax.psum(span_parts, 'trade')]
    dot_general x56 -> x0, matrix products: 112 us -> none  [the longest x8 27.3 us: forward(): jnp.einsum('bpk,ks->bps', values, slot_table, preferred_element_type=jnp....]
    pallas_call x0 -> x1, Pallas kernels: none -> 82.3 us  [price_and_adjoint(): pl.pallas_call(functools.partial(kernel, block), out_shape=(jax.ShapeDtyp...]
    ppermute x0 -> x4, waiting for transfers between devices: none -> 23.5 us  [the longest x1 11.8 us: on_device(): first = lax.ppermute(first, ('path', 'trade'), routes[0])]
    ppermute x0 -> x4, starting transfers between devices: none -> 18.3 us  [the longest x1 6.12 us: on_device(): second = lax.ppermute(second, ('path', 'trade'), routes[1])]
    all_to_all x0 -> x2, starting transfers between devices: none -> 16.3 us  [the longest x1 8.58 us: on_device(): trade_data = lax.all_to_all(sent, 'trade', 0, 0, tiled=True)]
  transfers between devices with their start and end apart: 3 -> 6, of which waited for: 3 -> 5; matrix products, arithmetic and copies ran while one was open for 0% -> 2% of each run, Pallas kernels for 0% -> 0%
where the time goes in v1:
time: 155 us; the launch traced here: 154 us
  Pallas kernels  82.3 us (53%)
  starting transfers between devices  34.6 us (22%)
  waiting for transfers between devices  25.9 us (17%)
  other arithmetic  7.4 us (5%)
  local copies, waits for them, and re-layouts  2.94 us (2%)
    pallas_call x1, Pallas kernels, price_and_adjoint(): pl.pallas_call(functools.partial(kernel, block), out_shape=(jax.ShapeDtyp...  82.3 us
    ppermute x1, waiting for transfers between devices, on_device(): first = lax.ppermute(first, ('path', 'trade'), routes[0])  11.8 us
    all_to_all x1, starting transfers between devices, on_device(): trade_data = lax.all_to_all(sent, 'trade', 0, 0, tiled=True)  8.58 us
    ppermute x1, waiting for transfers between devices, on_device(): lax.ppermute(jnp.where(odd_date, right, left), ('path', 'trade'), back[0])  8.24 us
    all_to_all x1, starting transfers between devices, on_device(): loading_part = lax.all_to_all(loading_part, 'trade', 0, 0, tiled=True)  7.68 us
    ppermute x1, starting transfers between devices, on_device(): second = lax.ppermute(second, ('path', 'trade'), routes[1])  6.12 us
    ppermute x1, starting transfers between devices, on_device(): first = lax.ppermute(first, ('path', 'trade'), routes[0])  5.04 us
    ppermute x1, starting transfers between devices, on_device(): lax.ppermute(jnp.where(odd_date, left, right), ('path', 'trade'), back[1])  4.02 us
  transfers between devices with their start and end apart: 6, of which 5 were waited for; matrix products, arithmetic and copies ran while one was open for 2% of the time, Pallas kernels for 0%

profile of v1, /device:TPU:1, one launch (start us, length us, event | category | flops | bytes accessed | tf_op | source)
XLA Modules:
  0.0 154.0 jit_solution(14787316711303698203)
XLA Ops:
  0.6 0.0 copy-start
  0.7 0.9 convert_element_type.33
  1.5 0.7 fusion.1
  2.3 0.7 fusion.3
  3.1 0.7 convert_element_type.38
  3.7 0.7 fusion.5
  4.4 0.2 dynamic-update-slice
  4.6 0.2 dynamic-update-slice.1
  4.8 0.2 dynamic-update-slice.2
  5.0 0.2 dynamic-update-slice.3
  5.2 0.2 dynamic-update-slice.4
  5.5 0.0 copy-done
  5.5 0.2 stack.45
  5.7 0.1 broadcast_in_dim.17
  5.8 0.1 broadcast_in_dim.15
  5.9 1.5 pad_maximum_fusion
  7.4 0.0 copy-start.3
  7.4 8.6 %all-to-all-start = ((bf16[16,16,4096]{2,1,0:T(8,128)(2,1)}), bf16[16,16,4096]{2,1,0:T(8,128)(2,1)}, u32[]{:S(2)}, u32[]{:S(2)}) async-start(bf16[16,16,4096]{2,1,0:T(8,128)(2,1)} %pad_maximum_fusion), calls=%async_computation | async-start | bytes 4194304 | tf_op jit(solution)/shard_map/all_to_all | solution.py:185
  15.9 0.7 select_bitcast_fusion.1
  16.6 5.0 %collective-permute-start.1 = (bf16[8,128]{1,0:T(8,128)(2,1)S(1)}, bf16[8,128]{1,0:T(8,128)(2,1)S(1)}, u32[]{:S(2)}, u32[]{:S(2)}) collective-permute-start(bf16[8,128]{1,0:T(8,128)(2,1)S(1)} %get-tuple-element.7), channel_id=1, source_target_pairs={{0,0},{1,8},{2,16},{3,24},{4,32},{5,40},{6,48},{7,56},{8,64},{9,72... | collective-permute-start | bytes 6152 | tf_op jit(solution)/shard_map/ppermute | solution.py:201
  21.7 6.1 %collective-permute-start = (bf16[8,128]{1,0:T(8,128)(2,1)S(1)}, bf16[8,128]{1,0:T(8,128)(2,1)S(1)}, u32[]{:S(2)}, u32[]{:S(2)}) collective-permute-start(bf16[8,128]{1,0:T(8,128)(2,1)S(1)} %get-tuple-element.6), channel_id=1, source_target_pairs={{0,4},{1,12},{2,20},{3,28},{4,36},{5,44},{6,52},{7,60},{8,68},{9,7... | collective-permute-start | bytes 6152 | tf_op jit(solution)/shard_map/ppermute | solution.py:202
  27.8 0.0 copy-done.3
  27.8 0.7 dynamic_slice.9
  28.5 11.8 %collective-permute-done.1 = bf16[8,128]{1,0:T(8,128)(2,1)S(1)} collective-permute-done((bf16[8,128]{1,0:T(8,128)(2,1)S(1)}, bf16[8,128]{1,0:T(8,128)(2,1)S(1)}, u32[]{:S(2)}, u32[]{:S(2)}) %collective-permute-start.1) | collective-permute-done | bytes 2080 | tf_op jit(solution)/shard_map/ppermute | solution.py:201
  40.3 1.0 collective-permute-done
  41.4 0.0 copy-start.1
  41.4 0.7 copy.11.column_ref
  42.1 2.4 %all-to-all-done.trade_ref = bf16[16,16,4096]{2,1,0:T(8,128)(2,1)} async-done(((bf16[16,16,4096]{2,1,0:T(8,128)(2,1)}), bf16[16,16,4096]{2,1,0:T(8,128)(2,1)}, u32[]{:S(2)}, u32[]{:S(2)}) %all-to-all-start) | async-done | bytes 2097184 | tf_op jit(solution)/shard_map/all_to_all | solution.py:185
  44.5 0.0 copy-done.1
  44.5 82.3 %shard_map.104 = (bf16[16,8,4096]{2,1,0:T(8,128)(2,1)}, f32[8,256]{1,0:T(8,128)}) custom-call(f32[1,1]{1,0:T(1,128)} %bitcast.weight_ref, bf16[16,16,4096]{2,1,0:T(8,128)(2,1)} %all-to-all-done.trade_ref, bf16[256,16]{1,0:T(8,128)(2,1)} %copy.11.column_ref, bf16[8,256]{1,0:T(8,128)(2,1)} %copy-done.1, f32[1,256]{1,0:T(1,128)} %bitcast.17), custom_call_target="tpu_custom_call" | custom-call | tf_op jit(solution)/shard_map/pallas_call | solution.py:134
  126.9 0.0 copy-start.2
  126.9 7.7 %all-to-all-start.1 = ((bf16[16,8,4096]{2,1,0:T(8,128)(2,1)}), bf16[16,8,4096]{2,1,0:T(8,128)(2,1)S(1)}, u32[]{:S(2)}, u32[]{:S(2)}) async-start(bf16[16,8,4096]{2,1,0:T(8,128)(2,1)} %get-tuple-element.4), calls=%async_computation.1 | async-start | bytes 2097152 | tf_op jit(solution)/shard_map/all_to_all | solution.py:221
  134.5 0.0 copy-done.2
  134.6 3.2 %collective-permute-start.3 = (f32[8,128]{1,0:T(8,128)S(1)}, f32[8,128]{1,0:T(8,128)S(1)}, u32[]{:S(2)}, u32[]{:S(2)}) collective-permute-start(f32[8,128]{1,0:T(8,128)S(1)} %get-tuple-element.13), channel_id=1, source_target_pairs={{0,0},{8,1},{16,2},{24,3},{32,4},{40,5},{48,6},{56,7},{64,8},{72,9... | collective-permute-start | bytes 12296 | tf_op jit(solution)/shard_map/ppermute | solution.py:217
  137.7 4.0 %collective-permute-start.2 = (f32[8,128]{1,0:T(8,128)S(1)}, f32[8,128]{1,0:T(8,128)S(1)}, u32[]{:S(2)}, u32[]{:S(2)}) collective-permute-start(f32[8,128]{1,0:T(8,128)S(1)} %get-tuple-element.12), channel_id=1, source_target_pairs={{4,0},{12,1},{20,2},{28,3},{36,4},{44,5},{52,6},{60,7},{68,8},{76,... | collective-permute-start | bytes 12296 | tf_op jit(solution)/shard_map/ppermute | solution.py:218
  141.8 8.2 %collective-permute-done.3 = f32[8,128]{1,0:T(8,128)S(1)} collective-permute-done((f32[8,128]{1,0:T(8,128)S(1)}, f32[8,128]{1,0:T(8,128)S(1)}, u32[]{:S(2)}, u32[]{:S(2)}) %collective-permute-start.3) | collective-permute-done | bytes 4128 | tf_op jit(solution)/shard_map/ppermute | solution.py:217
  150.0 2.4 %collective-permute-done.2 = f32[8,128]{1,0:T(8,128)S(1)} collective-permute-done((f32[8,128]{1,0:T(8,128)S(1)}, f32[8,128]{1,0:T(8,128)S(1)}, u32[]{:S(2)}, u32[]{:S(2)}) %collective-permute-start.2) | collective-permute-done | bytes 4128 | tf_op jit(solution)/shard_map/ppermute | solution.py:218
  152.4 0.6 maximum_select_fusion
  153.0 0.0 all-to-all-done.1
  153.0 0.2 convert_reduce_fusion
  153.2 0.8 broadcast_multiply_fusion
  (13 shorter events, 0.1 us)
Async XLA Ops:
  0.6 4.8 %copy-start = (bf16[32,8,4096]{2,1,0:T(8,128)(2,1)S(1)}, bf16[32,8,4096]{2,1,0:T(8,128)(2,1)}, u32[]{:S(2)}) copy-start(bf16[32,8,4096]{2,1,0:T(8,128)(2,1)} %param.10) | copy-start | bytes 6291460
  7.4 20.4 %copy-start.3 = (f32[32]{0:T(128)S(1)}, f32[32]{0:T(128)}, u32[]{:S(2)}) copy-start(f32[32]{0:T(128)} %param.13) | copy-start | bytes 388
  7.4 37.2 %all-to-all-start = ((bf16[16,16,4096]{2,1,0:T(8,128)(2,1)}), bf16[16,16,4096]{2,1,0:T(8,128)(2,1)}, u32[]{:S(2)}, u32[]{:S(2)}) async-start(bf16[16,16,4096]{2,1,0:T(8,128)(2,1)} %pad_maximum_fusion), calls=%async_computation | async-start | bytes 4194304 | tf_op jit(solution)/shard_map/all_to_all | solution.py:185
  16.6 23.7 %collective-permute-start.1 = (bf16[8,128]{1,0:T(8,128)(2,1)S(1)}, bf16[8,128]{1,0:T(8,128)(2,1)S(1)}, u32[]{:S(2)}, u32[]{:S(2)}) collective-permute-start(bf16[8,128]{1,0:T(8,128)(2,1)S(1)} %get-tuple-element.7), channel_id=1, source_target_pairs={{0,0},{1,8},{2,16},{3,24},{4,32},{5,40},{6,48},{7,56},{8,64},{9,72... | collective-permute-start | bytes 6152 | tf_op jit(solution)/shard_map/ppermute | solution.py:201
  21.7 19.7 %collective-permute-start = (bf16[8,128]{1,0:T(8,128)(2,1)S(1)}, bf16[8,128]{1,0:T(8,128)(2,1)S(1)}, u32[]{:S(2)}, u32[]{:S(2)}) collective-permute-start(bf16[8,128]{1,0:T(8,128)(2,1)S(1)} %get-tuple-element.6), channel_id=1, source_target_pairs={{0,4},{1,12},{2,20},{3,28},{4,36},{5,44},{6,52},{7,60},{8,68},{9,7... | collective-permute-start | bytes 6152 | tf_op jit(solution)/shard_map/ppermute | solution.py:202
  41.4 3.2 %copy-start.1 = (bf16[8,256]{1,0:T(8,128)(2,1)}, bf16[8,256]{1,0:T(8,128)(2,1)S(1)}, u32[]{:S(2)}) copy-start(bf16[8,256]{1,0:T(8,128)(2,1)S(1)} %maximum_select_fusion.1.row_ref) | copy-start | bytes 12292
  126.9 7.7 %copy-start.2 = (f32[8,256]{1,0:T(8,128)S(1)}, f32[8,256]{1,0:T(8,128)}, u32[]{:S(2)}) copy-start(f32[8,256]{1,0:T(8,128)} %get-tuple-element.5) | copy-start | bytes 24580
  126.9 26.1 %all-to-all-start.1 = ((bf16[16,8,4096]{2,1,0:T(8,128)(2,1)}), bf16[16,8,4096]{2,1,0:T(8,128)(2,1)S(1)}, u32[]{:S(2)}, u32[]{:S(2)}) async-start(bf16[16,8,4096]{2,1,0:T(8,128)(2,1)} %get-tuple-element.4), calls=%async_computation.1 | async-start | bytes 2097152 | tf_op jit(solution)/shard_map/all_to_all | solution.py:221
  134.6 15.4 %collective-permute-start.3 = (f32[8,128]{1,0:T(8,128)S(1)}, f32[8,128]{1,0:T(8,128)S(1)}, u32[]{:S(2)}, u32[]{:S(2)}) collective-permute-start(f32[8,128]{1,0:T(8,128)S(1)} %get-tuple-element.13), channel_id=1, source_target_pairs={{0,0},{8,1},{16,2},{24,3},{32,4},{40,5},{48,6},{56,7},{64,8},{72,9... | collective-permute-start | bytes 12296 | tf_op jit(solution)/shard_map/ppermute | solution.py:217
  137.7 14.7 %collective-permute-start.2 = (f32[8,128]{1,0:T(8,128)S(1)}, f32[8,128]{1,0:T(8,128)S(1)}, u32[]{:S(2)}, u32[]{:S(2)}) collective-permute-start(f32[8,128]{1,0:T(8,128)S(1)} %get-tuple-element.12), channel_id=1, source_target_pairs={{4,0},{12,1},{20,2},{28,3},{36,4},{44,5},{52,6},{60,7},{68,8},{76,... | collective-permute-start | bytes 12296 | tf_op jit(solution)/shard_map/ppermute | solution.py:218

commit v2 on v1

--- a/solution.py
+++ b/solution.py
@@ -125,7 +125,7 @@
     factor_out[...] = lax.fori_loop(0, shards, backward, jnp.zeros((factors, paths), f32))
 
 
-def price_and_adjoint(weight, trade_data, factor_rows, loss_spanning, block=1024):
+def price_and_adjoint(weight, trade_data, factor_rows, loss_spanning, block=4096):
     shards, _, trades = trade_data.shape
     factors, paths = factor_rows.shape
     slots = 256

time: 155 us -> 128 us (0.83)
  Pallas kernels: 82.3 us -> 55.7 us
    pallas_call x1, Pallas kernels: 82.3 us -> 55.7 us  [price_and_adjoint(): pl.pallas_call(functools.partial(kernel, block), out_shape=(jax.ShapeDtyp...]
where the time goes in v2:
time: 128 us; the launch traced here: 127 us
  Pallas kernels  55.7 us (44%)
  starting transfers between devices  34.6 us (27%)
  waiting for transfers between devices  25.9 us (20%)
  other arithmetic  7.4 us (6%)
  local copies, waits for them, and re-layouts  2.94 us (2%)
    pallas_call x1, Pallas kernels, price_and_adjoint(): pl.pallas_call(functools.partial(kernel, block), out_shape=(jax.ShapeDtyp...  55.7 us
    ppermute x1, waiting for transfers between devices, on_device(): first = lax.ppermute(first, ('path', 'trade'), routes[0])  11.8 us
    all_to_all x1, starting transfers between devices, on_device(): trade_data = lax.all_to_all(sent, 'trade', 0, 0, tiled=True)  8.58 us
    ppermute x1, waiting for transfers between devices, on_device(): lax.ppermute(jnp.where(odd_date, right, left), ('path', 'trade'), back[0])  8.24 us
    all_to_all x1, starting transfers between devices, on_device(): loading_part = lax.all_to_all(loading_part, 'trade', 0, 0, tiled=True)  7.68 us
    ppermute x1, starting transfers between devices, on_device(): second = lax.ppermute(second, ('path', 'trade'), routes[1])  6.12 us
    ppermute x1, starting transfers between devices, on_device(): first = lax.ppermute(first, ('path', 'trade'), routes[0])  5.04 us
    ppermute x1, starting transfers between devices, on_device(): lax.ppermute(jnp.where(odd_date, left, right), ('path', 'trade'), back[1])  4.02 us
  transfers between devices with their start and end apart: 6, of which 5 were waited for; matrix products, arithmetic and copies ran while one was open for 2% of the time, Pallas kernels for 0%

profile of v2, /device:TPU:1, one launch (start us, length us, event | category | flops | bytes accessed | tf_op | source)
XLA Modules:
  0.0 127.4 jit_solution(6930210303088624372)
XLA Ops:
  0.6 0.0 copy-start
  0.7 0.9 convert_element_type.33
  1.5 0.7 fusion.1
  2.3 0.7 fusion.3
  3.1 0.7 convert_element_type.38
  3.7 0.7 fusion.5
  4.4 0.2 dynamic-update-slice
  4.6 0.2 dynamic-update-slice.1
  4.8 0.2 dynamic-update-slice.2
  5.0 0.2 dynamic-update-slice.3
  5.2 0.2 dynamic-update-slice.4
  5.5 0.0 copy-done
  5.5 0.2 stack.45
  5.7 0.1 broadcast_in_dim.17
  5.8 0.1 broadcast_in_dim.15
  5.9 1.5 %pad_maximum_fusion = bf16[16,16,4096]{2,1,0:T(8,128)(2,1)} fusion(bf16[16,8,4096]{2,1,0:T(8,128)(2,1)S(1)} %broadcast_in_dim.17, bf16[16,8,4096]{2,1,0:T(8,128)(2,1)S(1)} %bitcast.14), kind=kLoop, calls=%fused_computation | loop fusion | flops 4194304 | bytes 4194304 | tf_op jit(solution)/shard_map/concatenate | solution.py:178
  7.4 0.0 copy-start.3
  7.4 8.6 %all-to-all-start = ((bf16[16,16,4096]{2,1,0:T(8,128)(2,1)}), bf16[16,16,4096]{2,1,0:T(8,128)(2,1)}, u32[]{:S(2)}, u32[]{:S(2)}) async-start(bf16[16,16,4096]{2,1,0:T(8,128)(2,1)} %pad_maximum_fusion), calls=%async_computation | async-start | bytes 4194304 | tf_op jit(solution)/shard_map/all_to_all | solution.py:185
  15.9 0.7 select_bitcast_fusion.1
  16.6 5.0 %collective-permute-start.1 = (bf16[8,128]{1,0:T(8,128)(2,1)S(1)}, bf16[8,128]{1,0:T(8,128)(2,1)S(1)}, u32[]{:S(2)}, u32[]{:S(2)}) collective-permute-start(bf16[8,128]{1,0:T(8,128)(2,1)S(1)} %get-tuple-element.7), channel_id=1, source_target_pairs={{0,0},{1,8},{2,16},{3,24},{4,32},{5,40},{6,48},{7,56},{8,64},{9,72... | collective-permute-start | bytes 6152 | tf_op jit(solution)/shard_map/ppermute | solution.py:201
  21.7 6.1 %collective-permute-start = (bf16[8,128]{1,0:T(8,128)(2,1)S(1)}, bf16[8,128]{1,0:T(8,128)(2,1)S(1)}, u32[]{:S(2)}, u32[]{:S(2)}) collective-permute-start(bf16[8,128]{1,0:T(8,128)(2,1)S(1)} %get-tuple-element.6), channel_id=1, source_target_pairs={{0,4},{1,12},{2,20},{3,28},{4,36},{5,44},{6,52},{7,60},{8,68},{9,7... | collective-permute-start | bytes 6152 | tf_op jit(solution)/shard_map/ppermute | solution.py:202
  27.8 0.0 copy-done.3
  27.8 0.7 dynamic_slice.9
  28.5 11.8 %collective-permute-done.1 = bf16[8,128]{1,0:T(8,128)(2,1)S(1)} collective-permute-done((bf16[8,128]{1,0:T(8,128)(2,1)S(1)}, bf16[8,128]{1,0:T(8,128)(2,1)S(1)}, u32[]{:S(2)}, u32[]{:S(2)}) %collective-permute-start.1) | collective-permute-done | bytes 2080 | tf_op jit(solution)/shard_map/ppermute | solution.py:201
  40.3 1.0 collective-permute-done
  41.4 0.0 copy-start.1
  41.4 0.7 copy.11.column_ref
  42.1 2.4 %all-to-all-done.trade_ref = bf16[16,16,4096]{2,1,0:T(8,128)(2,1)} async-done(((bf16[16,16,4096]{2,1,0:T(8,128)(2,1)}), bf16[16,16,4096]{2,1,0:T(8,128)(2,1)}, u32[]{:S(2)}, u32[]{:S(2)}) %all-to-all-start) | async-done | bytes 2097184 | tf_op jit(solution)/shard_map/all_to_all | solution.py:185
  44.5 0.0 copy-done.1
  44.5 55.7 %shard_map.104 = (bf16[16,8,4096]{2,1,0:T(8,128)(2,1)}, f32[8,256]{1,0:T(8,128)}) custom-call(f32[1,1]{1,0:T(1,128)} %bitcast.weight_ref, bf16[16,16,4096]{2,1,0:T(8,128)(2,1)} %all-to-all-done.trade_ref, bf16[256,16]{1,0:T(8,128)(2,1)} %copy.11.column_ref, bf16[8,256]{1,0:T(8,128)(2,1)} %copy-done.1, f32[1,256]{1,0:T(1,128)} %bitcast.17), custom_call_target="tpu_custom_call" | custom-call | tf_op jit(solution)/shard_map/pallas_call | solution.py:134
  100.2 0.0 copy-start.2
  100.2 7.7 %all-to-all-start.1 = ((bf16[16,8,4096]{2,1,0:T(8,128)(2,1)}), bf16[16,8,4096]{2,1,0:T(8,128)(2,1)S(1)}, u32[]{:S(2)}, u32[]{:S(2)}) async-start(bf16[16,8,4096]{2,1,0:T(8,128)(2,1)} %get-tuple-element.4), calls=%async_computation.1 | async-start | bytes 2097152 | tf_op jit(solution)/shard_map/all_to_all | solution.py:221
  107.9 0.0 copy-done.2
  107.9 3.2 %collective-permute-start.3 = (f32[8,128]{1,0:T(8,128)S(1)}, f32[8,128]{1,0:T(8,128)S(1)}, u32[]{:S(2)}, u32[]{:S(2)}) collective-permute-start(f32[8,128]{1,0:T(8,128)S(1)} %get-tuple-element.13), channel_id=1, source_target_pairs={{0,0},{8,1},{16,2},{24,3},{32,4},{40,5},{48,6},{56,7},{64,8},{72,9... | collective-permute-start | bytes 12296 | tf_op jit(solution)/shard_map/ppermute | solution.py:217
  111.1 4.0 %collective-permute-start.2 = (f32[8,128]{1,0:T(8,128)S(1)}, f32[8,128]{1,0:T(8,128)S(1)}, u32[]{:S(2)}, u32[]{:S(2)}) collective-permute-start(f32[8,128]{1,0:T(8,128)S(1)} %get-tuple-element.12), channel_id=1, source_target_pairs={{4,0},{12,1},{20,2},{28,3},{36,4},{44,5},{52,6},{60,7},{68,8},{76,... | collective-permute-start | bytes 12296 | tf_op jit(solution)/shard_map/ppermute | solution.py:218
  115.1 8.2 %collective-permute-done.3 = f32[8,128]{1,0:T(8,128)S(1)} collective-permute-done((f32[8,128]{1,0:T(8,128)S(1)}, f32[8,128]{1,0:T(8,128)S(1)}, u32[]{:S(2)}, u32[]{:S(2)}) %collective-permute-start.3) | collective-permute-done | bytes 4128 | tf_op jit(solution)/shard_map/ppermute | solution.py:217
  123.4 2.4 %collective-permute-done.2 = f32[8,128]{1,0:T(8,128)S(1)} collective-permute-done((f32[8,128]{1,0:T(8,128)S(1)}, f32[8,128]{1,0:T(8,128)S(1)}, u32[]{:S(2)}, u32[]{:S(2)}) %collective-permute-start.2) | collective-permute-done | bytes 4128 | tf_op jit(solution)/shard_map/ppermute | solution.py:218
  125.8 0.6 maximum_select_fusion
  126.4 0.0 all-to-all-done.1
  126.4 0.2 convert_reduce_fusion
  126.6 0.8 broadcast_multiply_fusion
  (13 shorter events, 0.1 us)
Async XLA Ops:
  0.6 4.8 %copy-start = (bf16[32,8,4096]{2,1,0:T(8,128)(2,1)S(1)}, bf16[32,8,4096]{2,1,0:T(8,128)(2,1)}, u32[]{:S(2)}) copy-start(bf16[32,8,4096]{2,1,0:T(8,128)(2,1)} %param.10) | copy-start | bytes 6291460
  7.4 20.4 %copy-start.3 = (f32[32]{0:T(128)S(1)}, f32[32]{0:T(128)}, u32[]{:S(2)}) copy-start(f32[32]{0:T(128)} %param.13) | copy-start | bytes 388
  7.4 37.2 %all-to-all-start = ((bf16[16,16,4096]{2,1,0:T(8,128)(2,1)}), bf16[16,16,4096]{2,1,0:T(8,128)(2,1)}, u32[]{:S(2)}, u32[]{:S(2)}) async-start(bf16[16,16,4096]{2,1,0:T(8,128)(2,1)} %pad_maximum_fusion), calls=%async_computation | async-start | bytes 4194304 | tf_op jit(solution)/shard_map/all_to_all | solution.py:185
  16.6 23.7 %collective-permute-start.1 = (bf16[8,128]{1,0:T(8,128)(2,1)S(1)}, bf16[8,128]{1,0:T(8,128)(2,1)S(1)}, u32[]{:S(2)}, u32[]{:S(2)}) collective-permute-start(bf16[8,128]{1,0:T(8,128)(2,1)S(1)} %get-tuple-element.7), channel_id=1, source_target_pairs={{0,0},{1,8},{2,16},{3,24},{4,32},{5,40},{6,48},{7,56},{8,64},{9,72... | collective-permute-start | bytes 6152 | tf_op jit(solution)/shard_map/ppermute | solution.py:201
  21.7 19.7 %collective-permute-start = (bf16[8,128]{1,0:T(8,128)(2,1)S(1)}, bf16[8,128]{1,0:T(8,128)(2,1)S(1)}, u32[]{:S(2)}, u32[]{:S(2)}) collective-permute-start(bf16[8,128]{1,0:T(8,128)(2,1)S(1)} %get-tuple-element.6), channel_id=1, source_target_pairs={{0,4},{1,12},{2,20},{3,28},{4,36},{5,44},{6,52},{7,60},{8,68},{9,7... | collective-permute-start | bytes 6152 | tf_op jit(solution)/shard_map/ppermute | solution.py:202
  41.4 3.2 %copy-start.1 = (bf16[8,256]{1,0:T(8,128)(2,1)}, bf16[8,256]{1,0:T(8,128)(2,1)S(1)}, u32[]{:S(2)}) copy-start(bf16[8,256]{1,0:T(8,128)(2,1)S(1)} %maximum_select_fusion.1.row_ref) | copy-start | bytes 12292
  100.2 7.7 %copy-start.2 = (f32[8,256]{1,0:T(8,128)S(1)}, f32[8,256]{1,0:T(8,128)}, u32[]{:S(2)}) copy-start(f32[8,256]{1,0:T(8,128)} %get-tuple-element.5) | copy-start | bytes 24580
  100.2 26.1 %all-to-all-start.1 = ((bf16[16,8,4096]{2,1,0:T(8,128)(2,1)}), bf16[16,8,4096]{2,1,0:T(8,128)(2,1)S(1)}, u32[]{:S(2)}, u32[]{:S(2)}) async-start(bf16[16,8,4096]{2,1,0:T(8,128)(2,1)} %get-tuple-element.4), calls=%async_computation.1 | async-start | bytes 2097152 | tf_op jit(solution)/shard_map/all_to_all | solution.py:221
  107.9 15.4 %collective-permute-start.3 = (f32[8,128]{1,0:T(8,128)S(1)}, f32[8,128]{1,0:T(8,128)S(1)}, u32[]{:S(2)}, u32[]{:S(2)}) collective-permute-start(f32[8,128]{1,0:T(8,128)S(1)} %get-tuple-element.13), channel_id=1, source_target_pairs={{0,0},{8,1},{16,2},{24,3},{32,4},{40,5},{48,6},{56,7},{64,8},{72,9... | collective-permute-start | bytes 12296 | tf_op jit(solution)/shard_map/ppermute | solution.py:217
  111.1 14.7 %collective-permute-start.2 = (f32[8,128]{1,0:T(8,128)S(1)}, f32[8,128]{1,0:T(8,128)S(1)}, u32[]{:S(2)}, u32[]{:S(2)}) collective-permute-start(f32[8,128]{1,0:T(8,128)S(1)} %get-tuple-element.12), channel_id=1, source_target_pairs={{4,0},{12,1},{20,2},{28,3},{36,4},{44,5},{52,6},{60,7},{68,8},{76,... | collective-permute-start | bytes 12296 | tf_op jit(solution)/shard_map/ppermute | solution.py:218

commit v3 on v2

v3 whole, which is shorter than its diff:
```python
import functools
import math

import jax
import jax.numpy as jnp
from jax import lax
from jax.experimental import pallas as pl
from jax.experimental.pallas import tpu as pltpu
from jax.sharding import PartitionSpec as P

smoothing = 0.5
log2e = math.log2(math.e)
f32 = jnp.float32
bf16 = jnp.bfloat16
nt = (((1,), (1,)), ((), ()))


def split(x):
    high = x.astype(bf16)
    return high, (x - high.astype(f32)).astype(bf16)


def split3(x):
    high, low = split(x)
    return high, low, split(x - high.astype(f32))[1]


def rows_of(data):
    half = data.shape[1]
    loading = jnp.concatenate([data[0:8], data[8:16]], axis=1)
    slot = jnp.concatenate([data[16:17], data[17:18]], axis=1)
    notional = jnp.concatenate(
        [data[18:19] + data[20:21], data[19:20] + data[21:22]], axis=1
    )
    return loading, slot, notional


def lists_of(data, span_local, slots):
    line = data[22:23]
    local = slots - span_local
    ends = [span_local]
    for width in (local, local, local, slots, slots, slots):
        ends.append(ends[-1] + width)
    part = [line[:, lo:hi] for lo, hi in zip([0] + ends, ends)]
    return part[0], part[1] + part[2] + part[3], part[4] + part[5] + part[6]


def pack_kernel(
    slots, first_ref, loading_ref, notional_ref, strike_ref, slot_ref, span_ref, loss_ref, sent_ref, own_ref, sem
):
    devices, _, half = sent_ref.shape
    group_dates = own_ref.shape[0]
    own = pltpu.make_async_copy(
        loading_ref.at[pl.ds(first_ref[0, 0], group_dates)], own_ref, sem
    )
    own.start()
    trades = notional_ref.shape[1]
    notional = notional_ref[...]
    slot = slot_ref[...].astype(f32)
    amount = notional * (1.0 - strike_ref[...])
    ids = lax.broadcasted_iota(jnp.int32, (slots, trades), 0).astype(f32)
    constant = jnp.where(ids == slot, amount, 0.0).sum(axis=1, keepdims=True)
    constant = jnp.broadcast_to(constant, (slots, 128)).T[0:1]
    lists = [span_ref[...].astype(f32)]
    for values in (loss_ref[...], constant):
        lists += [part.astype(f32) for part in split3(values)]
    lists = jnp.concatenate(lists, axis=1)
    lists = jnp.concatenate([lists, jnp.zeros((1, half - lists.shape[1]), f32)], axis=1)
    high, low = (part.astype(f32) for part in split(notional))
    extra = jnp.concatenate(
        [
            row[:, start : start + half]
            for row in (slot, high, low)
            for start in (0, half)
        ]
        + [lists, jnp.zeros((1, half), f32)],
        axis=0,
    )
    own.wait()
    for date in range(group_dates):
        loading = own_ref[date].astype(f32)
        block = jnp.concatenate([loading[:, :half], loading[:, half:], extra], axis=0).astype(bf16)
        for quarter in range(devices // group_dates):
            sent_ref[date * (devices // group_dates) + quarter] = block


def table_of(slot, slots):
    ids = lax.broadcasted_iota(jnp.int32, (slots, slot.shape[1]), 0).astype(f32)
    return jnp.where(ids == slot, 1.0, 0.0).astype(bf16)


def kernel(
    weight_ref,
    trade_ref,
    column_ref,
    row_ref,
    loss_ref,
    loading_out,
    sensitivity_out,
    values_ref,
    slot_weight_ref,
    sems,
):
    shards, _, half = trade_ref.shape
    trades = 2 * half
    paths = column_ref.shape[0]
    slots = slot_weight_ref.shape[2]
    span_local = slots // 2
    span_count = loss_ref.shape[1]
    weight = weight_ref[0, 0]
    column = column_ref[...]
    row = row_ref[...]

    def place(shard):
        return pl.ds(pl.multiple_of(shard * trades, trades), trades)

    def forward(shard, span_total):
        data = trade_ref[shard].astype(f32)
        loading, slot, notional = rows_of(data)
        names, loss, constant = lists_of(data, span_local, slots)
        both = jnp.concatenate(split(loading * log2e), axis=0)
        exponent = jnp.dot(column, both, preferred_element_type=f32)
        values = (notional * (jnp.exp2(exponent) - 1.0)).astype(bf16)
        values_ref[:, place(shard)] = values
        partial = constant + lax.dot_general(
            values, table_of(slot, slots), nt, preferred_element_type=f32
        )
        local = weight * loss * jax.nn.sigmoid(partial[:, span_local:] / smoothing)
        slot_weight_ref[shard, :, span_local:] = local.astype(bf16)
        table = table_of(names, span_count)
        for part in split(partial[:, :span_local]):
            span_total = span_total + lax.dot_general(
                part, table, nt, preferred_element_type=f32
            )
        return span_total

    span_total = lax.fori_loop(0, shards, forward, jnp.zeros((paths, span_count), f32))
    span_weight = (weight * loss_ref[...] * jax.nn.sigmoid(span_total / smoothing)).astype(bf16)

    def copy_out(shard):
        return pltpu.make_async_copy(
            values_ref.at[:, place(shard)], sensitivity_out.at[:, place(shard)], sems.at[shard]
        )

    def backward(shard, carry):
        data = trade_ref[shard].astype(f32)
        _, slot, notional = rows_of(data)
        names, _, _ = lists_of(data, span_local, slots)
        slot_weight_ref[shard, :, :span_local] = jnp.dot(
            span_weight, table_of(names, span_count), preferred_element_type=f32
        ).astype(bf16)
        trade_weight = jnp.dot(
            slot_weight_ref[shard], table_of(slot, slots), preferred_element_type=f32
        )
        scaled = values_ref[:, place(shard)].astype(f32) + notional
        sensitivity = (trade_weight * scaled).astype(bf16)
        values_ref[:, place(shard)] = sensitivity
        copy_out(shard).start()
        loading_out[shard] = jnp.dot(row, sensitivity, preferred_element_type=f32).astype(bf16)
        return carry

    lax.fori_loop(0, shards, backward, 0)

    def drain(shard, carry):
        copy_out(shard).wait()
        return carry

    lax.fori_loop(0, shards, drain, 0)


def factor_kernel(trade_ref, sensitivity_ref, factor_out):
    @pl.when(pl.program_id(0) == 0)
    def _():
        factor_out[...] = jnp.zeros_like(factor_out)

    loading, _, _ = rows_of(trade_ref[0].astype(f32))
    factor_out[...] += lax.dot_general(
        loading.astype(bf16), sensitivity_ref[...], nt, preferred_element_type=f32
    )


vmem = pl.BlockSpec(memory_space=pltpu.VMEM)
smem = pl.BlockSpec(memory_space=pltpu.SMEM)
params = pltpu.CompilerParams(vmem_limit_bytes=58 * 2**20)


def pack(first, loadings, notional, strike, trade_slot, span_list, loss_local, devices, group_dates):
    factors, trades = loadings.shape[1:]
    slots = span_list.shape[0] + loss_local.shape[0]
    return pl.pallas_call(
        functools.partial(pack_kernel, slots),
        out_shape=jax.ShapeDtypeStruct((devices, 24, trades // 2), bf16),
        in_specs=[smem, pl.BlockSpec(memory_space=pl.ANY)] + [vmem] * 5,
        out_specs=vmem,
        scratch_shapes=[
            pltpu.VMEM((group_dates, factors, trades), bf16),
            pltpu.SemaphoreType.DMA,
        ],
        compiler_params=params,
    )(
        first,
        loadings,
        notional[None],
        strike[None],
        trade_slot[None],
        span_list[None],
        loss_local[None],
    )


def price_and_adjoint(weight, trade_data, factor_rows, loss_spanning, slots=256):
    shards, _, half = trade_data.shape
    trades = 2 * half
    factors, paths = factor_rows.shape
    column = jnp.concatenate([factor_rows, factor_rows], axis=0).T
    return pl.pallas_call(
        kernel,
        out_shape=(
            jax.ShapeDtypeStruct((shards, factors, trades), bf16),
            jax.ShapeDtypeStruct((paths, shards * trades), bf16),
        ),
        in_specs=[smem, vmem, vmem, vmem, vmem],
        out_specs=(vmem, pl.BlockSpec(memory_space=pl.ANY)),
        scratch_shapes=[
            pltpu.VMEM((paths, shards * trades), bf16),
            pltpu.VMEM((shards, paths, slots), bf16),
            pltpu.SemaphoreType.DMA((shards,)),
        ],
        compiler_params=params,
        cost_estimate=pl.CostEstimate(
            flops=shards * trades * paths * 2 * 256 * 4,
            bytes_accessed=shards * trades * paths * 2,
            transcendentals=shards * trades * paths,
        ),
    )(weight, trade_data, column, factor_rows, loss_spanning)


def factor_sums(trade_data, sensitivity):
    shards, rows, half = trade_data.shape
    paths, trades = sensitivity.shape[0], 2 * half
    return pl.pallas_call(
        factor_kernel,
        grid=(shards,),
        out_shape=jax.ShapeDtypeStruct((8, paths), f32),
        in_specs=[
            pl.BlockSpec((1, rows, half), lambda shard: (shard, 0, 0)),
            pl.BlockSpec((paths, trades), lambda shard: (0, shard)),
        ],
        out_specs=pl.BlockSpec((8, paths), lambda shard: (0, 0)),
        compiler_params=params,
        cost_estimate=pl.CostEstimate(
            flops=shards * trades * paths * 2 * 256,
            bytes_accessed=shards * trades * paths * 2,
            transcendentals=0,
        ),
    )(trade_data, sensitivity)


def on_device(
    factors,
    loadings,
    notional,
    strike,
    date_weight,
    loss_spanning,
    loss_local,
    trade_slot,
    span_list,
):
    path_devices = lax.axis_size("path")
    trade_devices = lax.axis_size("trade")
    path_at = lax.axis_index("path")
    trade_at = lax.axis_index("trade")
    dates, factor_count, chunk = factors.shape
    trades = loadings.shape[2]
    group_dates = dates // path_devices
    quarters = trade_devices // group_dates

    first_date = (path_at * group_dates).astype(jnp.int32).reshape(1, 1)
    sent = pack(
        first_date,
        loadings,
        notional,
        strike,
        trade_slot,
        span_list,
        loss_local,
        trade_devices,
        group_dates,
    )
    trade_data = lax.all_to_all(sent, "trade", 0, 0, tiled=True)

    routes = []
    for turn in range(2):
        route = []
        for a in range(path_devices):
            for b in range(trade_devices):
                date = 2 * b + (a + turn) % 2
                to = (date // group_dates) * trade_devices + (date % group_dates) * quarters + a // 2
                route.append((a * trade_devices + b, to))
        routes.append(route)
    mine = lax.dynamic_slice_in_dim(factors, 2 * trade_at, 2, 0)
    odd_path = path_at % 2 == 1
    odd_date = (trade_at // quarters) % 2 == 1
    first = jnp.where(odd_path, mine[1], mine[0])
    second = jnp.where(odd_path, mine[0], mine[1])
    first = lax.ppermute(first, ("path", "trade"), routes[0])
    second = lax.ppermute(second, ("path", "trade"), routes[1])
    factor_rows = jnp.where(
        odd_date,
        jnp.concatenate([second, first], axis=1),
        jnp.concatenate([first, second], axis=1),
    )

    date_at = path_at * group_dates + trade_at // quarters
    weight = lax.dynamic_slice_in_dim(date_weight, date_at, 1).reshape(1, 1)
    loading_part, sensitivity = price_and_adjoint(
        weight, trade_data, factor_rows, loss_spanning[None, :]
    )
    loading_part = lax.all_to_all(loading_part, "trade", 0, 0, tiled=True)
    factor_part = factor_sums(trade_data, sensitivity)

    back = [[(to, origin) for origin, to in route] for route in routes]
    left, right = factor_part[:, :chunk], factor_part[:, chunk:]
    first = lax.ppermute(jnp.where(odd_date, right, left), ("path", "trade"), back[0])
    second = lax.ppermute(jnp.where(odd_date, left, right), ("path", "trade"), back[1])
    factor_grad = jnp.where(odd_path, jnp.stack([second, first]), jnp.stack([first, second]))

    loading_part = loading_part.reshape(group_dates, quarters, factor_count, trades)
    loading_grad = loading_part.astype(f32).sum(axis=1) / (path_devices * chunk)
    return (loading_grad, factor_grad)


def solution(mesh):
    return jax.shard_map(
        on_device,
        mesh=mesh,
        in_specs=(
            P(None, None, "path"),
            P(None, None, "trade"),
            P("trade"),
            P("trade"),
            P(),
            P(),
            P("trade"),
            P("trade"),
            P("trade"),
        ),
        out_specs=(P("path", None, "trade"), P("trade", None, "path")),
        check_vma=False,
    )
```

time: 128 us -> 130 us (1.016)
  the two profiles are of different devices: /device:TPU:1 before, /device:TPU:6 now
where the time goes in v3:
time: 130 us; the launch traced here: 129 us
  Pallas kernels  73.3 us (56%)
  starting transfers between devices  30 us (23%)
  waiting for transfers between devices  19.3 us (15%)
  other arithmetic  3 us (2%)
  local copies, waits for them, and re-layouts  2.53 us (2%)
    pallas_call x1, Pallas kernels, price_and_adjoint(): pl.pallas_call(kernel, out_shape=(jax.ShapeDtypeStruct((shards, factors,...  49.6 us
    pallas_call x1, Pallas kernels, factor_sums(): pl.pallas_call(factor_kernel, grid=(shards,), out_shape=jax.ShapeDtypeStr...  20.7 us
    all_to_all x1, starting transfers between devices, on_device(): loading_part = lax.all_to_all(loading_part, 'trade', 0, 0, tiled=True)  10.3 us
    ppermute x1, waiting for transfers between devices, on_device(): second = lax.ppermute(second, ('path', 'trade'), routes[1])  9.85 us
    all_to_all x1, starting transfers between devices, on_device(): trade_data = lax.all_to_all(sent, 'trade', 0, 0, tiled=True)  7.46 us
    ppermute x1, waiting for transfers between devices, on_device(): lax.ppermute(jnp.where(odd_date, right, left), ('path', 'trade'), back[0])  5.5 us
    ppermute x1, starting transfers between devices, on_device(): first = lax.ppermute(first, ('path', 'trade'), routes[0])  5.46 us
    ppermute x1, waiting for transfers between devices, on_device(): lax.ppermute(jnp.where(odd_date, left, right), ('path', 'trade'), back[1])  3.82 us
  transfers between devices with their start and end apart: 6, of which 4 were waited for; matrix products, arithmetic and copies ran while one was open for 3% of the time, Pallas kernels for 16%

profile of v3, /device:TPU:6, one launch (start us, length us, event | category | flops | bytes accessed | tf_op | source)
XLA Modules:
  0.0 128.8 jit_solution(10532792946556302410)
XLA Ops:
  0.6 3.0 %shard_map.104 = bf16[16,24,2048]{2,1,0:T(8,128)(2,1)} custom-call(s32[1,1]{1,0:T(1,128)} %bitcast.1.first_ref, bf16[32,8,4096]{2,1,0:T(8,128)(2,1)} %loading_ref.1, f32[1,4096]{1,0:T(1,128)} %bitcast.19, f32[1,4096]{1,0:T(1,128)} %bitcast.20, s32[1,4096]{1,0:T(1,128)} %bitcast.21, s32[1,128]{1,0:T(1,128)} %bitcast.24, f32[1,128]{1,0:T(1,128)} %bitcast.25), custom_call_target="tpu_custom_call" | custom-call | tf_op jit(solution)/shard_map/pallas_call | solution.py:190
  3.7 0.0 copy-start.2
  3.7 7.5 %all-to-all-start = ((bf16[16,24,2048]{2,1,0:T(8,128)(2,1)}), bf16[16,24,2048]{2,1,0:T(8,128)(2,1)S(1)}, u32[]{:S(2)}, u32[]{:S(2)}) async-start(bf16[16,24,2048]{2,1,0:T(8,128)(2,1)} %shard_map.104), calls=%async_computation | async-start | bytes 3145728 | tf_op jit(solution)/shard_map/all_to_all | solution.py:291
  11.1 0.7 select_bitcast_fusion.1
  11.8 3.4 %collective-permute-start = (bf16[8,128]{1,0:T(8,128)(2,1)S(1)}, bf16[8,128]{1,0:T(8,128)(2,1)S(1)}, u32[]{:S(2)}, u32[]{:S(2)}) collective-permute-start(bf16[8,128]{1,0:T(8,128)(2,1)S(1)} %get-tuple-element.6), channel_id=1, source_target_pairs={{0,4},{1,12},{2,20},{3,28},{4,36},{5,44},{6,52},{7,60},{8,68},{9,7... | collective-permute-start | bytes 6152 | tf_op jit(solution)/shard_map/ppermute | solution.py:308
  15.2 5.5 %collective-permute-start.1 = (bf16[8,128]{1,0:T(8,128)(2,1)S(1)}, bf16[8,128]{1,0:T(8,128)(2,1)S(1)}, u32[]{:S(2)}, u32[]{:S(2)}) collective-permute-start(bf16[8,128]{1,0:T(8,128)(2,1)S(1)} %get-tuple-element.7), channel_id=1, source_target_pairs={{0,0},{1,8},{2,16},{3,24},{4,32},{5,40},{6,48},{7,56},{8,64},{9,72... | collective-permute-start | bytes 6152 | tf_op jit(solution)/shard_map/ppermute | solution.py:307
  20.8 0.0 copy-done.2
  20.8 0.6 dynamic_slice.6
  21.4 9.9 %collective-permute-done = bf16[8,128]{1,0:T(8,128)(2,1)S(1)} collective-permute-done((bf16[8,128]{1,0:T(8,128)(2,1)S(1)}, bf16[8,128]{1,0:T(8,128)(2,1)S(1)}, u32[]{:S(2)}, u32[]{:S(2)}) %collective-permute-start) | collective-permute-done | bytes 2080 | tf_op jit(solution)/shard_map/ppermute | solution.py:308
  31.3 0.0 collective-permute-done.1
  31.3 0.0 copy-start.1
  31.3 0.7 copy.11.column_ref
  32.0 0.1 all-to-all-done.trade_ref
  32.1 0.0 copy-start
  32.1 0.0 copy-done.1
  32.1 1.1 copy-done
  33.3 49.6 %shard_map.105 = (bf16[16,8,4096]{2,1,0:T(8,128)(2,1)}, bf16[256,65536]{1,0:T(8,128)(2,1)}) custom-call(f32[1,1]{1,0:T(1,128)} %bitcast.weight_ref, bf16[16,24,2048]{2,1,0:T(8,128)(2,1)} %copy-done, bf16[256,16]{1,0:T(8,128)(2,1)} %copy.11.column_ref, bf16[8,256]{1,0:T(8,128)(2,1)} %copy-done.1, f32[1,256]{1,0:T(1,128)} %bitcast.26), custom_call_target="tpu_custom_call" | custom-call | flops 34359738368 | bytes 33554432 | tf_op jit(solution)/shard_map/pallas_call | solution.py:216
  82.9 10.3 %all-to-all-start.1 = ((bf16[16,8,4096]{2,1,0:T(8,128)(2,1)}), bf16[16,8,4096]{2,1,0:T(8,128)(2,1)S(1)}, u32[]{:S(2)}, u32[]{:S(2)}) async-start(bf16[16,8,4096]{2,1,0:T(8,128)(2,1)} %get-tuple-element.4), calls=%async_computation.1 | async-start | bytes 2097152 | tf_op jit(solution)/shard_map/all_to_all | solution.py:320
  93.2 20.7 %shard_map.106 = f32[8,256]{1,0:T(8,128)} custom-call(bf16[16,24,2048]{2,1,0:T(8,128)(2,1)} %copy-done, bf16[256,65536]{1,0:T(8,128)(2,1)} %get-tuple-element.5.sensitivity_ref), custom_call_target="tpu_custom_call" | custom-call | flops 8589934592 | bytes 33554432 | tf_op jit(solution)/shard_map/pallas_call | solution.py:241
  113.8 0.7 slice_select_fusion.1
  114.5 1.2 collective-permute-start.2
  115.7 2.2 %collective-permute-start.3 = (f32[8,128]{1,0:T(8,128)S(1)}, f32[8,128]{1,0:T(8,128)S(1)}, u32[]{:S(2)}, u32[]{:S(2)}) collective-permute-start(f32[8,128]{1,0:T(8,128)S(1)} %get-tuple-element.9), channel_id=1, source_target_pairs={{0,0},{8,1},{16,2},{24,3},{32,4},{40,5},{48,6},{56,7},{64,8},{72,9... | collective-permute-start | bytes 12296 | tf_op jit(solution)/shard_map/ppermute | solution.py:325
  117.9 3.8 %collective-permute-done.2 = f32[8,128]{1,0:T(8,128)S(1)} collective-permute-done((f32[8,128]{1,0:T(8,128)S(1)}, f32[8,128]{1,0:T(8,128)S(1)}, u32[]{:S(2)}, u32[]{:S(2)}) %collective-permute-start.2) | collective-permute-done | bytes 4128 | tf_op jit(solution)/shard_map/ppermute | solution.py:326
  121.7 5.5 %collective-permute-done.3 = f32[8,128]{1,0:T(8,128)S(1)} collective-permute-done((f32[8,128]{1,0:T(8,128)S(1)}, f32[8,128]{1,0:T(8,128)S(1)}, u32[]{:S(2)}, u32[]{:S(2)}) %collective-permute-start.3) | collective-permute-done | bytes 4128 | tf_op jit(solution)/shard_map/ppermute | solution.py:325
  127.2 0.6 maximum_select_fusion
  127.8 0.0 all-to-all-done.1
  127.8 0.2 convert_reduce_fusion
  128.0 0.8 broadcast_multiply_fusion
  (2 shorter events, 0.0 us)
Async XLA Ops:
  3.7 17.1 %copy-start.2 = (f32[32]{0:T(128)S(1)}, f32[32]{0:T(128)}, u32[]{:S(2)}) copy-start(f32[32]{0:T(128)} %param.13) | copy-start | bytes 388
  3.7 28.4 %all-to-all-start = ((bf16[16,24,2048]{2,1,0:T(8,128)(2,1)}), bf16[16,24,2048]{2,1,0:T(8,128)(2,1)S(1)}, u32[]{:S(2)}, u32[]{:S(2)}) async-start(bf16[16,24,2048]{2,1,0:T(8,128)(2,1)} %shard_map.104), calls=%async_computation | async-start | bytes 3145728 | tf_op jit(solution)/shard_map/all_to_all | solution.py:291
  11.8 19.4 %collective-permute-start = (bf16[8,128]{1,0:T(8,128)(2,1)S(1)}, bf16[8,128]{1,0:T(8,128)(2,1)S(1)}, u32[]{:S(2)}, u32[]{:S(2)}) collective-permute-start(bf16[8,128]{1,0:T(8,128)(2,1)S(1)} %get-tuple-element.6), channel_id=1, source_target_pairs={{0,4},{1,12},{2,20},{3,28},{4,36},{5,44},{6,52},{7,60},{8,68},{9,7... | collective-permute-start | bytes 6152 | tf_op jit(solution)/shard_map/ppermute | solution.py:308
  15.2 16.0 %collective-permute-start.1 = (bf16[8,128]{1,0:T(8,128)(2,1)S(1)}, bf16[8,128]{1,0:T(8,128)(2,1)S(1)}, u32[]{:S(2)}, u32[]{:S(2)}) collective-permute-start(bf16[8,128]{1,0:T(8,128)(2,1)S(1)} %get-tuple-element.7), channel_id=1, source_target_pairs={{0,0},{1,8},{2,16},{3,24},{4,32},{5,40},{6,48},{7,56},{8,64},{9,72... | collective-permute-start | bytes 6152 | tf_op jit(solution)/shard_map/ppermute | solution.py:307
  31.3 0.8 copy-start.1
  32.1 1.1 copy-start
  82.9 45.0 %all-to-all-start.1 = ((bf16[16,8,4096]{2,1,0:T(8,128)(2,1)}), bf16[16,8,4096]{2,1,0:T(8,128)(2,1)S(1)}, u32[]{:S(2)}, u32[]{:S(2)}) async-start(bf16[16,8,4096]{2,1,0:T(8,128)(2,1)} %get-tuple-element.4), calls=%async_computation.1 | async-start | bytes 2097152 | tf_op jit(solution)/shard_map/all_to_all | solution.py:320
  114.5 7.2 %collective-permute-start.2 = (f32[8,128]{1,0:T(8,128)S(1)}, f32[8,128]{1,0:T(8,128)S(1)}, u32[]{:S(2)}, u32[]{:S(2)}) collective-permute-start(f32[8,128]{1,0:T(8,128)S(1)} %get-tuple-element.8), channel_id=1, source_target_pairs={{4,0},{12,1},{20,2},{28,3},{36,4},{44,5},{52,6},{60,7},{68,8},{76,... | collective-permute-start | bytes 12296 | tf_op jit(solution)/shard_map/ppermute | solution.py:326
  115.7 11.5 %collective-permute-start.3 = (f32[8,128]{1,0:T(8,128)S(1)}, f32[8,128]{1,0:T(8,128)S(1)}, u32[]{:S(2)}, u32[]{:S(2)}) collective-permute-start(f32[8,128]{1,0:T(8,128)S(1)} %get-tuple-element.9), channel_id=1, source_target_pairs={{0,0},{8,1},{16,2},{24,3},{32,4},{40,5},{48,6},{56,7},{64,8},{72,9... | collective-permute-start | bytes 12296 | tf_op jit(solution)/shard_map/ppermute | solution.py:325

commit v4 on v3

--- a/solution.py
+++ b/solution.py
@@ -92,24 +92,22 @@
 def kernel(
     weight_ref,
     trade_ref,
-    column_ref,
     row_ref,
     loss_ref,
     loading_out,
-    sensitivity_out,
+    factor_out,
     values_ref,
     slot_weight_ref,
-    sems,
 ):
     shards, _, half = trade_ref.shape
     trades = 2 * half
-    paths = column_ref.shape[0]
+    factors, paths = row_ref.shape
     slots = slot_weight_ref.shape[2]
     span_local = slots // 2
     span_count = loss_ref.shape[1]
     weight = weight_ref[0, 0]
-    column = column_ref[...]
     row = row_ref[...]
+    column = jnp.concatenate([row.astype(f32)] * 2, axis=0).T.astype(bf16)
 
     def place(shard):
         return pl.ds(pl.multiple_of(shard * trades, trades), trades)
@@ -137,14 +135,9 @@
     span_total = lax.fori_loop(0, shards, forward, jnp.zeros((paths, span_count), f32))
     span_weight = (weight * loss_ref[...] * jax.nn.sigmoid(span_total / smoothing)).astype(bf16)
 
-    def copy_out(shard):
-        return pltpu.make_async_copy(
-            values_ref.at[:, place(shard)], sensitivity_out.at[:, place(shard)], sems.at[shard]
-        )
-
-    def backward(shard, carry):
+    def backward(shard, total):
         data = trade_ref[shard].astype(f32)
-        _, slot, notional = rows_of(data)
+        loading, slot, notional = rows_of(data)
         names, _, _ = lists_of(data, span_local, slots)
         slot_weight_ref[shard, :, :span_local] = jnp.dot(
             span_weight, table_of(names, span_count), preferred_element_type=f32
@@ -154,29 +147,12 @@
         )
         scaled = values_ref[:, place(shard)].astype(f32) + notional
         sensitivity = (trade_weight * scaled).astype(bf16)
-        values_ref[:, place(shard)] = sensitivity
-        copy_out(shard).start()
         loading_out[shard] = jnp.dot(row, sensitivity, preferred_element_type=f32).astype(bf16)
-        return carry
-
-    lax.fori_loop(0, shards, backward, 0)
-
-    def drain(shard, carry):
-        copy_out(shard).wait()
-        return carry
-
-    lax.fori_loop(0, shards, drain, 0)
-
-
-def factor_kernel(trade_ref, sensitivity_ref, factor_out):
-    @pl.when(pl.program_id(0) == 0)
-    def _():
-        factor_out[...] = jnp.zeros_like(factor_out)
-
-    loading, _, _ = rows_of(trade_ref[0].astype(f32))
-    factor_out[...] += lax.dot_general(
-        loading.astype(bf16), sensitivity_ref[...], nt, preferred_element_type=f32
-    )
+        return total + lax.dot_general(
+            loading.astype(bf16), sensitivity, nt, preferred_element_type=f32
+        )
+
+    factor_out[...] = lax.fori_loop(0, shards, backward, jnp.zeros((factors, paths), f32))
 
 
 vmem = pl.BlockSpec(memory_space=pltpu.VMEM)
@@ -212,19 +188,17 @@
     shards, _, half = trade_data.shape
     trades = 2 * half
     factors, paths = factor_rows.shape
-    column = jnp.concatenate([factor_rows, factor_rows], axis=0).T
     return pl.pallas_call(
         kernel,
         out_shape=(
             jax.ShapeDtypeStruct((shards, factors, trades), bf16),
-            jax.ShapeDtypeStruct((paths, shards * trades), bf16),
+            jax.ShapeDtypeStruct((factors, paths), f32),
         ),
-        in_specs=[smem, vmem, vmem, vmem, vmem],
-        out_specs=(vmem, pl.BlockSpec(memory_space=pl.ANY)),
+        in_specs=[smem, vmem, vmem, vmem],
+        out_specs=(vmem, vmem),
         scratch_shapes=[
             pltpu.VMEM((paths, shards * trades), bf16),
             pltpu.VMEM((shards, paths, slots), bf16),
-            pltpu.SemaphoreType.DMA((shards,)),
         ],
         compiler_params=params,
         cost_estimate=pl.CostEstimate(
@@ -232,28 +206,7 @@
             bytes_accessed=shards * trades * paths * 2,
             transcendentals=shards * trades * paths,
         ),
-    )(weight, trade_data, column, factor_rows, loss_spanning)
-
-
-def factor_sums(trade_data, sensitivity):
-    shards, rows, half = trade_data.shape
-    paths, trades = sensitivity.shape[0], 2 * half
-    return pl.pallas_call(
-        factor_kernel,
-        grid=(shards,),
-        out_shape=jax.ShapeDtypeStruct((8, paths), f32),
-        in_specs=[
-            pl.BlockSpec((1, rows, half), lambda shard: (shard, 0, 0)),
-            pl.BlockSpec((paths, trades), lambda shard: (0, shard)),
-        ],
-        out_specs=pl.BlockSpec((8, paths), lambda shard: (0, 0)),
-        compiler_params=params,
-        cost_estimate=pl.CostEstimate(
-            flops=shards * trades * paths * 2 * 256,
-            bytes_accessed=shards * trades * paths * 2,
-            transcendentals=0,
-        ),
-    )(trade_data, sensitivity)
+    )(weight, trade_data, factor_rows, loss_spanning)
 
 
 def on_device(
@@ -314,12 +267,10 @@
 
     date_at = path_at * group_dates + trade_at // quarters
     weight = lax.dynamic_slice_in_dim(date_weight, date_at, 1).reshape(1, 1)
-    loading_part, sensitivity = price_and_adjoint(
+    loading_part, factor_part = price_and_adjoint(
         weight, trade_data, factor_rows, loss_spanning[None, :]
     )
     loading_part = lax.all_to_all(loading_part, "trade", 0, 0, tiled=True)
-    factor_part = factor_sums(trade_data, sensitivity)
-
     back = [[(to, origin) for origin, to in route] for route in routes]
     left, right = factor_part[:, :chunk], factor_part[:, chunk:]
     first = lax.ppermute(jnp.where(odd_date, right, left), ("path", "trade"), back[0])

time: 130 us -> 118 us (0.908)
  the two profiles are of different devices: /device:TPU:6 before, /device:TPU:1 now
where the time goes in v4:
time: 118 us
  Pallas kernels  58.8 us (50%)
  starting transfers between devices  33.3 us (28%)
  waiting for transfers between devices  20.5 us (17%)
  other arithmetic  2.89 us (2%)
  local copies, waits for them, and re-layouts  1.78 us (2%)
    pallas_call x1, Pallas kernels, price_and_adjoint(): pl.pallas_call(kernel, out_shape=(jax.ShapeDtypeStruct((shards, factors,...  55.7 us
    all_to_all x1, starting transfers between devices, on_device(): trade_data = lax.all_to_all(sent, 'trade', 0, 0, tiled=True)  8.46 us
    ppermute x1, waiting for transfers between devices, on_device(): lax.ppermute(jnp.where(odd_date, right, left), ('path', 'trade'), back[0])  8.24 us
    all_to_all x1, starting transfers between devices, on_device(): loading_part = lax.all_to_all(loading_part, 'trade', 0, 0, tiled=True)  6.56 us
    ppermute x1, starting transfers between devices, on_device(): second = lax.ppermute(second, ('path', 'trade'), routes[1])  6.07 us
    ppermute x1, waiting for transfers between devices, on_device(): first = lax.ppermute(first, ('path', 'trade'), routes[0])  5.12 us
    ppermute x1, starting transfers between devices, on_device(): first = lax.ppermute(first, ('path', 'trade'), routes[0])  5.04 us
    ppermute x1, starting transfers between devices, on_device(): lax.ppermute(jnp.where(odd_date, left, right), ('path', 'trade'), back[1])  4.24 us
  transfers between devices with their start and end apart: 6, of which 5 were waited for; matrix products, arithmetic and copies ran while one was open for 2% of the time, Pallas kernels for 0%

profile of v4, /device:TPU:1, one launch (start us, length us, event | category | flops | bytes accessed | tf_op | source)
XLA Modules:
  0.0 117.9 jit_solution(11030423838291601053)
XLA Ops:
  0.6 3.0 %shard_map.104 = bf16[16,24,2048]{2,1,0:T(8,128)(2,1)} custom-call(s32[1,1]{1,0:T(1,128)} %bitcast.1.first_ref, bf16[32,8,4096]{2,1,0:T(8,128)(2,1)} %loading_ref.1, f32[1,4096]{1,0:T(1,128)} %bitcast.17, f32[1,4096]{1,0:T(1,128)} %bitcast.18, s32[1,4096]{1,0:T(1,128)} %bitcast.19, s32[1,128]{1,0:T(1,128)} %bitcast.22, f32[1,128]{1,0:T(1,128)} %bitcast.23), custom_call_target="tpu_custom_call" | custom-call | tf_op jit(solution)/shard_map/pallas_call | solution.py:166
  3.7 0.0 copy-start.2
  3.7 8.5 %all-to-all-start = ((bf16[16,24,2048]{2,1,0:T(8,128)(2,1)}), bf16[16,24,2048]{2,1,0:T(8,128)(2,1)S(1)}, u32[]{:S(2)}, u32[]{:S(2)}) async-start(bf16[16,24,2048]{2,1,0:T(8,128)(2,1)} %shard_map.104), calls=%async_computation | async-start | bytes 3145728 | tf_op jit(solution)/shard_map/all_to_all | solution.py:244
  12.1 0.7 select_bitcast_fusion.1
  12.8 5.0 %collective-permute-start.1 = (bf16[8,128]{1,0:T(8,128)(2,1)S(1)}, bf16[8,128]{1,0:T(8,128)(2,1)S(1)}, u32[]{:S(2)}, u32[]{:S(2)}) collective-permute-start(bf16[8,128]{1,0:T(8,128)(2,1)S(1)} %get-tuple-element.7), channel_id=1, source_target_pairs={{0,0},{1,8},{2,16},{3,24},{4,32},{5,40},{6,48},{7,56},{8,64},{9,72... | collective-permute-start | bytes 6152 | tf_op jit(solution)/shard_map/ppermute | solution.py:260
  17.9 6.1 %collective-permute-start = (bf16[8,128]{1,0:T(8,128)(2,1)S(1)}, bf16[8,128]{1,0:T(8,128)(2,1)S(1)}, u32[]{:S(2)}, u32[]{:S(2)}) collective-permute-start(bf16[8,128]{1,0:T(8,128)(2,1)S(1)} %get-tuple-element.6), channel_id=1, source_target_pairs={{0,4},{1,12},{2,20},{3,28},{4,36},{5,44},{6,52},{7,60},{8,68},{9,7... | collective-permute-start | bytes 6152 | tf_op jit(solution)/shard_map/ppermute | solution.py:261
  24.0 0.0 copy-done.2
  24.0 0.6 dynamic_slice.6
  24.6 5.1 %collective-permute-done.1 = bf16[8,128]{1,0:T(8,128)(2,1)S(1)} collective-permute-done((bf16[8,128]{1,0:T(8,128)(2,1)S(1)}, bf16[8,128]{1,0:T(8,128)(2,1)S(1)}, u32[]{:S(2)}, u32[]{:S(2)}) %collective-permute-start.1) | collective-permute-done | bytes 2080 | tf_op jit(solution)/shard_map/ppermute | solution.py:260
  29.7 2.2 %collective-permute-done = bf16[8,128]{1,0:T(8,128)(2,1)S(1)} collective-permute-done((bf16[8,128]{1,0:T(8,128)(2,1)S(1)}, bf16[8,128]{1,0:T(8,128)(2,1)S(1)}, u32[]{:S(2)}, u32[]{:S(2)}) %collective-permute-start) | collective-permute-done | bytes 2080 | tf_op jit(solution)/shard_map/ppermute | solution.py:261
  31.9 0.6 maximum_select_fusion.1.row_ref
  32.5 2.5 %all-to-all-done.trade_ref = bf16[16,24,2048]{2,1,0:T(8,128)(2,1)S(1)} async-done(((bf16[16,24,2048]{2,1,0:T(8,128)(2,1)}), bf16[16,24,2048]{2,1,0:T(8,128)(2,1)S(1)}, u32[]{:S(2)}, u32[]{:S(2)}) %all-to-all-start) | async-done | bytes 1572896 | tf_op jit(solution)/shard_map/all_to_all | solution.py:244
  35.0 0.0 copy-start
  35.0 1.2 copy-done
  36.1 55.7 %shard_map.105 = (bf16[16,8,4096]{2,1,0:T(8,128)(2,1)}, f32[8,256]{1,0:T(8,128)}) custom-call(f32[1,1]{1,0:T(1,128)} %bitcast.weight_ref, bf16[16,24,2048]{2,1,0:T(8,128)(2,1)} %copy-done, bf16[8,256]{1,0:T(8,128)(2,1)} %maximum_select_fusion.1.row_ref, f32[1,256]{1,0:T(1,128)} %bitcast.24), custom_call_target="tpu_custom_call" | custom-call | flops 34359738368 | bytes 33554432 | tf_op jit(solution)/shard_map/pallas_call | solution.py:191
  91.9 0.0 copy-start.1
  91.9 6.6 %all-to-all-start.1 = ((bf16[16,8,4096]{2,1,0:T(8,128)(2,1)}), bf16[16,8,4096]{2,1,0:T(8,128)(2,1)S(1)}, u32[]{:S(2)}, u32[]{:S(2)}) async-start(bf16[16,8,4096]{2,1,0:T(8,128)(2,1)} %get-tuple-element.4), calls=%async_computation.1 | async-start | bytes 2097152 | tf_op jit(solution)/shard_map/all_to_all | solution.py:273
  98.5 0.0 copy-done.1
  98.5 2.9 %collective-permute-start.3 = (f32[8,128]{1,0:T(8,128)S(1)}, f32[8,128]{1,0:T(8,128)S(1)}, u32[]{:S(2)}, u32[]{:S(2)}) collective-permute-start(f32[8,128]{1,0:T(8,128)S(1)} %get-tuple-element.9), channel_id=1, source_target_pairs={{0,0},{8,1},{16,2},{24,3},{32,4},{40,5},{48,6},{56,7},{64,8},{72,9... | collective-permute-start | bytes 12296 | tf_op jit(solution)/shard_map/ppermute | solution.py:276
  101.4 4.2 %collective-permute-start.2 = (f32[8,128]{1,0:T(8,128)S(1)}, f32[8,128]{1,0:T(8,128)S(1)}, u32[]{:S(2)}, u32[]{:S(2)}) collective-permute-start(f32[8,128]{1,0:T(8,128)S(1)} %get-tuple-element.8), channel_id=1, source_target_pairs={{4,0},{12,1},{20,2},{28,3},{36,4},{44,5},{52,6},{60,7},{68,8},{76,... | collective-permute-start | bytes 12296 | tf_op jit(solution)/shard_map/ppermute | solution.py:277
  105.7 8.2 %collective-permute-done.3 = f32[8,128]{1,0:T(8,128)S(1)} collective-permute-done((f32[8,128]{1,0:T(8,128)S(1)}, f32[8,128]{1,0:T(8,128)S(1)}, u32[]{:S(2)}, u32[]{:S(2)}) %collective-permute-start.3) | collective-permute-done | bytes 4128 | tf_op jit(solution)/shard_map/ppermute | solution.py:276
  113.9 2.4 %collective-permute-done.2 = f32[8,128]{1,0:T(8,128)S(1)} collective-permute-done((f32[8,128]{1,0:T(8,128)S(1)}, f32[8,128]{1,0:T(8,128)S(1)}, u32[]{:S(2)}, u32[]{:S(2)}) %collective-permute-start.2) | collective-permute-done | bytes 4128 | tf_op jit(solution)/shard_map/ppermute | solution.py:277
  116.3 0.6 maximum_select_fusion
  116.9 0.0 all-to-all-done.1
  116.9 0.2 convert_reduce_fusion
  117.1 0.8 broadcast_multiply_fusion
  (1 shorter events, 0.0 us)
Async XLA Ops:
  3.7 20.3 %copy-start.2 = (f32[32]{0:T(128)S(1)}, f32[32]{0:T(128)}, u32[]{:S(2)}) copy-start(f32[32]{0:T(128)} %param.13) | copy-start | bytes 388
  3.7 31.3 %all-to-all-start = ((bf16[16,24,2048]{2,1,0:T(8,128)(2,1)}), bf16[16,24,2048]{2,1,0:T(8,128)(2,1)S(1)}, u32[]{:S(2)}, u32[]{:S(2)}) async-start(bf16[16,24,2048]{2,1,0:T(8,128)(2,1)} %shard_map.104), calls=%async_computation | async-start | bytes 3145728 | tf_op jit(solution)/shard_map/all_to_all | solution.py:244
  12.8 16.9 %collective-permute-start.1 = (bf16[8,128]{1,0:T(8,128)(2,1)S(1)}, bf16[8,128]{1,0:T(8,128)(2,1)S(1)}, u32[]{:S(2)}, u32[]{:S(2)}) collective-permute-start(bf16[8,128]{1,0:T(8,128)(2,1)S(1)} %get-tuple-element.7), channel_id=1, source_target_pairs={{0,0},{1,8},{2,16},{3,24},{4,32},{5,40},{6,48},{7,56},{8,64},{9,72... | collective-permute-start | bytes 6152 | tf_op jit(solution)/shard_map/ppermute | solution.py:260
  17.9 14.0 %collective-permute-start = (bf16[8,128]{1,0:T(8,128)(2,1)S(1)}, bf16[8,128]{1,0:T(8,128)(2,1)S(1)}, u32[]{:S(2)}, u32[]{:S(2)}) collective-permute-start(bf16[8,128]{1,0:T(8,128)(2,1)S(1)} %get-tuple-element.6), channel_id=1, source_target_pairs={{0,4},{1,12},{2,20},{3,28},{4,36},{5,44},{6,52},{7,60},{8,68},{9,7... | collective-permute-start | bytes 6152 | tf_op jit(solution)/shard_map/ppermute | solution.py:261
  35.0 1.2 copy-start
  91.9 6.6 %copy-start.1 = (f32[8,256]{1,0:T(8,128)S(1)}, f32[8,256]{1,0:T(8,128)}, u32[]{:S(2)}) copy-start(f32[8,256]{1,0:T(8,128)} %get-tuple-element.5) | copy-start | bytes 24580
  91.9 25.0 %all-to-all-start.1 = ((bf16[16,8,4096]{2,1,0:T(8,128)(2,1)}), bf16[16,8,4096]{2,1,0:T(8,128)(2,1)S(1)}, u32[]{:S(2)}, u32[]{:S(2)}) async-start(bf16[16,8,4096]{2,1,0:T(8,128)(2,1)} %get-tuple-element.4), calls=%async_computation.1 | async-start | bytes 2097152 | tf_op jit(solution)/shard_map/all_to_all | solution.py:273
  98.5 15.4 %collective-permute-start.3 = (f32[8,128]{1,0:T(8,128)S(1)}, f32[8,128]{1,0:T(8,128)S(1)}, u32[]{:S(2)}, u32[]{:S(2)}) collective-permute-start(f32[8,128]{1,0:T(8,128)S(1)} %get-tuple-element.9), channel_id=1, source_target_pairs={{0,0},{8,1},{16,2},{24,3},{32,4},{40,5},{48,6},{56,7},{64,8},{72,9... | collective-permute-start | bytes 12296 | tf_op jit(solution)/shard_map/ppermute | solution.py:276
  101.4 14.9 %collective-permute-start.2 = (f32[8,128]{1,0:T(8,128)S(1)}, f32[8,128]{1,0:T(8,128)S(1)}, u32[]{:S(2)}, u32[]{:S(2)}) collective-permute-start(f32[8,128]{1,0:T(8,128)S(1)} %get-tuple-element.8), channel_id=1, source_target_pairs={{4,0},{12,1},{20,2},{28,3},{36,4},{44,5},{52,6},{60,7},{68,8},{76,... | collective-permute-start | bytes 12296 | tf_op jit(solution)/shard_map/ppermute | solution.py:277

commit v5 on v4

--- a/solution.py
+++ b/solution.py
@@ -25,31 +25,34 @@
     return high, low, split(x - high.astype(f32))[1]
 
 
-def rows_of(data):
-    half = data.shape[1]
-    loading = jnp.concatenate([data[0:8], data[8:16]], axis=1)
-    slot = jnp.concatenate([data[16:17], data[17:18]], axis=1)
-    notional = jnp.concatenate(
-        [data[18:19] + data[20:21], data[19:20] + data[21:22]], axis=1
-    )
-    return loading, slot, notional
-
-
-def lists_of(data, span_local, slots):
-    line = data[22:23]
-    local = slots - span_local
-    ends = [span_local]
-    for width in (local, local, local, slots, slots, slots):
-        ends.append(ends[-1] + width)
-    part = [line[:, lo:hi] for lo, hi in zip([0] + ends, ends)]
-    return part[0], part[1] + part[2] + part[3], part[4] + part[5] + part[6]
+def folded(row):
+    width = row.shape[1] // 8
+    return jnp.concatenate([row[:, at * width : (at + 1) * width] for at in range(8)], axis=0)
+
+
+def unfolded(block):
+    return jnp.concatenate([block[at : at + 1] for at in range(8)], axis=1)
+
+
+def rows_of(data, trades):
+    width = trades // 8
+    slot, high, low = (data[:, trades + at * width : trades + (at + 1) * width] for at in range(3))
+    return data[:, :trades], unfolded(slot), unfolded(high + low)
+
+
+def lists_of(data):
+    lists = data[:, data.shape[1] - 128 :]
+    constant = lists[4:6] + lists[6:8]
+    constant = jnp.concatenate([constant[0:1], constant[1:2]], axis=1)
+    return lists[0:1], lists[1:2] + lists[2:3] + lists[3:4], constant
 
 
 def pack_kernel(
     slots, first_ref, loading_ref, notional_ref, strike_ref, slot_ref, span_ref, loss_ref, sent_ref, own_ref, sem
 ):
-    devices, _, half = sent_ref.shape
+    devices = sent_ref.shape[0]
     group_dates = own_ref.shape[0]
+    quarters = devices // group_dates
     own = pltpu.make_async_copy(
         loading_ref.at[pl.ds(first_ref[0, 0], group_dates)], own_ref, sem
     )
@@ -61,46 +64,41 @@
     ids = lax.broadcasted_iota(jnp.int32, (slots, trades), 0).astype(f32)
     constant = jnp.where(ids == slot, amount, 0.0).sum(axis=1, keepdims=True)
     constant = jnp.broadcast_to(constant, (slots, 128)).T[0:1]
-    lists = [span_ref[...].astype(f32)]
-    for values in (loss_ref[...], constant):
-        lists += [part.astype(f32) for part in split3(values)]
-    lists = jnp.concatenate(lists, axis=1)
-    lists = jnp.concatenate([lists, jnp.zeros((1, half - lists.shape[1]), f32)], axis=1)
+    lists = [span_ref[...].astype(f32)] + [part.astype(f32) for part in split3(loss_ref[...])]
+    for part in split(constant):
+        part = part.astype(f32)
+        lists += [part[:, : slots // 2], part[:, slots // 2 :]]
     high, low = (part.astype(f32) for part in split(notional))
-    extra = jnp.concatenate(
-        [
-            row[:, start : start + half]
-            for row in (slot, high, low)
-            for start in (0, half)
-        ]
-        + [lists, jnp.zeros((1, half), f32)],
-        axis=0,
-    )
+    extra = [folded(row) for row in (slot, high, low)] + [jnp.concatenate(lists, axis=0)]
     own.wait()
     for date in range(group_dates):
-        loading = own_ref[date].astype(f32)
-        block = jnp.concatenate([loading[:, :half], loading[:, half:], extra], axis=0).astype(bf16)
-        for quarter in range(devices // group_dates):
-            sent_ref[date * (devices // group_dates) + quarter] = block
+        block = jnp.concatenate([own_ref[date].astype(f32)] + extra, axis=1).astype(bf16)
+        for quarter in range(quarters):
+            sent_ref[date * quarters + quarter] = block
 
 
 def table_of(slot, slots):
-    ids = lax.broadcasted_iota(jnp.int32, (slots, slot.shape[1]), 0).astype(f32)
-    return jnp.where(ids == slot, 1.0, 0.0).astype(bf16)
+    ids = lax.broadcasted_iota(jnp.int32, (slots, slot.shape[1]), 0).astype(f32).astype(bf16)
+    return jnp.where(ids == slot.astype(bf16), jnp.ones((), bf16), jnp.zeros((), bf16))
 
 
 def kernel(
+    scale,
     weight_ref,
-    trade_ref,
+    trade_in,
     row_ref,
     loss_ref,
     loading_out,
     factor_out,
     values_ref,
     slot_weight_ref,
+    trade_ref,
+    loading_ref,
+    trade_sem,
+    loading_sem,
 ):
-    shards, _, half = trade_ref.shape
-    trades = 2 * half
+    shards, _, width = trade_ref.shape
+    trades = loading_ref.shape[2]
     factors, paths = row_ref.shape
     slots = slot_weight_ref.shape[2]
     span_local = slots // 2
@@ -112,10 +110,25 @@
     def place(shard):
         return pl.ds(pl.multiple_of(shard * trades, trades), trades)
 
+    def copy_in(shard):
+        return pltpu.make_async_copy(trade_in.at[shard], trade_ref.at[shard], trade_sem.at[shard])
+
+    def copy_out(shard):
+        return pltpu.make_async_copy(
+            loading_ref.at[shard], loading_out.at[shard], loading_sem.at[shard]
+        )
+
+    def fetch(shard, carry):
+        copy_in(shard).start()
+        return carry
+
+    lax.fori_loop(0, shards, fetch, 0)
+
     def forward(shard, span_total):
+        copy_in(shard).wait()
         data = trade_ref[shard].astype(f32)
-        loading, slot, notional = rows_of(data)
-        names, loss, constant = lists_of(data, span_local, slots)
+        loading, slot, notional = rows_of(data, trades)
+        names, loss, constant = lists_of(data)
         both = jnp.concatenate(split(loading * log2e), axis=0)
         exponent = jnp.dot(column, both, preferred_element_type=f32)
         values = (notional * (jnp.exp2(exponent) - 1.0)).astype(bf16)
@@ -132,13 +145,13 @@
             )
         return span_total
 
-    span_total = lax.fori_loop(0, shards, forward, jnp.zeros((paths, span_count), f32))
+    span_total = lax.fori_loop(0, shards, forward, jnp.zeros((paths, span_count), f32), unroll=4)
     span_weight = (weight * loss_ref[...] * jax.nn.sigmoid(span_total / smoothing)).astype(bf16)
 
     def backward(shard, total):
         data = trade_ref[shard].astype(f32)
-        loading, slot, notional = rows_of(data)
-        names, _, _ = lists_of(data, span_local, slots)
+        loading, slot, notional = rows_of(data, trades)
+        names, _, _ = lists_of(data)
         slot_weight_ref[shard, :, :span_local] = jnp.dot(
             span_weight, table_of(names, span_count), preferred_element_type=f32
         ).astype(bf16)
@@ -147,15 +160,24 @@
         )
         scaled = values_ref[:, place(shard)].astype(f32) + notional
         sensitivity = (trade_weight * scaled).astype(bf16)
-        loading_out[shard] = jnp.dot(row, sensitivity, preferred_element_type=f32).astype(bf16)
+        paths_sum = jnp.dot(row, sensitivity, preferred_element_type=f32)
+        loading_ref[shard] = (paths_sum * scale).astype(bf16)
+        copy_out(shard).start()
         return total + lax.dot_general(
             loading.astype(bf16), sensitivity, nt, preferred_element_type=f32
         )
 
     factor_out[...] = lax.fori_loop(0, shards, backward, jnp.zeros((factors, paths), f32))
 
+    def drain(shard, carry):
+        copy_out(shard).wait()
+        return carry
+
+    lax.fori_loop(0, shards, drain, 0)
+
 
 vmem = pl.BlockSpec(memory_space=pltpu.VMEM)
+anywhere = pl.BlockSpec(memory_space=pl.ANY)
 smem = pl.BlockSpec(memory_space=pltpu.SMEM)
 params = pltpu.CompilerParams(vmem_limit_bytes=58 * 2**20)
 
@@ -165,8 +187,8 @@
     slots = span_list.shape[0] + loss_local.shape[0]
     return pl.pallas_call(
         functools.partial(pack_kernel, slots),
-        out_shape=jax.ShapeDtypeStruct((devices, 24, trades // 2), bf16),
-        in_specs=[smem, pl.BlockSpec(memory_space=pl.ANY)] + [vmem] * 5,
+        out_shape=jax.ShapeDtypeStruct((devices, factors, trades + 3 * (trades // 8) + 128), bf16),
+        in_specs=[smem, anywhere] + [vmem] * 5,
         out_specs=vmem,
         scratch_shapes=[
             pltpu.VMEM((group_dates, factors, trades), bf16),
@@ -184,21 +206,24 @@
     )
 
 
-def price_and_adjoint(weight, trade_data, factor_rows, loss_spanning, slots=256):
-    shards, _, half = trade_data.shape
-    trades = 2 * half
+def price_and_adjoint(weight, trade_data, factor_rows, loss_spanning, trades, slots, scale):
+    shards = trade_data.shape[0]
     factors, paths = factor_rows.shape
     return pl.pallas_call(
-        kernel,
+        functools.partial(kernel, scale),
         out_shape=(
             jax.ShapeDtypeStruct((shards, factors, trades), bf16),
             jax.ShapeDtypeStruct((factors, paths), f32),
         ),
-        in_specs=[smem, vmem, vmem, vmem],
-        out_specs=(vmem, vmem),
+        in_specs=[smem, pl.BlockSpec(memory_space=pltpu.HBM), vmem, vmem],
+        out_specs=(anywhere, vmem),
         scratch_shapes=[
             pltpu.VMEM((paths, shards * trades), bf16),
             pltpu.VMEM((shards, paths, slots), bf16),
+            pltpu.VMEM(trade_data.shape, bf16),
+            pltpu.VMEM((shards, factors, trades), bf16),
+            pltpu.SemaphoreType.DMA((shards,)),
+            pltpu.SemaphoreType.DMA((shards,)),
         ],
         compiler_params=params,
         cost_estimate=pl.CostEstimate(
@@ -268,7 +293,13 @@
     date_at = path_at * group_dates + trade_at // quarters
     weight = lax.dynamic_slice_in_dim(date_weight, date_at, 1).reshape(1, 1)
     loading_part, factor_part = price_and_adjoint(
-        weight, trade_data, factor_rows, loss_spanning[None, :]
+        weight,
+        trade_data,
+        factor_rows,
+        loss_spanning[None, :],
+        trades,
+        span_list.shape[0] + loss_local.shape[0],
+        1.0 / (path_devices * chunk),
     )
     loading_part = lax.all_to_all(loading_part, "trade", 0, 0, tiled=True)
     back = [[(to, origin) for origin, to in route] for route in routes]
@@ -278,7 +309,7 @@
     factor_grad = jnp.where(odd_path, jnp.stack([second, first]), jnp.stack([first, second]))
 
     loading_part = loading_part.reshape(group_dates, quarters, factor_count, trades)
-    loading_grad = loading_part.astype(f32).sum(axis=1) / (path_devices * chunk)
+    loading_grad = loading_part.astype(f32).sum(axis=1)
     return (loading_grad, factor_grad)
 
 

time: 118 us -> 115 us (0.975)
  Pallas kernels: 58.8 us -> 56.9 us
    pallas_call x1, Pallas kernels: 55.7 us -> 53.9 us  [price_and_adjoint(): pl.pallas_call(functools.partial(kernel, scale), out_shape=(jax.ShapeDtyp...]
where the time goes in v5:
time: 115 us
  Pallas kernels  56.9 us (49%)
  starting transfers between devices  33.2 us (29%)
  waiting for transfers between devices  19.4 us (17%)
  other arithmetic  2.86 us (2%)
  local copies, waits for them, and re-layouts  1.79 us (2%)
    pallas_call x1, Pallas kernels, price_and_adjoint(): pl.pallas_call(functools.partial(kernel, scale), out_shape=(jax.ShapeDtyp...  53.9 us
    all_to_all x1, starting transfers between devices, on_device(): trade_data = lax.all_to_all(sent, 'trade', 0, 0, tiled=True)  8.46 us
    ppermute x1, waiting for transfers between devices, on_device(): lax.ppermute(jnp.where(odd_date, right, left), ('path', 'trade'), back[0])  8.24 us
    all_to_all x1, starting transfers between devices, on_device(): loading_part = lax.all_to_all(loading_part, 'trade', 0, 0, tiled=True)  6.44 us
    ppermute x1, starting transfers between devices, on_device(): second = lax.ppermute(second, ('path', 'trade'), routes[1])  6.07 us
    ppermute x1, starting transfers between devices, on_device(): first = lax.ppermute(first, ('path', 'trade'), routes[0])  5.04 us
    ppermute x1, starting transfers between devices, on_device(): lax.ppermute(jnp.where(odd_date, left, right), ('path', 'trade'), back[1])  4.31 us
    ppermute x1, waiting for transfers between devices, on_device(): first = lax.ppermute(first, ('path', 'trade'), routes[0])  4.04 us
  transfers between devices with their start and end apart: 6, of which 5 were waited for; matrix products, arithmetic and copies ran while one was open for 2% of the time, Pallas kernels for 0%

profile of v5, /device:TPU:1, one launch (start us, length us, event | category | flops | bytes accessed | tf_op | source)
XLA Modules:
  0.0 114.8 jit_solution(5695488075759597018)
XLA Ops:
  0.6 3.0 %shard_map.104 = bf16[16,8,5760]{2,1,0:T(8,128)(2,1)} custom-call(s32[1,1]{1,0:T(1,128)} %bitcast.1.first_ref, bf16[32,8,4096]{2,1,0:T(8,128)(2,1)} %loading_ref.1, f32[1,4096]{1,0:T(1,128)} %bitcast.17, f32[1,4096]{1,0:T(1,128)} %bitcast.18, s32[1,4096]{1,0:T(1,128)} %bitcast.19, s32[1,128]{1,0:T(1,128)} %bitcast.22, f32[1,128]{1,0:T(1,128)} %bitcast.23), custom_call_target="tpu_custom_call" | custom-call | tf_op jit(solution)/shard_map/pallas_call | solution.py:188
  3.6 0.0 copy-start.2
  3.6 8.5 %all-to-all-start = ((bf16[16,8,5760]{2,1,0:T(8,128)(2,1)}), bf16[16,8,5760]{2,1,0:T(8,128)(2,1)S(1)}, u32[]{:S(2)}, u32[]{:S(2)}) async-start(bf16[16,8,5760]{2,1,0:T(8,128)(2,1)} %shard_map.104), calls=%async_computation | async-start | bytes 2949120 | tf_op jit(solution)/shard_map/all_to_all | solution.py:269
  12.1 0.7 select_bitcast_fusion.1
  12.8 5.0 %collective-permute-start.1 = (bf16[8,128]{1,0:T(8,128)(2,1)S(1)}, bf16[8,128]{1,0:T(8,128)(2,1)S(1)}, u32[]{:S(2)}, u32[]{:S(2)}) collective-permute-start(bf16[8,128]{1,0:T(8,128)(2,1)S(1)} %get-tuple-element.7), channel_id=1, source_target_pairs={{0,0},{1,8},{2,16},{3,24},{4,32},{5,40},{6,48},{7,56},{8,64},{9,72... | collective-permute-start | bytes 6152 | tf_op jit(solution)/shard_map/ppermute | solution.py:285
  17.8 6.1 %collective-permute-start = (bf16[8,128]{1,0:T(8,128)(2,1)S(1)}, bf16[8,128]{1,0:T(8,128)(2,1)S(1)}, u32[]{:S(2)}, u32[]{:S(2)}) collective-permute-start(bf16[8,128]{1,0:T(8,128)(2,1)S(1)} %get-tuple-element.6), channel_id=1, source_target_pairs={{0,4},{1,12},{2,20},{3,28},{4,36},{5,44},{6,52},{7,60},{8,68},{9,7... | collective-permute-start | bytes 6152 | tf_op jit(solution)/shard_map/ppermute | solution.py:286
  23.9 0.0 copy-done.2
  23.9 0.6 dynamic_slice.6
  24.6 4.0 %collective-permute-done.1 = bf16[8,128]{1,0:T(8,128)(2,1)S(1)} collective-permute-done((bf16[8,128]{1,0:T(8,128)(2,1)S(1)}, bf16[8,128]{1,0:T(8,128)(2,1)S(1)}, u32[]{:S(2)}, u32[]{:S(2)}) %collective-permute-start.1) | collective-permute-done | bytes 2080 | tf_op jit(solution)/shard_map/ppermute | solution.py:285
  28.6 2.2 %collective-permute-done = bf16[8,128]{1,0:T(8,128)(2,1)S(1)} collective-permute-done((bf16[8,128]{1,0:T(8,128)(2,1)S(1)}, bf16[8,128]{1,0:T(8,128)(2,1)S(1)}, u32[]{:S(2)}, u32[]{:S(2)}) %collective-permute-start) | collective-permute-done | bytes 2080 | tf_op jit(solution)/shard_map/ppermute | solution.py:286
  30.8 0.6 maximum_select_fusion.1.row_ref
  31.4 2.5 %all-to-all-done.trade_in = bf16[16,8,5760]{2,1,0:T(8,128)(2,1)S(1)} async-done(((bf16[16,8,5760]{2,1,0:T(8,128)(2,1)}), bf16[16,8,5760]{2,1,0:T(8,128)(2,1)S(1)}, u32[]{:S(2)}, u32[]{:S(2)}) %all-to-all-start) | async-done | bytes 1474592 | tf_op jit(solution)/shard_map/all_to_all | solution.py:269
  33.9 0.0 copy-start
  33.9 1.1 copy-done
  35.0 53.9 %shard_map.105 = (bf16[16,8,4096]{2,1,0:T(8,128)(2,1)}, f32[8,256]{1,0:T(8,128)}) custom-call(f32[1,1]{1,0:T(1,128)} %bitcast.weight_ref, bf16[16,8,5760]{2,1,0:T(8,128)(2,1)} %copy-done, bf16[8,256]{1,0:T(8,128)(2,1)} %maximum_select_fusion.1.row_ref, f32[1,256]{1,0:T(1,128)} %bitcast.24), custom_call_target="tpu_custom_call" | custom-call | flops 34359738368 | bytes 33554432 | tf_op jit(solution)/shard_map/pallas_call | solution.py:212
  88.9 0.0 copy-start.1
  88.9 6.4 %all-to-all-start.1 = ((bf16[16,8,4096]{2,1,0:T(8,128)(2,1)}), bf16[16,8,4096]{2,1,0:T(8,128)(2,1)S(1)}, u32[]{:S(2)}, u32[]{:S(2)}) async-start(bf16[16,8,4096]{2,1,0:T(8,128)(2,1)} %get-tuple-element.4), calls=%async_computation.1 | async-start | bytes 2097152 | tf_op jit(solution)/shard_map/all_to_all | solution.py:304
  95.4 0.0 copy-done.1
  95.4 2.9 %collective-permute-start.3 = (f32[8,128]{1,0:T(8,128)S(1)}, f32[8,128]{1,0:T(8,128)S(1)}, u32[]{:S(2)}, u32[]{:S(2)}) collective-permute-start(f32[8,128]{1,0:T(8,128)S(1)} %get-tuple-element.9), channel_id=1, source_target_pairs={{0,0},{8,1},{16,2},{24,3},{32,4},{40,5},{48,6},{56,7},{64,8},{72,9... | collective-permute-start | bytes 12296 | tf_op jit(solution)/shard_map/ppermute | solution.py:307
  98.3 4.3 %collective-permute-start.2 = (f32[8,128]{1,0:T(8,128)S(1)}, f32[8,128]{1,0:T(8,128)S(1)}, u32[]{:S(2)}, u32[]{:S(2)}) collective-permute-start(f32[8,128]{1,0:T(8,128)S(1)} %get-tuple-element.8), channel_id=1, source_target_pairs={{4,0},{12,1},{20,2},{28,3},{36,4},{44,5},{52,6},{60,7},{68,8},{76,... | collective-permute-start | bytes 12296 | tf_op jit(solution)/shard_map/ppermute | solution.py:308
  102.6 8.2 %collective-permute-done.3 = f32[8,128]{1,0:T(8,128)S(1)} collective-permute-done((f32[8,128]{1,0:T(8,128)S(1)}, f32[8,128]{1,0:T(8,128)S(1)}, u32[]{:S(2)}, u32[]{:S(2)}) %collective-permute-start.3) | collective-permute-done | bytes 4128 | tf_op jit(solution)/shard_map/ppermute | solution.py:307
  110.8 2.4 %collective-permute-done.2 = f32[8,128]{1,0:T(8,128)S(1)} collective-permute-done((f32[8,128]{1,0:T(8,128)S(1)}, f32[8,128]{1,0:T(8,128)S(1)}, u32[]{:S(2)}, u32[]{:S(2)}) %collective-permute-start.2) | collective-permute-done | bytes 4128 | tf_op jit(solution)/shard_map/ppermute | solution.py:308
  113.2 0.6 maximum_select_fusion
  113.8 0.0 all-to-all-done.1
  113.8 1.0 convert_reduce_fusion
  (1 shorter events, 0.0 us)
Async XLA Ops:
  3.6 20.3 %copy-start.2 = (f32[32]{0:T(128)S(1)}, f32[32]{0:T(128)}, u32[]{:S(2)}) copy-start(f32[32]{0:T(128)} %param.13) | copy-start | bytes 388
  3.6 30.3 %all-to-all-start = ((bf16[16,8,5760]{2,1,0:T(8,128)(2,1)}), bf16[16,8,5760]{2,1,0:T(8,128)(2,1)S(1)}, u32[]{:S(2)}, u32[]{:S(2)}) async-start(bf16[16,8,5760]{2,1,0:T(8,128)(2,1)} %shard_map.104), calls=%async_computation | async-start | bytes 2949120 | tf_op jit(solution)/shard_map/all_to_all | solution.py:269
  12.8 15.8 %collective-permute-start.1 = (bf16[8,128]{1,0:T(8,128)(2,1)S(1)}, bf16[8,128]{1,0:T(8,128)(2,1)S(1)}, u32[]{:S(2)}, u32[]{:S(2)}) collective-permute-start(bf16[8,128]{1,0:T(8,128)(2,1)S(1)} %get-tuple-element.7), channel_id=1, source_target_pairs={{0,0},{1,8},{2,16},{3,24},{4,32},{5,40},{6,48},{7,56},{8,64},{9,72... | collective-permute-start | bytes 6152 | tf_op jit(solution)/shard_map/ppermute | solution.py:285
  17.8 12.9 %collective-permute-start = (bf16[8,128]{1,0:T(8,128)(2,1)S(1)}, bf16[8,128]{1,0:T(8,128)(2,1)S(1)}, u32[]{:S(2)}, u32[]{:S(2)}) collective-permute-start(bf16[8,128]{1,0:T(8,128)(2,1)S(1)} %get-tuple-element.6), channel_id=1, source_target_pairs={{0,4},{1,12},{2,20},{3,28},{4,36},{5,44},{6,52},{7,60},{8,68},{9,7... | collective-permute-start | bytes 6152 | tf_op jit(solution)/shard_map/ppermute | solution.py:286
  33.9 1.1 copy-start
  88.9 6.5 %copy-start.1 = (f32[8,256]{1,0:T(8,128)S(1)}, f32[8,256]{1,0:T(8,128)}, u32[]{:S(2)}) copy-start(f32[8,256]{1,0:T(8,128)} %get-tuple-element.5) | copy-start | bytes 24580
  88.9 24.9 %all-to-all-start.1 = ((bf16[16,8,4096]{2,1,0:T(8,128)(2,1)}), bf16[16,8,4096]{2,1,0:T(8,128)(2,1)S(1)}, u32[]{:S(2)}, u32[]{:S(2)}) async-start(bf16[16,8,4096]{2,1,0:T(8,128)(2,1)} %get-tuple-element.4), calls=%async_computation.1 | async-start | bytes 2097152 | tf_op jit(solution)/shard_map/all_to_all | solution.py:304
  95.4 15.4 %collective-permute-start.3 = (f32[8,128]{1,0:T(8,128)S(1)}, f32[8,128]{1,0:T(8,128)S(1)}, u32[]{:S(2)}, u32[]{:S(2)}) collective-permute-start(f32[8,128]{1,0:T(8,128)S(1)} %get-tuple-element.9), channel_id=1, source_target_pairs={{0,0},{8,1},{16,2},{24,3},{32,4},{40,5},{48,6},{56,7},{64,8},{72,9... | collective-permute-start | bytes 12296 | tf_op jit(solution)/shard_map/ppermute | solution.py:307
  98.3 15.0 %collective-permute-start.2 = (f32[8,128]{1,0:T(8,128)S(1)}, f32[8,128]{1,0:T(8,128)S(1)}, u32[]{:S(2)}, u32[]{:S(2)}) collective-permute-start(f32[8,128]{1,0:T(8,128)S(1)} %get-tuple-element.8), channel_id=1, source_target_pairs={{4,0},{12,1},{20,2},{28,3},{36,4},{44,5},{52,6},{60,7},{68,8},{76,... | collective-permute-start | bytes 12296 | tf_op jit(solution)/shard_map/ppermute | solution.py:308

commit v6 on v5

--- a/solution.py
+++ b/solution.py
@@ -82,47 +82,50 @@
     return jnp.where(ids == slot.astype(bf16), jnp.ones((), bf16), jnp.zeros((), bf16))
 
 
-def kernel(
-    scale,
+def start_all(copy_of, count):
+    def start(shard, carry):
+        copy_of(shard).start()
+        return carry
+
+    lax.fori_loop(0, count, start, 0)
+
+
+def wait_all(copy_of, count):
+    def wait(shard, carry):
+        copy_of(shard).wait()
+        return carry
+
+    lax.fori_loop(0, count, wait, 0)
+
+
+def forward_kernel(
+    slots,
     weight_ref,
     trade_in,
     row_ref,
-    loss_ref,
-    loading_out,
-    factor_out,
+    values_out,
+    local_out,
+    span_out,
     values_ref,
-    slot_weight_ref,
     trade_ref,
-    loading_ref,
     trade_sem,
-    loading_sem,
+    values_sem,
 ):
-    shards, _, width = trade_ref.shape
-    trades = loading_ref.shape[2]
-    factors, paths = row_ref.shape
-    slots = slot_weight_ref.shape[2]
-    span_local = slots // 2
-    span_count = loss_ref.shape[1]
+    shards, paths, trades = values_ref.shape
+    span_count = span_out.shape[1]
+    span_local = slots - local_out.shape[2]
     weight = weight_ref[0, 0]
-    row = row_ref[...]
-    column = jnp.concatenate([row.astype(f32)] * 2, axis=0).T.astype(bf16)
-
-    def place(shard):
-        return pl.ds(pl.multiple_of(shard * trades, trades), trades)
+    column = jnp.concatenate([row_ref[...].astype(f32)] * 2, axis=0).T.astype(bf16)
 
     def copy_in(shard):
         return pltpu.make_async_copy(trade_in.at[shard], trade_ref.at[shard], trade_sem.at[shard])
 
     def copy_out(shard):
         return pltpu.make_async_copy(
-            loading_ref.at[shard], loading_out.at[shard], loading_sem.at[shard]
+            values_ref.at[shard], values_out.at[shard], values_sem.at[shard]
         )
 
-    def fetch(shard, carry):
-        copy_in(shard).start()
-        return carry
-
-    lax.fori_loop(0, shards, fetch, 0)
+    start_all(copy_in, shards)
 
     def forward(shard, span_total):
         copy_in(shard).wait()
@@ -132,12 +135,13 @@
         both = jnp.concatenate(split(loading * log2e), axis=0)
         exponent = jnp.dot(column, both, preferred_element_type=f32)
         values = (notional * (jnp.exp2(exponent) - 1.0)).astype(bf16)
-        values_ref[:, place(shard)] = values
+        values_ref[shard] = values
+        copy_out(shard).start()
         partial = constant + lax.dot_general(
             values, table_of(slot, slots), nt, preferred_element_type=f32
         )
         local = weight * loss * jax.nn.sigmoid(partial[:, span_local:] / smoothing)
-        slot_weight_ref[shard, :, span_local:] = local.astype(bf16)
+        local_out[shard] = local.astype(bf16)
         table = table_of(names, span_count)
         for part in split(partial[:, :span_local]):
             span_total = span_total + lax.dot_general(
@@ -145,20 +149,68 @@
             )
         return span_total
 
-    span_total = lax.fori_loop(0, shards, forward, jnp.zeros((paths, span_count), f32), unroll=4)
+    span_out[...] = lax.fori_loop(
+        0, shards, forward, jnp.zeros((paths, span_count), f32), unroll=2
+    )
+    wait_all(copy_out, shards)
+
+
+def backward_kernel(
+    scale,
+    weight_ref,
+    trade_in,
+    row_ref,
+    loss_ref,
+    span_ref,
+    other_ref,
+    local_ref,
+    values_in,
+    loading_out,
+    factor_out,
+    values_ref,
+    trade_ref,
+    loading_ref,
+    trade_sem,
+    values_sem,
+    loading_sem,
+):
+    shards, paths, trades = values_ref.shape
+    factors = row_ref.shape[0]
+    span_count = loss_ref.shape[1]
+    slots = 2 * local_ref.shape[2]
+    weight = weight_ref[0, 0]
+    row = row_ref[...]
+
+    def copy_in(shard):
+        return pltpu.make_async_copy(trade_in.at[shard], trade_ref.at[shard], trade_sem.at[shard])
+
+    def copy_values(shard):
+        return pltpu.make_async_copy(
+            values_in.at[shard], values_ref.at[shard], values_sem.at[shard]
+        )
+
+    def copy_out(shard):
+        return pltpu.make_async_copy(
+            loading_ref.at[shard], loading_out.at[shard], loading_sem.at[shard]
+        )
+
+    start_all(copy_in, shards)
+    start_all(copy_values, shards)
+    span_total = span_ref[...] + other_ref[...]
     span_weight = (weight * loss_ref[...] * jax.nn.sigmoid(span_total / smoothing)).astype(bf16)
 
     def backward(shard, total):
+        copy_in(shard).wait()
+        copy_values(shard).wait()
         data = trade_ref[shard].astype(f32)
         loading, slot, notional = rows_of(data, trades)
         names, _, _ = lists_of(data)
-        slot_weight_ref[shard, :, :span_local] = jnp.dot(
+        span_slots = jnp.dot(
             span_weight, table_of(names, span_count), preferred_element_type=f32
         ).astype(bf16)
-        trade_weight = jnp.dot(
-            slot_weight_ref[shard], table_of(slot, slots), preferred_element_type=f32
-        )
-        scaled = values_ref[:, place(shard)].astype(f32) + notional
+        slot_weight = jnp.concatenate([span_slots, local_ref[shard]], axis=1)
+        trade_weight = jnp.dot(slot_weight, table_of(slot, slots), preferred_element_type=f32)
+        scaled = values_ref[shard].astype(f32) + notional
         sensitivity = (trade_weight * scaled).astype(bf16)
         paths_sum = jnp.dot(row, sensitivity, preferred_element_type=f32)
         loading_ref[shard] = (paths_sum * scale).astype(bf16)
@@ -167,17 +219,13 @@
             loading.astype(bf16), sensitivity, nt, preferred_element_type=f32
         )
 
-    factor_out[...] = lax.fori_loop(0, shards, backward, jnp.zeros((factors, paths), f32))
-
-    def drain(shard, carry):
-        copy_out(shard).wait()
-        return carry
-
-    lax.fori_loop(0, shards, drain, 0)
+    factor_out[...] = lax.fori_loop(0, shards, backward, jnp.zeros((factors, paths), f32), unroll=2)
+    wait_all(copy_out, shards)
 
 
 vmem = pl.BlockSpec(memory_space=pltpu.VMEM)
 anywhere = pl.BlockSpec(memory_space=pl.ANY)
+dma = pltpu.SemaphoreType.DMA
 smem = pl.BlockSpec(memory_space=pltpu.SMEM)
 params = pltpu.CompilerParams(vmem_limit_bytes=58 * 2**20)
 
@@ -206,32 +254,49 @@
     )
 
 
-def price_and_adjoint(weight, trade_data, factor_rows, loss_spanning, trades, slots, scale):
+def price(weight, trade_data, factor_rows, trades, local_count, slots, span_count):
     shards = trade_data.shape[0]
-    factors, paths = factor_rows.shape
+    paths = factor_rows.shape[1]
     return pl.pallas_call(
-        functools.partial(kernel, scale),
+        functools.partial(forward_kernel, slots),
+        out_shape=(
+            jax.ShapeDtypeStruct((shards, paths, trades), bf16),
+            jax.ShapeDtypeStruct((shards, paths, local_count), bf16),
+            jax.ShapeDtypeStruct((paths, span_count), f32),
+        ),
+        in_specs=[smem, anywhere, vmem],
+        out_specs=(anywhere, vmem, vmem),
+        scratch_shapes=[
+            pltpu.VMEM((shards, paths, trades), bf16),
+            pltpu.VMEM(trade_data.shape, bf16),
+            dma((shards,)),
+            dma((shards,)),
+        ],
+        compiler_params=params,
+    )(weight, trade_data, factor_rows)
+
+
+def adjoint(weight, trade_data, factor_rows, loss_spanning, span, other, local, values, scale):
+    shards, paths, trades = values.shape
+    factors = factor_rows.shape[0]
+    return pl.pallas_call(
+        functools.partial(backward_kernel, scale),
         out_shape=(
             jax.ShapeDtypeStruct((shards, factors, trades), bf16),
             jax.ShapeDtypeStruct((factors, paths), f32),
         ),
-        in_specs=[smem, pl.BlockSpec(memory_space=pltpu.HBM), vmem, vmem],
+        in_specs=[smem, anywhere] + [vmem] * 5 + [anywhere],
         out_specs=(anywhere, vmem),
         scratch_shapes=[
-            pltpu.VMEM((paths, shards * trades), bf16),
-            pltpu.VMEM((shards, paths, slots), bf16),
+            pltpu.VMEM(values.shape, bf16),
             pltpu.VMEM(trade_data.shape, bf16),
             pltpu.VMEM((shards, factors, trades), bf16),
-            pltpu.SemaphoreType.DMA((shards,)),
-            pltpu.SemaphoreType.DMA((shards,)),
+            dma((shards,)),
+            dma((shards,)),
+            dma((shards,)),
         ],
         compiler_params=params,
-        cost_estimate=pl.CostEstimate(
-            flops=shards * trades * paths * 2 * 256 * 4,
-            bytes_accessed=shards * trades * paths * 2,
-            transcendentals=shards * trades * paths,
-        ),
-    )(weight, trade_data, factor_rows, loss_spanning)
+    )(weight, trade_data, factor_rows, loss_spanning, span, other, local, values)
 
 
 def on_device(
@@ -252,7 +317,12 @@
     dates, factor_count, chunk = factors.shape
     trades = loadings.shape[2]
     group_dates = dates // path_devices
-    quarters = trade_devices // group_dates
+    columns = trade_devices // 2
+    halves = columns // group_dates
+    chunks = path_devices // halves
+    slots = span_list.shape[0] + loss_local.shape[0]
+    sides = [[2 * at + side for at in range(columns)] for side in range(2)]
+    partner = [(at, at ^ 1) for at in range(trade_devices)]
 
     first_date = (path_at * group_dates).astype(jnp.int32).reshape(1, 1)
     sent = pack(
@@ -263,52 +333,80 @@
         trade_slot,
         span_list,
         loss_local,
-        trade_devices,
+        columns,
         group_dates,
     )
-    trade_data = lax.all_to_all(sent, "trade", 0, 0, tiled=True)
-
-    routes = []
-    for turn in range(2):
-        route = []
-        for a in range(path_devices):
-            for b in range(trade_devices):
-                date = 2 * b + (a + turn) % 2
-                to = (date // group_dates) * trade_devices + (date % group_dates) * quarters + a // 2
-                route.append((a * trade_devices + b, to))
-        routes.append(route)
+    trade_data = lax.all_to_all(sent, "trade", 0, 0, axis_index_groups=sides, tiled=True)
+
+    axes = ("path", "trade")
+    routes = {}
+    for high in range(2):
+        for low in range(2):
+            route = []
+            for a in range(path_devices):
+                for b in range(trade_devices):
+                    date = 2 * b + (((a // 2) % 2) ^ high)
+                    column = (date % group_dates) * halves + a // chunks
+                    to = (date // group_dates) * trade_devices + 2 * column + ((a % 2) ^ low)
+                    route.append((a * trade_devices + b, to))
+            routes[high, low] = route
     mine = lax.dynamic_slice_in_dim(factors, 2 * trade_at, 2, 0)
-    odd_path = path_at % 2 == 1
-    odd_date = (trade_at // quarters) % 2 == 1
-    first = jnp.where(odd_path, mine[1], mine[0])
-    second = jnp.where(odd_path, mine[0], mine[1])
-    first = lax.ppermute(first, ("path", "trade"), routes[0])
-    second = lax.ppermute(second, ("path", "trade"), routes[1])
-    factor_rows = jnp.where(
-        odd_date,
-        jnp.concatenate([second, first], axis=1),
-        jnp.concatenate([first, second], axis=1),
-    )
-
-    date_at = path_at * group_dates + trade_at // quarters
+    odd_pair = (path_at // 2) % 2 == 1
+    ready = (
+        jnp.where(odd_pair, mine[1], mine[0]),
+        jnp.where(odd_pair, mine[0], mine[1]),
+    )
+    came = {at: lax.ppermute(ready[at[0]], axes, route) for at, route in routes.items()}
+    column_at = trade_at // 2
+    odd_date = (column_at // halves) % 2 == 1
+    odd_core = trade_at % 2 == 1
+
+    def ordered(grid):
+        rows = [
+            [jnp.where(odd_date, grid[1 - high, low], grid[high, low]) for low in range(2)]
+            for high in range(2)
+        ]
+        return {
+            (high, low): jnp.where(odd_core, rows[high][1 - low], rows[high][low])
+            for high in range(2)
+            for low in range(2)
+        }
+
+    places = [(0, 0), (0, 1), (1, 0), (1, 1)]
+    grid = ordered(came)
+    factor_rows = jnp.concatenate([grid[at] for at in places], axis=1)
+
+    date_at = path_at * group_dates + column_at // halves
     weight = lax.dynamic_slice_in_dim(date_weight, date_at, 1).reshape(1, 1)
-    loading_part, factor_part = price_and_adjoint(
+    values, local, span = price(
+        weight, trade_data, factor_rows, trades, loss_local.shape[0], slots, loss_spanning.shape[0]
+    )
+    other = lax.ppermute(span, "trade", partner)
+    loading_part, factor_part = adjoint(
         weight,
         trade_data,
         factor_rows,
         loss_spanning[None, :],
-        trades,
-        span_list.shape[0] + loss_local.shape[0],
+        span,
+        other,
+        local,
+        values,
         1.0 / (path_devices * chunk),
     )
-    loading_part = lax.all_to_all(loading_part, "trade", 0, 0, tiled=True)
-    back = [[(to, origin) for origin, to in route] for route in routes]
-    left, right = factor_part[:, :chunk], factor_part[:, chunk:]
-    first = lax.ppermute(jnp.where(odd_date, right, left), ("path", "trade"), back[0])
-    second = lax.ppermute(jnp.where(odd_date, left, right), ("path", "trade"), back[1])
-    factor_grad = jnp.where(odd_path, jnp.stack([second, first]), jnp.stack([first, second]))
-
-    loading_part = loading_part.reshape(group_dates, quarters, factor_count, trades)
+    loading_part = lax.all_to_all(
+        loading_part, "trade", 0, 0, axis_index_groups=sides, tiled=True
+    )
+
+    parts = {at: factor_part[:, k * chunk : (k + 1) * chunk] for k, at in enumerate(places)}
+    leaving = ordered(parts)
+    came = {
+        at: lax.ppermute(leaving[at], axes, [(to, origin) for origin, to in route])
+        for at, route in routes.items()
+    }
+    same, opposite = (came[high, 0] + came[high, 1] for high in range(2))
+    factor_grad = jnp.where(odd_pair, jnp.stack([opposite, same]), jnp.stack([same, opposite]))
+
+    loading_part = loading_part.reshape(group_dates, halves, factor_count, trades)
     loading_grad = loading_part.astype(f32).sum(axis=1)
     return (loading_grad, factor_grad)
 

time: 115 us -> 121 us (1.052)
  the two profiles are of different devices: /device:TPU:1 before, /device:TPU:97 now
where the time goes in v6:
time: 121 us; the launch traced here: 120 us
  Pallas kernels  59.7 us (49%)
  starting transfers between devices  39.3 us (32%)
  waiting for transfers between devices  13.8 us (11%)
  other arithmetic  3.49 us (3%)
  local copies, waits for them, and re-layouts  2.98 us (2%)
    pallas_call x1, Pallas kernels, adjoint(): pl.pallas_call(functools.partial(backward_kernel, scale), out_shape=(jax....  30.5 us
    pallas_call x1, Pallas kernels, price(): pl.pallas_call(functools.partial(forward_kernel, slots), out_shape=(jax.S...  26.5 us
    ppermute x4, starting transfers between devices, on_device(): lax.ppermute(leaving[at], axes, [(to, origin) for origin, to in route])  15.2 us
    ppermute x4, starting transfers between devices, on_device(): lax.ppermute(ready[at[0]], axes, route)  13.7 us
    all_to_all x1, starting transfers between devices, on_device(): lax.all_to_all(sent, 'trade', 0, 0, axis_index_groups=sides, tiled=True)  6.66 us
    ppermute x4, waiting for transfers between devices, on_device(): lax.ppermute(leaving[at], axes, [(to, origin) for origin, to in route])  6.4 us
    ppermute x4, waiting for transfers between devices, on_device(): lax.ppermute(ready[at[0]], axes, route)  5.29 us
    all_to_all x1, starting transfers between devices, on_device(): lax.all_to_all(loading_part, 'trade', 0, 0, axis_index_groups=sides, tile...  3.49 us
  transfers between devices with their start and end apart: 11, of which 5 were waited for; matrix products, arithmetic and copies ran while one was open for 3% of the time, Pallas kernels for 0%

profile of v6, /device:TPU:97, one launch (start us, length us, event | category | flops | bytes accessed | tf_op | source)
XLA Modules:
  0.0 120.0 jit_solution(6447021281267550935)
XLA Ops:
  0.6 2.7 %shard_map.104 = bf16[8,8,5760]{2,1,0:T(8,128)(2,1)} custom-call(s32[1,1]{1,0:T(1,128)} %bitcast.1.first_ref, bf16[32,8,4096]{2,1,0:T(8,128)(2,1)} %loading_ref.1, f32[1,4096]{1,0:T(1,128)} %bitcast.19, f32[1,4096]{1,0:T(1,128)} %bitcast.20, s32[1,4096]{1,0:T(1,128)} %bitcast.21, s32[1,128]{1,0:T(1,128)} %bitcast.23, f32[1,128]{1,0:T(1,128)} %bitcast.24), custom_call_target="tpu_custom_call" | custom-call | tf_op jit(solution)/shard_map/pallas_call | solution.py:236
  3.3 6.7 %all-to-all-start = ((bf16[8,8,5760]{2,1,0:T(8,128)(2,1)}), bf16[8,8,5760]{2,1,0:T(8,128)(2,1)S(1)}, u32[]{:S(2)}, u32[]{:S(2)}) async-start(bf16[8,8,5760]{2,1,0:T(8,128)(2,1)} %shard_map.104), calls=%async_computation | async-start | bytes 1474560 | tf_op jit(solution)/shard_map/all_to_all | solution.py:339
  10.0 0.7 select_bitcast_fusion.1
  10.7 3.6 %collective-permute-start.2 = (bf16[8,128]{1,0:T(8,128)(2,1)S(1)}, bf16[8,128]{1,0:T(8,128)(2,1)S(1)}, u32[]{:S(2)}, u32[]{:S(2)}) collective-permute-start(bf16[8,128]{1,0:T(8,128)(2,1)S(1)} %get-tuple-element.12), channel_id=1, source_target_pairs={{0,4},{1,12},{2,20},{3,28},{4,36},{5,44},{6,52},{7,60},{8,68},{9,7... | collective-permute-start | bytes 6152 | tf_op jit(solution)/shard_map/ppermute | solution.py:359
  14.3 5.1 %collective-permute-start = (bf16[8,128]{1,0:T(8,128)(2,1)S(1)}, bf16[8,128]{1,0:T(8,128)(2,1)S(1)}, u32[]{:S(2)}, u32[]{:S(2)}) collective-permute-start(bf16[8,128]{1,0:T(8,128)(2,1)S(1)} %get-tuple-element.12), channel_id=1, source_target_pairs={{0,5},{1,13},{2,21},{3,29},{4,37},{5,45},{6,53},{7,61},{8,69},{9,7... | collective-permute-start | bytes 6152 | tf_op jit(solution)/shard_map/ppermute | solution.py:359
  19.5 2.4 %collective-permute-start.3 = (bf16[8,128]{1,0:T(8,128)(2,1)S(1)}, bf16[8,128]{1,0:T(8,128)(2,1)S(1)}, u32[]{:S(2)}, u32[]{:S(2)}) collective-permute-start(bf16[8,128]{1,0:T(8,128)(2,1)S(1)} %get-tuple-element.13), channel_id=1, source_target_pairs={{0,0},{1,8},{2,16},{3,24},{4,32},{5,40},{6,48},{7,56},{8,64},{9,72... | collective-permute-start | bytes 6152 | tf_op jit(solution)/shard_map/ppermute | solution.py:359
  21.8 2.5 %collective-permute-start.1 = (bf16[8,128]{1,0:T(8,128)(2,1)S(1)}, bf16[8,128]{1,0:T(8,128)(2,1)S(1)}, u32[]{:S(2)}, u32[]{:S(2)}) collective-permute-start(bf16[8,128]{1,0:T(8,128)(2,1)S(1)} %get-tuple-element.13), channel_id=1, source_target_pairs={{0,1},{1,9},{2,17},{3,25},{4,33},{5,41},{6,49},{7,57},{8,65},{9,73... | collective-permute-start | bytes 6152 | tf_op jit(solution)/shard_map/ppermute | solution.py:359
  24.4 1.3 %dynamic_slice.6 = f32[1]{0:T(128)} dynamic-slice(f32[32]{0:T(128)} %param.13, s32[]{:T(128)S(6)} %select_n.130), dynamic_slice_sizes={1} | dynamic-slice | bytes 12 | tf_op jit(solution)/shard_map/dynamic_slice | solution.py:380
  25.6 0.0 collective-permute-done.2
  25.6 0.0 collective-permute-done
  25.6 4.4 %collective-permute-done.3 = bf16[8,128]{1,0:T(8,128)(2,1)S(1)} collective-permute-done((bf16[8,128]{1,0:T(8,128)(2,1)S(1)}, bf16[8,128]{1,0:T(8,128)(2,1)S(1)}, u32[]{:S(2)}, u32[]{:S(2)}) %collective-permute-start.3) | collective-permute-done | bytes 2080 | tf_op jit(solution)/shard_map/ppermute | solution.py:359
  30.1 0.9 collective-permute-done.1
  30.9 0.6 pad_maximum_fusion.row_ref
  31.5 0.0 all-to-all-done.trade_in
  31.5 0.0 copy-start
  31.5 0.9 copy-done
  32.4 26.5 %shard_map.105 = (bf16[8,512,4096]{2,1,0:T(8,128)(2,1)}, bf16[8,512,128]{2,1,0:T(8,128)(2,1)}, f32[512,256]{1,0:T(8,128)}) custom-call(f32[1,1]{1,0:T(1,128)} %bitcast.weight_ref, bf16[8,8,5760]{2,1,0:T(8,128)(2,1)} %copy-done, bf16[8,512]{1,0:T(8,128)(2,1)} %pad_maximum_fusion.row_ref), custom_call_target="tpu_custom_call" | custom-call | tf_op jit(solution)/shard_map/pallas_call | solution.py:260
  59.0 0.3 collective-permute-start.4
  59.3 2.1 %collective-permute-done.4.other_ref = f32[512,256]{1,0:T(8,128)S(1)} collective-permute-done((f32[512,256]{1,0:T(8,128)}, f32[512,256]{1,0:T(8,128)S(1)}, u32[]{:S(2)}, u32[]{:S(2)}) %collective-permute-start.4) | collective-permute-done | bytes 524320 | tf_op jit(solution)/shard_map/ppermute | solution.py:384
  61.4 0.0 copy-start.1
  61.4 0.8 copy-done.1
  62.2 30.5 %shard_map.106 = (bf16[8,8,4096]{2,1,0:T(8,128)(2,1)}, f32[8,512]{1,0:T(8,128)}) custom-call(f32[1,1]{1,0:T(1,128)} %bitcast.weight_ref, bf16[8,8,5760]{2,1,0:T(8,128)(2,1)} %copy-done, bf16[8,512]{1,0:T(8,128)(2,1)} %pad_maximum_fusion.row_ref, f32[1,256]{1,0:T(1,128)} %bitcast.22, f32[512,256]{1,0:T(8,128)} %get-tuple-element.7.span_ref, ...), custom_call_target="tpu_custom_call" | custom-call | tf_op jit(solution)/shard_map/pallas_call | solution.py:282
  92.7 0.7 broadcast_select_fusion.6
  93.4 0.0 collective-permute-start.6
  93.4 5.4 %collective-permute-start.5 = (f32[8,128]{1,0:T(8,128)S(1)}, f32[8,128]{1,0:T(8,128)S(1)}, u32[]{:S(2)}, u32[]{:S(2)}) collective-permute-start(f32[8,128]{1,0:T(8,128)S(1)} %get-tuple-element.15), channel_id=1, source_target_pairs={{4,0},{12,1},{20,2},{28,3},{36,4},{44,5},{52,6},{60,7},{68,8},{76,... | collective-permute-start | bytes 12296 | tf_op jit(solution)/shard_map/ppermute | solution.py:403
  98.8 3.5 %all-to-all-start.1 = ((bf16[8,8,4096]{2,1,0:T(8,128)(2,1)}), bf16[8,8,4096]{2,1,0:T(8,128)(2,1)S(1)}, u32[]{:S(2)}, u32[]{:S(2)}) async-start(bf16[8,8,4096]{2,1,0:T(8,128)(2,1)} %get-tuple-element.10), calls=%async_computation.1 | async-start | bytes 1048576 | tf_op jit(solution)/shard_map/all_to_all | solution.py:396
  102.3 8.0 %collective-permute-start.7 = (f32[8,128]{1,0:T(8,128)S(1)}, f32[8,128]{1,0:T(8,128)S(1)}, u32[]{:S(2)}, u32[]{:S(2)}) collective-permute-start(f32[8,128]{1,0:T(8,128)S(1)} %get-tuple-element.16), channel_id=1, source_target_pairs={{0,0},{8,1},{16,2},{24,3},{32,4},{40,5},{48,6},{56,7},{64,8},{72,9... | collective-permute-start | bytes 12296 | tf_op jit(solution)/shard_map/ppermute | solution.py:403
  110.2 1.9 %collective-permute-start.8 = (f32[8,128]{1,0:T(8,128)S(1)}, f32[8,128]{1,0:T(8,128)S(1)}, u32[]{:S(2)}, u32[]{:S(2)}) collective-permute-start(f32[8,128]{1,0:T(8,128)S(1)} %get-tuple-element.17), channel_id=1, source_target_pairs={{1,0},{9,1},{17,2},{25,3},{33,4},{41,5},{49,6},{57,7},{65,8},{73,9... | collective-permute-start | bytes 12296 | tf_op jit(solution)/shard_map/ppermute | solution.py:403
  112.1 0.0 collective-permute-done.6
  112.1 0.0 collective-permute-done.5
  112.1 2.0 %collective-permute-done.7 = f32[8,128]{1,0:T(8,128)S(1)} collective-permute-done((f32[8,128]{1,0:T(8,128)S(1)}, f32[8,128]{1,0:T(8,128)S(1)}, u32[]{:S(2)}, u32[]{:S(2)}) %collective-permute-start.7) | collective-permute-done | bytes 4128 | tf_op jit(solution)/shard_map/ppermute | solution.py:403
  114.2 4.3 %collective-permute-done.8 = f32[8,128]{1,0:T(8,128)S(1)} collective-permute-done((f32[8,128]{1,0:T(8,128)S(1)}, f32[8,128]{1,0:T(8,128)S(1)}, u32[]{:S(2)}, u32[]{:S(2)}) %collective-permute-start.8) | collective-permute-done | bytes 4128 | tf_op jit(solution)/shard_map/ppermute | solution.py:403
  118.5 0.6 maximum_select_fusion
  119.1 0.0 all-to-all-done.1
  119.1 0.9 convert_reduce_fusion
  (3 shorter events, 0.0 us)
Async XLA Ops:
  3.3 28.2 %all-to-all-start = ((bf16[8,8,5760]{2,1,0:T(8,128)(2,1)}), bf16[8,8,5760]{2,1,0:T(8,128)(2,1)S(1)}, u32[]{:S(2)}, u32[]{:S(2)}) async-start(bf16[8,8,5760]{2,1,0:T(8,128)(2,1)} %shard_map.104), calls=%async_computation | async-start | bytes 1474560 | tf_op jit(solution)/shard_map/all_to_all | solution.py:339
  10.7 14.9 %collective-permute-start.2 = (bf16[8,128]{1,0:T(8,128)(2,1)S(1)}, bf16[8,128]{1,0:T(8,128)(2,1)S(1)}, u32[]{:S(2)}, u32[]{:S(2)}) collective-permute-start(bf16[8,128]{1,0:T(8,128)(2,1)S(1)} %get-tuple-element.12), channel_id=1, source_target_pairs={{0,4},{1,12},{2,20},{3,28},{4,36},{5,44},{6,52},{7,60},{8,68},{9,7... | collective-permute-start | bytes 6152 | tf_op jit(solution)/shard_map/ppermute | solution.py:359
  14.3 11.3 %collective-permute-start = (bf16[8,128]{1,0:T(8,128)(2,1)S(1)}, bf16[8,128]{1,0:T(8,128)(2,1)S(1)}, u32[]{:S(2)}, u32[]{:S(2)}) collective-permute-start(bf16[8,128]{1,0:T(8,128)(2,1)S(1)} %get-tuple-element.12), channel_id=1, source_target_pairs={{0,5},{1,13},{2,21},{3,29},{4,37},{5,45},{6,53},{7,61},{8,69},{9,7... | collective-permute-start | bytes 6152 | tf_op jit(solution)/shard_map/ppermute | solution.py:359
  19.5 10.6 %collective-permute-start.3 = (bf16[8,128]{1,0:T(8,128)(2,1)S(1)}, bf16[8,128]{1,0:T(8,128)(2,1)S(1)}, u32[]{:S(2)}, u32[]{:S(2)}) collective-permute-start(bf16[8,128]{1,0:T(8,128)(2,1)S(1)} %get-tuple-element.13), channel_id=1, source_target_pairs={{0,0},{1,8},{2,16},{3,24},{4,32},{5,40},{6,48},{7,56},{8,64},{9,72... | collective-permute-start | bytes 6152 | tf_op jit(solution)/shard_map/ppermute | solution.py:359
  21.8 9.1 %collective-permute-start.1 = (bf16[8,128]{1,0:T(8,128)(2,1)S(1)}, bf16[8,128]{1,0:T(8,128)(2,1)S(1)}, u32[]{:S(2)}, u32[]{:S(2)}) collective-permute-start(bf16[8,128]{1,0:T(8,128)(2,1)S(1)} %get-tuple-element.13), channel_id=1, source_target_pairs={{0,1},{1,9},{2,17},{3,25},{4,33},{5,41},{6,49},{7,57},{8,65},{9,73... | collective-permute-start | bytes 6152 | tf_op jit(solution)/shard_map/ppermute | solution.py:359
  31.5 0.9 copy-start
  59.0 2.4 %collective-permute-start.4 = (f32[512,256]{1,0:T(8,128)}, f32[512,256]{1,0:T(8,128)S(1)}, u32[]{:S(2)}, u32[]{:S(2)}) collective-permute-start(f32[512,256]{1,0:T(8,128)} %get-tuple-element.7.span_ref), channel_id=1, source_target_pairs={{0,1},{1,0},{2,3},{3,2},{4,5},{5,4},{6,7},{7,6},{8,9},{9,8},{10,11... | collective-permute-start | bytes 1572872 | tf_op jit(solution)/shard_map/ppermute | solution.py:384
  61.4 0.8 copy-start.1
  93.4 18.7 %collective-permute-start.6 = (f32[8,128]{1,0:T(8,128)S(1)}, f32[8,128]{1,0:T(8,128)S(1)}, u32[]{:S(2)}, u32[]{:S(2)}) collective-permute-start(f32[8,128]{1,0:T(8,128)S(1)} %get-tuple-element.14), channel_id=1, source_target_pairs={{5,0},{13,1},{21,2},{29,3},{37,4},{45,5},{53,6},{61,7},{69,8},{77,... | collective-permute-start | bytes 12296 | tf_op jit(solution)/shard_map/ppermute | solution.py:403
  93.4 18.7 %collective-permute-start.5 = (f32[8,128]{1,0:T(8,128)S(1)}, f32[8,128]{1,0:T(8,128)S(1)}, u32[]{:S(2)}, u32[]{:S(2)}) collective-permute-start(f32[8,128]{1,0:T(8,128)S(1)} %get-tuple-element.15), channel_id=1, source_target_pairs={{4,0},{12,1},{20,2},{28,3},{36,4},{44,5},{52,6},{60,7},{68,8},{76,... | collective-permute-start | bytes 12296 | tf_op jit(solution)/shard_map/ppermute | solution.py:403
  98.8 20.3 %all-to-all-start.1 = ((bf16[8,8,4096]{2,1,0:T(8,128)(2,1)}), bf16[8,8,4096]{2,1,0:T(8,128)(2,1)S(1)}, u32[]{:S(2)}, u32[]{:S(2)}) async-start(bf16[8,8,4096]{2,1,0:T(8,128)(2,1)} %get-tuple-element.10), calls=%async_computation.1 | async-start | bytes 1048576 | tf_op jit(solution)/shard_map/all_to_all | solution.py:396
  102.3 11.9 %collective-permute-start.7 = (f32[8,128]{1,0:T(8,128)S(1)}, f32[8,128]{1,0:T(8,128)S(1)}, u32[]{:S(2)}, u32[]{:S(2)}) collective-permute-start(f32[8,128]{1,0:T(8,128)S(1)} %get-tuple-element.16), channel_id=1, source_target_pairs={{0,0},{8,1},{16,2},{24,3},{32,4},{40,5},{48,6},{56,7},{64,8},{72,9... | collective-permute-start | bytes 12296 | tf_op jit(solution)/shard_map/ppermute | solution.py:403
  110.2 8.3 %collective-permute-start.8 = (f32[8,128]{1,0:T(8,128)S(1)}, f32[8,128]{1,0:T(8,128)S(1)}, u32[]{:S(2)}, u32[]{:S(2)}) collective-permute-start(f32[8,128]{1,0:T(8,128)S(1)} %get-tuple-element.17), channel_id=1, source_target_pairs={{1,0},{9,1},{17,2},{25,3},{33,4},{41,5},{49,6},{57,7},{65,8},{73,9... | collective-permute-start | bytes 12296 | tf_op jit(solution)/shard_map/ppermute | solution.py:403

commit v7 on v5

--- a/solution.py
+++ b/solution.py
@@ -85,20 +85,24 @@
 def kernel(
     scale,
     weight_ref,
-    trade_in,
+    own_in,
+    other_in,
     row_ref,
     loss_ref,
-    loading_out,
+    own_out,
+    other_out,
     factor_out,
     values_ref,
     slot_weight_ref,
     trade_ref,
-    loading_ref,
+    own_ref,
+    other_ref,
     trade_sem,
     loading_sem,
 ):
     shards, _, width = trade_ref.shape
-    trades = loading_ref.shape[2]
+    half = own_ref.shape[0]
+    trades = own_ref.shape[2]
     factors, paths = row_ref.shape
     slots = slot_weight_ref.shape[2]
     span_local = slots // 2
@@ -110,22 +114,27 @@
     def place(shard):
         return pl.ds(pl.multiple_of(shard * trades, trades), trades)
 
-    def copy_in(shard):
-        return pltpu.make_async_copy(trade_in.at[shard], trade_ref.at[shard], trade_sem.at[shard])
-
-    def copy_out(shard):
+    def copy_in(source, first, at):
         return pltpu.make_async_copy(
-            loading_ref.at[shard], loading_out.at[shard], loading_sem.at[shard]
-        )
-
-    def fetch(shard, carry):
-        copy_in(shard).start()
-        return carry
-
-    lax.fori_loop(0, shards, fetch, 0)
-
-    def forward(shard, span_total):
-        copy_in(shard).wait()
+            source.at[at], trade_ref.at[first + at], trade_sem.at[first + at]
+        )
+
+    def copy_out(held, target, first, at):
+        return pltpu.make_async_copy(held.at[at], target.at[at], loading_sem.at[first + at])
+
+    sources = ((own_in, 0), (other_in, half))
+    targets = ((other_ref, other_out, half), (own_ref, own_out, 0))
+    for source, first in sources:
+
+        def fetch(at, carry, source=source, first=first):
+            copy_in(source, first, at).start()
+            return carry
+
+        lax.fori_loop(0, half, fetch, 0)
+
+    def forward(source, first, at, span_total):
+        copy_in(source, first, at).wait()
+        shard = first + at
         data = trade_ref[shard].astype(f32)
         loading, slot, notional = rows_of(data, trades)
         names, loss, constant = lists_of(data)
@@ -145,10 +154,15 @@
             )
         return span_total
 
-    span_total = lax.fori_loop(0, shards, forward, jnp.zeros((paths, span_count), f32), unroll=4)
+    span_total = jnp.zeros((paths, span_count), f32)
+    for source, first in sources:
+        span_total = lax.fori_loop(
+            0, half, functools.partial(forward, source, first), span_total, unroll=2
+        )
     span_weight = (weight * loss_ref[...] * jax.nn.sigmoid(span_total / smoothing)).astype(bf16)
 
-    def backward(shard, total):
+    def backward(held, target, first, at, total):
+        shard = first + at
         data = trade_ref[shard].astype(f32)
         loading, slot, notional = rows_of(data, trades)
         names, _, _ = lists_of(data)
@@ -161,19 +175,23 @@
         scaled = values_ref[:, place(shard)].astype(f32) + notional
         sensitivity = (trade_weight * scaled).astype(bf16)
         paths_sum = jnp.dot(row, sensitivity, preferred_element_type=f32)
-        loading_ref[shard] = (paths_sum * scale).astype(bf16)
-        copy_out(shard).start()
+        held[at] = (paths_sum * scale).astype(held.dtype)
+        copy_out(held, target, first, at).start()
         return total + lax.dot_general(
             loading.astype(bf16), sensitivity, nt, preferred_element_type=f32
         )
 
-    factor_out[...] = lax.fori_loop(0, shards, backward, jnp.zeros((factors, paths), f32))
-
-    def drain(shard, carry):
-        copy_out(shard).wait()
-        return carry
-
-    lax.fori_loop(0, shards, drain, 0)
+    total = jnp.zeros((factors, paths), f32)
+    for way in targets:
+        total = lax.fori_loop(0, half, functools.partial(backward, *way), total)
+    factor_out[...] = total
+    for way in targets:
+
+        def drain(at, carry, way=way):
+            copy_out(*way, at).wait()
+            return carry
+
+        lax.fori_loop(0, half, drain, 0)
 
 
 vmem = pl.BlockSpec(memory_space=pltpu.VMEM)
@@ -206,22 +224,23 @@
     )
 
 
-def price_and_adjoint(weight, trade_data, factor_rows, loss_spanning, trades, slots, scale):
-    shards = trade_data.shape[0]
+def price_and_adjoint(weight, own, other, factor_rows, loss_spanning, trades, slots, scale):
+    half = own.shape[0]
+    shards = 2 * half
     factors, paths = factor_rows.shape
+    parts = (((half, factors, trades), f32), ((half, factors, trades), bf16))
     return pl.pallas_call(
         functools.partial(kernel, scale),
-        out_shape=(
-            jax.ShapeDtypeStruct((shards, factors, trades), bf16),
-            jax.ShapeDtypeStruct((factors, paths), f32),
-        ),
-        in_specs=[smem, pl.BlockSpec(memory_space=pltpu.HBM), vmem, vmem],
-        out_specs=(anywhere, vmem),
+        out_shape=tuple(jax.ShapeDtypeStruct(*part) for part in parts)
+        + (jax.ShapeDtypeStruct((factors, paths), f32),),
+        in_specs=[smem, anywhere, anywhere, vmem, vmem],
+        out_specs=(anywhere, anywhere, vmem),
         scratch_shapes=[
             pltpu.VMEM((paths, shards * trades), bf16),
             pltpu.VMEM((shards, paths, slots), bf16),
-            pltpu.VMEM(trade_data.shape, bf16),
-            pltpu.VMEM((shards, factors, trades), bf16),
+            pltpu.VMEM((shards,) + own.shape[1:], bf16),
+            pltpu.VMEM(*parts[0]),
+            pltpu.VMEM(*parts[1]),
             pltpu.SemaphoreType.DMA((shards,)),
             pltpu.SemaphoreType.DMA((shards,)),
         ],
@@ -231,7 +250,7 @@
             bytes_accessed=shards * trades * paths * 2,
             transcendentals=shards * trades * paths,
         ),
-    )(weight, trade_data, factor_rows, loss_spanning)
+    )(weight, own, other, factor_rows, loss_spanning)
 
 
 def on_device(
@@ -253,6 +272,9 @@
     trades = loadings.shape[2]
     group_dates = dates // path_devices
     quarters = trade_devices // group_dates
+    columns = trade_devices // 2
+    sides = [[2 * at + side for at in range(columns)] for side in range(2)]
+    partner = [(at, at ^ 1) for at in range(trade_devices)]
 
     first_date = (path_at * group_dates).astype(jnp.int32).reshape(1, 1)
     sent = pack(
@@ -263,10 +285,9 @@
         trade_slot,
         span_list,
         loss_local,
-        trade_devices,
+        columns,
         group_dates,
     )
-    trade_data = lax.all_to_all(sent, "trade", 0, 0, tiled=True)
 
     routes = []
     for turn in range(2):
@@ -284,6 +305,9 @@
     second = jnp.where(odd_path, mine[0], mine[1])
     first = lax.ppermute(first, ("path", "trade"), routes[0])
     second = lax.ppermute(second, ("path", "trade"), routes[1])
+    own = lax.all_to_all(sent, "trade", 0, 0, axis_index_groups=sides, tiled=True)
+    own, first, second = lax.optimization_barrier((own, first, second))
+    other = lax.ppermute(own, "trade", partner)
     factor_rows = jnp.where(
         odd_date,
         jnp.concatenate([second, first], axis=1),
@@ -292,23 +316,30 @@
 
     date_at = path_at * group_dates + trade_at // quarters
     weight = lax.dynamic_slice_in_dim(date_weight, date_at, 1).reshape(1, 1)
-    loading_part, factor_part = price_and_adjoint(
+    own_part, other_part, factor_part = price_and_adjoint(
         weight,
-        trade_data,
+        own,
+        other,
         factor_rows,
         loss_spanning[None, :],
         trades,
         span_list.shape[0] + loss_local.shape[0],
         1.0 / (path_devices * chunk),
     )
-    loading_part = lax.all_to_all(loading_part, "trade", 0, 0, tiled=True)
+    passed = lax.ppermute(other_part, "trade", partner)
+    loading_part = (own_part + passed.astype(f32)).astype(bf16)
+    loading_part, factor_part = lax.optimization_barrier((loading_part, factor_part))
+    loading_part = lax.all_to_all(
+        loading_part, "trade", 0, 0, axis_index_groups=sides, tiled=True
+    )
+
     back = [[(to, origin) for origin, to in route] for route in routes]
     left, right = factor_part[:, :chunk], factor_part[:, chunk:]
     first = lax.ppermute(jnp.where(odd_date, right, left), ("path", "trade"), back[0])
     second = lax.ppermute(jnp.where(odd_date, left, right), ("path", "trade"), back[1])
     factor_grad = jnp.where(odd_path, jnp.stack([second, first]), jnp.stack([first, second]))
 
-    loading_part = loading_part.reshape(group_dates, quarters, factor_count, trades)
+    loading_part = loading_part.reshape(group_dates, columns // group_dates, factor_count, trades)
     loading_grad = loading_part.astype(f32).sum(axis=1)
     return (loading_grad, factor_grad)
 

time: 115 us -> 109 us (0.948)
  waiting for transfers between devices: 19.4 us -> 7.25 us
  starting transfers between devices: 33.2 us -> 36.4 us
  other arithmetic: 2.86 us -> 4.88 us
    ppermute x1, waiting for transfers between devices: 8.24 us -> 0.01 us  [on_device(): lax.ppermute(jnp.where(odd_date, right, left), ('path', 'trade'), back[0])]
    ppermute x1, starting transfers between devices: 2.88 us -> 8.36 us  [on_device(): lax.ppermute(jnp.where(odd_date, right, left), ('path', 'trade'), back[0])]
    ppermute x1, starting transfers between devices: 4.31 us -> 0.08 us  [on_device(): lax.ppermute(jnp.where(odd_date, left, right), ('path', 'trade'), back[1])]
    ppermute x1, waiting for transfers between devices: 4.04 us -> 0.7 us  [on_device(): first = lax.ppermute(first, ('path', 'trade'), routes[0])]
    ppermute x0 -> x2, waiting for transfers between devices: none -> 2.69 us  [the longest x1 1.93 us: on_device(): passed = lax.ppermute(other_part, 'trade', partner)]
    all_to_all x2, waiting for transfers between devices: 2.52 us -> 0.01 us  [the longest x1 0.01 us: on_device(): lax.all_to_all(sent, 'trade', 0, 0, axis_index_groups=sides, tiled=True)]
    ppermute x1, waiting for transfers between devices: 2.19 us -> 0.01 us  [on_device(): second = lax.ppermute(second, ('path', 'trade'), routes[1])]
    convert_element_type x0 -> x1, other arithmetic: none -> 2.11 us  [on_device(): loading_part = (own_part + passed.astype(f32)).astype(bf16)]
  transfers between devices with their start and end apart: 6 -> 8, of which waited for: 5 -> 4; matrix products, arithmetic and copies ran while one was open for 2% -> 2% of each run, Pallas kernels for 0% -> 0%
where the time goes in v7:
time: 109 us; the launch traced here: 108 us
  Pallas kernels  57.2 us (52%)
  starting transfers between devices  36.4 us (33%)
  waiting for transfers between devices  7.25 us (7%)
  other arithmetic  4.88 us (4%)
  local copies, waits for them, and re-layouts  1.55 us (1%)
    pallas_call x1, Pallas kernels, price_and_adjoint(): pl.pallas_call(functools.partial(kernel, scale), out_shape=tuple((jax.Sha...  54.6 us
    ppermute x1, starting transfers between devices, on_device(): lax.ppermute(jnp.where(odd_date, right, left), ('path', 'trade'), back[0])  8.36 us
    all_to_all x1, starting transfers between devices, on_device(): lax.all_to_all(loading_part, 'trade', 0, 0, axis_index_groups=sides, tile...  7.71 us
    all_to_all x1, starting transfers between devices, on_device(): lax.all_to_all(sent, 'trade', 0, 0, axis_index_groups=sides, tiled=True)  7.49 us
    ppermute x1, starting transfers between devices, on_device(): second = lax.ppermute(second, ('path', 'trade'), routes[1])  6.49 us
    ppermute x1, starting transfers between devices, on_device(): first = lax.ppermute(first, ('path', 'trade'), routes[0])  5.77 us
    ppermute x1, waiting for transfers between devices, on_device(): lax.ppermute(jnp.where(odd_date, left, right), ('path', 'trade'), back[1])  3.85 us
    pallas_call x1, Pallas kernels, pack(): pl.pallas_call(functools.partial(pack_kernel, slots), out_shape=jax.Shape...  2.68 us
  transfers between devices with their start and end apart: 8, of which 4 were waited for; matrix products, arithmetic and copies ran while one was open for 2% of the time, Pallas kernels for 0%

profile of v7, /device:TPU:1, one launch (start us, length us, event | category | flops | bytes accessed | tf_op | source)
XLA Modules:
  0.0 108.0 jit_solution(10173271004188940430)
XLA Ops:
  0.6 0.0 copy-start.3
  0.6 2.7 %shard_map.104 = bf16[8,8,5760]{2,1,0:T(8,128)(2,1)} custom-call(s32[1,1]{1,0:T(1,128)} %bitcast.1.first_ref, bf16[32,8,4096]{2,1,0:T(8,128)(2,1)} %loading_ref.1, f32[1,4096]{1,0:T(1,128)} %bitcast.17, f32[1,4096]{1,0:T(1,128)} %bitcast.18, s32[1,4096]{1,0:T(1,128)} %bitcast.19, s32[1,128]{1,0:T(1,128)} %bitcast.22, f32[1,128]{1,0:T(1,128)} %bitcast.23), custom_call_target="tpu_custom_call" | custom-call | tf_op jit(solution)/shard_map/pallas_call | solution.py:206
  3.3 7.5 %all-to-all-start = ((bf16[8,8,5760]{2,1,0:T(8,128)(2,1)}), bf16[8,8,5760]{2,1,0:T(8,128)(2,1)S(1)}, u32[]{:S(2)}, u32[]{:S(2)}) async-start(bf16[8,8,5760]{2,1,0:T(8,128)(2,1)} %shard_map.104), calls=%async_computation | async-start | bytes 1474560 | tf_op jit(solution)/shard_map/all_to_all | solution.py:308
  10.8 0.7 select_bitcast_fusion
  11.5 6.5 %collective-permute-start.1 = (bf16[8,128]{1,0:T(8,128)(2,1)S(1)}, bf16[8,128]{1,0:T(8,128)(2,1)S(1)}, u32[]{:S(2)}, u32[]{:S(2)}) collective-permute-start(bf16[8,128]{1,0:T(8,128)(2,1)S(1)} %get-tuple-element.18), channel_id=1, source_target_pairs={{0,4},{1,12},{2,20},{3,28},{4,36},{5,44},{6,52},{7,60},{8,68},{9,7... | collective-permute-start | bytes 6152 | tf_op jit(solution)/shard_map/ppermute | solution.py:307
  18.0 5.8 %collective-permute-start = (bf16[8,128]{1,0:T(8,128)(2,1)S(1)}, bf16[8,128]{1,0:T(8,128)(2,1)S(1)}, u32[]{:S(2)}, u32[]{:S(2)}) collective-permute-start(bf16[8,128]{1,0:T(8,128)(2,1)S(1)} %get-tuple-element.19), channel_id=1, source_target_pairs={{0,0},{1,8},{2,16},{3,24},{4,32},{5,40},{6,48},{7,56},{8,64},{9,72... | collective-permute-start | bytes 6152 | tf_op jit(solution)/shard_map/ppermute | solution.py:306
  23.8 0.0 collective-permute-done.1
  23.8 0.7 collective-permute-done
  24.5 0.0 all-to-all-done.own_in
  24.5 0.0 copy-start
  24.5 0.2 collective-permute-start.2
  24.7 0.0 copy-done.3
  24.7 0.7 dynamic_slice.6
  25.4 0.6 maximum_select_fusion.1.row_ref
  26.0 0.8 collective-permute-done.2.other_in
  26.7 0.0 copy-start.2
  26.7 0.0 copy-done
  26.7 0.9 copy-done.2
  27.6 54.6 %shard_map.105 = (f32[8,8,4096]{2,1,0:T(8,128)}, bf16[8,8,4096]{2,1,0:T(8,128)(2,1)}, f32[8,256]{1,0:T(8,128)}) custom-call(f32[1,1]{1,0:T(1,128)} %bitcast.weight_ref, bf16[8,8,5760]{2,1,0:T(8,128)(2,1)} %copy-done, bf16[8,8,5760]{2,1,0:T(8,128)(2,1)} %copy-done.2, bf16[8,256]{1,0:T(8,128)(2,1)} %maximum_select_fusion.1.row_ref, f32[1,256]{1,0:T(1,128)} %bitcast.24), custom_call_target="tpu_custom_call" | custom-call | flops 34359738368 | bytes 33554432 | tf_op jit(solution)/shard_map/pallas_call | solution.py:232
  82.2 0.0 copy-start.1
  82.2 0.3 collective-permute-start.3
  82.5 1.9 %collective-permute-done.3 = bf16[8,8,4096]{2,1,0:T(8,128)(2,1)S(1)} collective-permute-done((bf16[8,8,4096]{2,1,0:T(8,128)(2,1)}, bf16[8,8,4096]{2,1,0:T(8,128)(2,1)S(1)}, u32[]{:S(2)}, u32[]{:S(2)}) %collective-permute-start.3) | collective-permute-done | bytes 524320 | tf_op jit(solution)/shard_map/ppermute | solution.py:329
  84.4 2.1 %add_convert_fusion = bf16[8,8,4096]{2,1,0:T(8,128)(2,1)} fusion(f32[8,8,4096]{2,1,0:T(8,128)} %get-tuple-element.13, bf16[8,8,4096]{2,1,0:T(8,128)(2,1)S(1)} %collective-permute-done.3), kind=kLoop, calls=%fused_computation.1 | loop fusion | flops 786432 | bytes 2097152 | tf_op jit(solution)/shard_map/convert_element_type | solution.py:330
  86.5 7.7 %all-to-all-start.1 = ((bf16[8,8,4096]{2,1,0:T(8,128)(2,1)}), bf16[8,8,4096]{2,1,0:T(8,128)(2,1)S(1)}, u32[]{:S(2)}, u32[]{:S(2)}) async-start(bf16[8,8,4096]{2,1,0:T(8,128)(2,1)} %add_convert_fusion), calls=%async_computation.1 | async-start | bytes 1048576 | tf_op jit(solution)/shard_map/all_to_all | solution.py:332
  94.2 0.0 copy-done.1
  94.2 0.1 collective-permute-start.4
  94.3 8.4 %collective-permute-start.5 = (f32[8,128]{1,0:T(8,128)S(1)}, f32[8,128]{1,0:T(8,128)S(1)}, u32[]{:S(2)}, u32[]{:S(2)}) collective-permute-start(f32[8,128]{1,0:T(8,128)S(1)} %get-tuple-element.21), channel_id=1, source_target_pairs={{0,0},{8,1},{16,2},{24,3},{32,4},{40,5},{48,6},{56,7},{64,8},{72,9... | collective-permute-start | bytes 12296 | tf_op jit(solution)/shard_map/ppermute | solution.py:338
  102.7 3.9 %collective-permute-done.4 = f32[8,128]{1,0:T(8,128)S(1)} collective-permute-done((f32[8,128]{1,0:T(8,128)S(1)}, f32[8,128]{1,0:T(8,128)S(1)}, u32[]{:S(2)}, u32[]{:S(2)}) %collective-permute-start.4) | collective-permute-done | bytes 4128 | tf_op jit(solution)/shard_map/ppermute | solution.py:339
  106.5 0.0 collective-permute-done.5
  106.5 0.6 maximum_select_fusion
  107.1 0.0 all-to-all-done.1
  107.1 0.9 convert_reduce_fusion
  (1 shorter events, 0.0 us)
Async XLA Ops:
  0.6 24.1 %copy-start.3 = (f32[32]{0:T(128)S(1)}, f32[32]{0:T(128)}, u32[]{:S(2)}) copy-start(f32[32]{0:T(128)} %param.13) | copy-start | bytes 388
  3.3 21.2 %all-to-all-start = ((bf16[8,8,5760]{2,1,0:T(8,128)(2,1)}), bf16[8,8,5760]{2,1,0:T(8,128)(2,1)S(1)}, u32[]{:S(2)}, u32[]{:S(2)}) async-start(bf16[8,8,5760]{2,1,0:T(8,128)(2,1)} %shard_map.104), calls=%async_computation | async-start | bytes 1474560 | tf_op jit(solution)/shard_map/all_to_all | solution.py:308
  11.5 12.3 %collective-permute-start.1 = (bf16[8,128]{1,0:T(8,128)(2,1)S(1)}, bf16[8,128]{1,0:T(8,128)(2,1)S(1)}, u32[]{:S(2)}, u32[]{:S(2)}) collective-permute-start(bf16[8,128]{1,0:T(8,128)(2,1)S(1)} %get-tuple-element.18), channel_id=1, source_target_pairs={{0,4},{1,12},{2,20},{3,28},{4,36},{5,44},{6,52},{7,60},{8,68},{9,7... | collective-permute-start | bytes 6152 | tf_op jit(solution)/shard_map/ppermute | solution.py:307
  18.0 6.5 %collective-permute-start = (bf16[8,128]{1,0:T(8,128)(2,1)S(1)}, bf16[8,128]{1,0:T(8,128)(2,1)S(1)}, u32[]{:S(2)}, u32[]{:S(2)}) collective-permute-start(bf16[8,128]{1,0:T(8,128)(2,1)S(1)} %get-tuple-element.19), channel_id=1, source_target_pairs={{0,0},{1,8},{2,16},{3,24},{4,32},{5,40},{6,48},{7,56},{8,64},{9,72... | collective-permute-start | bytes 6152 | tf_op jit(solution)/shard_map/ppermute | solution.py:306
  24.5 2.2 %copy-start = (bf16[8,8,5760]{2,1,0:T(8,128)(2,1)}, bf16[8,8,5760]{2,1,0:T(8,128)(2,1)S(1)}, u32[]{:S(2)}) copy-start(bf16[8,8,5760]{2,1,0:T(8,128)(2,1)S(1)} %all-to-all-done.own_in) | copy-start | bytes 2211844
  24.5 2.2 %collective-permute-start.2 = (bf16[8,8,5760]{2,1,0:T(8,128)(2,1)S(1)}, bf16[8,8,5760]{2,1,0:T(8,128)(2,1)S(1)}, u32[]{:S(2)}, u32[]{:S(2)}) collective-permute-start(bf16[8,8,5760]{2,1,0:T(8,128)(2,1)S(1)} %all-to-all-done.own_in), channel_id=1, source_target_pairs={{0,1},{1,0},{2,3},{3,2},{4,5},{5,4},{6,7},{7,6},{8,9},{9,8},{10,11... | collective-permute-start | bytes 2211848 | tf_op jit(solution)/shard_map/ppermute | solution.py:310
  26.7 0.9 copy-start.2
  82.2 12.0 %copy-start.1 = (f32[8,256]{1,0:T(8,128)S(1)}, f32[8,256]{1,0:T(8,128)}, u32[]{:S(2)}) copy-start(f32[8,256]{1,0:T(8,128)} %get-tuple-element.17) | copy-start | bytes 24580
  82.2 2.2 %collective-permute-start.3 = (bf16[8,8,4096]{2,1,0:T(8,128)(2,1)}, bf16[8,8,4096]{2,1,0:T(8,128)(2,1)S(1)}, u32[]{:S(2)}, u32[]{:S(2)}) collective-permute-start(bf16[8,8,4096]{2,1,0:T(8,128)(2,1)} %get-tuple-element.14), channel_id=1, source_target_pairs={{0,1},{1,0},{2,3},{3,2},{4,5},{5,4},{6,7},{7,6},{8,9},{9,8},{10,11... | collective-permute-start | bytes 1572872 | tf_op jit(solution)/shard_map/ppermute | solution.py:329
  86.5 20.6 %all-to-all-start.1 = ((bf16[8,8,4096]{2,1,0:T(8,128)(2,1)}), bf16[8,8,4096]{2,1,0:T(8,128)(2,1)S(1)}, u32[]{:S(2)}, u32[]{:S(2)}) async-start(bf16[8,8,4096]{2,1,0:T(8,128)(2,1)} %add_convert_fusion), calls=%async_computation.1 | async-start | bytes 1048576 | tf_op jit(solution)/shard_map/all_to_all | solution.py:332
  94.2 12.3 %collective-permute-start.4 = (f32[8,128]{1,0:T(8,128)S(1)}, f32[8,128]{1,0:T(8,128)S(1)}, u32[]{:S(2)}, u32[]{:S(2)}) collective-permute-start(f32[8,128]{1,0:T(8,128)S(1)} %get-tuple-element.20), channel_id=1, source_target_pairs={{4,0},{12,1},{20,2},{28,3},{36,4},{44,5},{52,6},{60,7},{68,8},{76,... | collective-permute-start | bytes 12296 | tf_op jit(solution)/shard_map/ppermute | solution.py:339
  94.3 12.2 %collective-permute-start.5 = (f32[8,128]{1,0:T(8,128)S(1)}, f32[8,128]{1,0:T(8,128)S(1)}, u32[]{:S(2)}, u32[]{:S(2)}) collective-permute-start(f32[8,128]{1,0:T(8,128)S(1)} %get-tuple-element.21), channel_id=1, source_target_pairs={{0,0},{8,1},{16,2},{24,3},{32,4},{40,5},{48,6},{56,7},{64,8},{72,9... | collective-permute-start | bytes 12296 | tf_op jit(solution)/shard_map/ppermute | solution.py:338

commit v8 on v7

--- a/solution.py
+++ b/solution.py
@@ -157,7 +157,7 @@
     span_total = jnp.zeros((paths, span_count), f32)
     for source, first in sources:
         span_total = lax.fori_loop(
-            0, half, functools.partial(forward, source, first), span_total, unroll=2
+            0, half, functools.partial(forward, source, first), span_total, unroll=4
         )
     span_weight = (weight * loss_ref[...] * jax.nn.sigmoid(span_total / smoothing)).astype(bf16)
 
@@ -328,15 +328,15 @@
     )
     passed = lax.ppermute(other_part, "trade", partner)
     loading_part = (own_part + passed.astype(f32)).astype(bf16)
-    loading_part, factor_part = lax.optimization_barrier((loading_part, factor_part))
-    loading_part = lax.all_to_all(
-        loading_part, "trade", 0, 0, axis_index_groups=sides, tiled=True
-    )
-
     back = [[(to, origin) for origin, to in route] for route in routes]
     left, right = factor_part[:, :chunk], factor_part[:, chunk:]
     first = lax.ppermute(jnp.where(odd_date, right, left), ("path", "trade"), back[0])
-    second = lax.ppermute(jnp.where(odd_date, left, right), ("path", "trade"), back[1])
+    loading_part, second = lax.optimization_barrier((loading_part, jnp.where(odd_date, left, right)))
+    loading_part = lax.all_to_all(
+        loading_part, "trade", 0, 0, axis_index_groups=sides, tiled=True
+    )
+
+    second = lax.ppermute(second, ("path", "trade"), back[1])
     factor_grad = jnp.where(odd_path, jnp.stack([second, first]), jnp.stack([first, second]))
 
     loading_part = loading_part.reshape(group_dates, columns // group_dates, factor_count, trades)

time: 109 us -> 108 us (level)
    ppermute x1, starting transfers between devices: 8.36 us -> 1.91 us  [on_device(): lax.ppermute(jnp.where(odd_date, right, left), ('path', 'trade'), back[0])]
    ppermute x1, starting transfers between devices: 0.08 us -> 5.69 us  [on_device(): second = lax.ppermute(second, ('path', 'trade'), back[1])]
    ppermute x1, waiting for transfers between devices: 0.01 us -> 2.54 us  [on_device(): lax.ppermute(jnp.where(odd_date, right, left), ('path', 'trade'), back[0])]
    ppermute x1, waiting for transfers between devices: 3.85 us -> 2.17 us  [on_device(): second = lax.ppermute(second, ('path', 'trade'), back[1])]
  transfers between devices with their start and end apart: 8 -> 8, of which waited for: 4 -> 5; matrix products, arithmetic and copies ran while one was open for 2% -> 3% of each run, Pallas kernels for 0% -> 0%
where the time goes in v8:
time: 108 us; the launch traced here: 107 us
  Pallas kernels  56.5 us (52%)
  starting transfers between devices  35.5 us (33%)
  waiting for transfers between devices  7.5 us (7%)
  other arithmetic  5.57 us (5%)
  local copies, waits for them, and re-layouts  1.46 us (1%)
    pallas_call x1, Pallas kernels, price_and_adjoint(): pl.pallas_call(functools.partial(kernel, scale), out_shape=tuple((jax.Sha...  53.8 us
    all_to_all x1, starting transfers between devices, on_device(): lax.all_to_all(loading_part, 'trade', 0, 0, axis_index_groups=sides, tile...  7.71 us
    all_to_all x1, starting transfers between devices, on_device(): lax.all_to_all(sent, 'trade', 0, 0, axis_index_groups=sides, tiled=True)  7.49 us
    ppermute x1, starting transfers between devices, on_device(): second = lax.ppermute(second, ('path', 'trade'), routes[1])  6.49 us
    ppermute x1, starting transfers between devices, on_device(): first = lax.ppermute(first, ('path', 'trade'), routes[0])  5.77 us
    ppermute x1, starting transfers between devices, on_device(): second = lax.ppermute(second, ('path', 'trade'), back[1])  5.69 us
    pallas_call x1, Pallas kernels, pack(): pl.pallas_call(functools.partial(pack_kernel, slots), out_shape=jax.Shape...  2.66 us
    ppermute x1, waiting for transfers between devices, on_device(): lax.ppermute(jnp.where(odd_date, right, left), ('path', 'trade'), back[0])  2.54 us
  transfers between devices with their start and end apart: 8, of which 5 were waited for; matrix products, arithmetic and copies ran while one was open for 3% of the time, Pallas kernels for 0%

profile of v8, /device:TPU:1, one launch (start us, length us, event | category | flops | bytes accessed | tf_op | source)
XLA Modules:
  0.0 107.3 jit_solution(16291036727481499060)
XLA Ops:
  0.6 0.0 copy-start.2
  0.6 2.7 %shard_map.104 = bf16[8,8,5760]{2,1,0:T(8,128)(2,1)} custom-call(s32[1,1]{1,0:T(1,128)} %bitcast.1.first_ref, bf16[32,8,4096]{2,1,0:T(8,128)(2,1)} %loading_ref.1, f32[1,4096]{1,0:T(1,128)} %bitcast.17, f32[1,4096]{1,0:T(1,128)} %bitcast.18, s32[1,4096]{1,0:T(1,128)} %bitcast.19, s32[1,128]{1,0:T(1,128)} %bitcast.22, f32[1,128]{1,0:T(1,128)} %bitcast.23), custom_call_target="tpu_custom_call" | custom-call | tf_op jit(solution)/shard_map/pallas_call | solution.py:206
  3.3 7.5 %all-to-all-start = ((bf16[8,8,5760]{2,1,0:T(8,128)(2,1)}), bf16[8,8,5760]{2,1,0:T(8,128)(2,1)S(1)}, u32[]{:S(2)}, u32[]{:S(2)}) async-start(bf16[8,8,5760]{2,1,0:T(8,128)(2,1)} %shard_map.104), calls=%async_computation | async-start | bytes 1474560 | tf_op jit(solution)/shard_map/all_to_all | solution.py:308
  10.8 0.7 select_bitcast_fusion
  11.5 6.5 %collective-permute-start.1 = (bf16[8,128]{1,0:T(8,128)(2,1)S(1)}, bf16[8,128]{1,0:T(8,128)(2,1)S(1)}, u32[]{:S(2)}, u32[]{:S(2)}) collective-permute-start(bf16[8,128]{1,0:T(8,128)(2,1)S(1)} %get-tuple-element.18), channel_id=1, source_target_pairs={{0,4},{1,12},{2,20},{3,28},{4,36},{5,44},{6,52},{7,60},{8,68},{9,7... | collective-permute-start | bytes 6152 | tf_op jit(solution)/shard_map/ppermute | solution.py:307
  18.0 5.8 %collective-permute-start = (bf16[8,128]{1,0:T(8,128)(2,1)S(1)}, bf16[8,128]{1,0:T(8,128)(2,1)S(1)}, u32[]{:S(2)}, u32[]{:S(2)}) collective-permute-start(bf16[8,128]{1,0:T(8,128)(2,1)S(1)} %get-tuple-element.19), channel_id=1, source_target_pairs={{0,0},{1,8},{2,16},{3,24},{4,32},{5,40},{6,48},{7,56},{8,64},{9,72... | collective-permute-start | bytes 6152 | tf_op jit(solution)/shard_map/ppermute | solution.py:306
  23.8 0.0 collective-permute-done.1
  23.8 0.7 collective-permute-done
  24.5 0.0 all-to-all-done.own_in
  24.5 0.0 copy-start
  24.5 0.2 collective-permute-start.2
  24.7 0.0 copy-done.2
  24.7 0.6 dynamic_slice.6
  25.3 0.6 maximum_select_fusion.1.row_ref
  25.9 0.8 collective-permute-done.2.other_in
  26.7 0.0 copy-start.1
  26.7 0.0 copy-done
  26.7 0.9 copy-done.1
  27.6 53.8 %shard_map.105 = (f32[8,8,4096]{2,1,0:T(8,128)}, bf16[8,8,4096]{2,1,0:T(8,128)(2,1)}, f32[8,256]{1,0:T(8,128)}) custom-call(f32[1,1]{1,0:T(1,128)} %bitcast.weight_ref, bf16[8,8,5760]{2,1,0:T(8,128)(2,1)} %copy-done, bf16[8,8,5760]{2,1,0:T(8,128)(2,1)} %copy-done.1, bf16[8,256]{1,0:T(8,128)(2,1)} %maximum_select_fusion.1.row_ref, f32[1,256]{1,0:T(1,128)} %bitcast.24), custom_call_target="tpu_custom_call" | custom-call | flops 34359738368 | bytes 33554432 | tf_op jit(solution)/shard_map/pallas_call | solution.py:232
  81.4 0.3 collective-permute-start.3
  81.7 0.7 slice_select_fusion
  82.4 1.2 %collective-permute-done.3 = bf16[8,8,4096]{2,1,0:T(8,128)(2,1)S(1)} collective-permute-done((bf16[8,8,4096]{2,1,0:T(8,128)(2,1)}, bf16[8,8,4096]{2,1,0:T(8,128)(2,1)S(1)}, u32[]{:S(2)}, u32[]{:S(2)}) %collective-permute-start.3) | collective-permute-done | bytes 524320 | tf_op jit(solution)/shard_map/ppermute | solution.py:329
  83.6 2.1 %add_convert_fusion = bf16[8,8,4096]{2,1,0:T(8,128)(2,1)} fusion(f32[8,8,4096]{2,1,0:T(8,128)} %get-tuple-element.13, bf16[8,8,4096]{2,1,0:T(8,128)(2,1)S(1)} %collective-permute-done.3), kind=kLoop, calls=%fused_computation.1 | loop fusion | flops 786432 | bytes 2097152 | tf_op jit(solution)/shard_map/convert_element_type | solution.py:330
  85.7 7.7 %all-to-all-start.1 = ((bf16[8,8,4096]{2,1,0:T(8,128)(2,1)}), bf16[8,8,4096]{2,1,0:T(8,128)(2,1)S(1)}, u32[]{:S(2)}, u32[]{:S(2)}) async-start(bf16[8,8,4096]{2,1,0:T(8,128)(2,1)} %add_convert_fusion), calls=%async_computation.1 | async-start | bytes 1048576 | tf_op jit(solution)/shard_map/all_to_all | solution.py:335
  93.5 1.9 %collective-permute-start.5 = (f32[8,128]{1,0:T(8,128)S(1)}, f32[8,128]{1,0:T(8,128)S(1)}, u32[]{:S(2)}, u32[]{:S(2)}) collective-permute-start(f32[8,128]{1,0:T(8,128)S(1)} %get-tuple-element.20), channel_id=1, source_target_pairs={{0,0},{8,1},{16,2},{24,3},{32,4},{40,5},{48,6},{56,7},{64,8},{72,9... | collective-permute-start | bytes 12296 | tf_op jit(solution)/shard_map/ppermute | solution.py:333
  95.4 5.7 %collective-permute-start.4 = (f32[8,128]{1,0:T(8,128)S(1)}, f32[8,128]{1,0:T(8,128)S(1)}, u32[]{:S(2)}, u32[]{:S(2)}) collective-permute-start(f32[8,128]{1,0:T(8,128)S(1)} %get-tuple-element.17), channel_id=1, source_target_pairs={{4,0},{12,1},{20,2},{28,3},{36,4},{44,5},{52,6},{60,7},{68,8},{76,... | collective-permute-start | bytes 12296 | tf_op jit(solution)/shard_map/ppermute | solution.py:339
  101.1 2.5 %collective-permute-done.5 = f32[8,128]{1,0:T(8,128)S(1)} collective-permute-done((f32[8,128]{1,0:T(8,128)S(1)}, f32[8,128]{1,0:T(8,128)S(1)}, u32[]{:S(2)}, u32[]{:S(2)}) %collective-permute-start.5) | collective-permute-done | bytes 4128 | tf_op jit(solution)/shard_map/ppermute | solution.py:333
  103.6 2.2 %collective-permute-done.4 = f32[8,128]{1,0:T(8,128)S(1)} collective-permute-done((f32[8,128]{1,0:T(8,128)S(1)}, f32[8,128]{1,0:T(8,128)S(1)}, u32[]{:S(2)}, u32[]{:S(2)}) %collective-permute-start.4) | collective-permute-done | bytes 4128 | tf_op jit(solution)/shard_map/ppermute | solution.py:339
  105.8 0.6 maximum_select_fusion
  106.4 0.0 all-to-all-done.1
  106.4 0.9 convert_reduce_fusion
Async XLA Ops:
  0.6 24.1 %copy-start.2 = (f32[32]{0:T(128)S(1)}, f32[32]{0:T(128)}, u32[]{:S(2)}) copy-start(f32[32]{0:T(128)} %param.13) | copy-start | bytes 388
  3.3 21.2 %all-to-all-start = ((bf16[8,8,5760]{2,1,0:T(8,128)(2,1)}), bf16[8,8,5760]{2,1,0:T(8,128)(2,1)S(1)}, u32[]{:S(2)}, u32[]{:S(2)}) async-start(bf16[8,8,5760]{2,1,0:T(8,128)(2,1)} %shard_map.104), calls=%async_computation | async-start | bytes 1474560 | tf_op jit(solution)/shard_map/all_to_all | solution.py:308
  11.5 12.3 %collective-permute-start.1 = (bf16[8,128]{1,0:T(8,128)(2,1)S(1)}, bf16[8,128]{1,0:T(8,128)(2,1)S(1)}, u32[]{:S(2)}, u32[]{:S(2)}) collective-permute-start(bf16[8,128]{1,0:T(8,128)(2,1)S(1)} %get-tuple-element.18), channel_id=1, source_target_pairs={{0,4},{1,12},{2,20},{3,28},{4,36},{5,44},{6,52},{7,60},{8,68},{9,7... | collective-permute-start | bytes 6152 | tf_op jit(solution)/shard_map/ppermute | solution.py:307
  18.0 6.5 %collective-permute-start = (bf16[8,128]{1,0:T(8,128)(2,1)S(1)}, bf16[8,128]{1,0:T(8,128)(2,1)S(1)}, u32[]{:S(2)}, u32[]{:S(2)}) collective-permute-start(bf16[8,128]{1,0:T(8,128)(2,1)S(1)} %get-tuple-element.19), channel_id=1, source_target_pairs={{0,0},{1,8},{2,16},{3,24},{4,32},{5,40},{6,48},{7,56},{8,64},{9,72... | collective-permute-start | bytes 6152 | tf_op jit(solution)/shard_map/ppermute | solution.py:306
  24.5 2.2 %copy-start = (bf16[8,8,5760]{2,1,0:T(8,128)(2,1)}, bf16[8,8,5760]{2,1,0:T(8,128)(2,1)S(1)}, u32[]{:S(2)}) copy-start(bf16[8,8,5760]{2,1,0:T(8,128)(2,1)S(1)} %all-to-all-done.own_in) | copy-start | bytes 2211844
  24.5 2.2 %collective-permute-start.2 = (bf16[8,8,5760]{2,1,0:T(8,128)(2,1)S(1)}, bf16[8,8,5760]{2,1,0:T(8,128)(2,1)S(1)}, u32[]{:S(2)}, u32[]{:S(2)}) collective-permute-start(bf16[8,8,5760]{2,1,0:T(8,128)(2,1)S(1)} %all-to-all-done.own_in), channel_id=1, source_target_pairs={{0,1},{1,0},{2,3},{3,2},{4,5},{5,4},{6,7},{7,6},{8,9},{9,8},{10,11... | collective-permute-start | bytes 2211848 | tf_op jit(solution)/shard_map/ppermute | solution.py:310
  26.7 0.9 copy-start.1
  81.4 2.2 %collective-permute-start.3 = (bf16[8,8,4096]{2,1,0:T(8,128)(2,1)}, bf16[8,8,4096]{2,1,0:T(8,128)(2,1)S(1)}, u32[]{:S(2)}, u32[]{:S(2)}) collective-permute-start(bf16[8,8,4096]{2,1,0:T(8,128)(2,1)} %get-tuple-element.14), channel_id=1, source_target_pairs={{0,1},{1,0},{2,3},{3,2},{4,5},{5,4},{6,7},{7,6},{8,9},{9,8},{10,11... | collective-permute-start | bytes 1572872 | tf_op jit(solution)/shard_map/ppermute | solution.py:329
  85.7 20.6 %all-to-all-start.1 = ((bf16[8,8,4096]{2,1,0:T(8,128)(2,1)}), bf16[8,8,4096]{2,1,0:T(8,128)(2,1)S(1)}, u32[]{:S(2)}, u32[]{:S(2)}) async-start(bf16[8,8,4096]{2,1,0:T(8,128)(2,1)} %add_convert_fusion), calls=%async_computation.1 | async-start | bytes 1048576 | tf_op jit(solution)/shard_map/all_to_all | solution.py:335
  93.5 10.2 %collective-permute-start.5 = (f32[8,128]{1,0:T(8,128)S(1)}, f32[8,128]{1,0:T(8,128)S(1)}, u32[]{:S(2)}, u32[]{:S(2)}) collective-permute-start(f32[8,128]{1,0:T(8,128)S(1)} %get-tuple-element.20), channel_id=1, source_target_pairs={{0,0},{8,1},{16,2},{24,3},{32,4},{40,5},{48,6},{56,7},{64,8},{72,9... | collective-permute-start | bytes 12296 | tf_op jit(solution)/shard_map/ppermute | solution.py:333
  95.4 10.4 %collective-permute-start.4 = (f32[8,128]{1,0:T(8,128)S(1)}, f32[8,128]{1,0:T(8,128)S(1)}, u32[]{:S(2)}, u32[]{:S(2)}) collective-permute-start(f32[8,128]{1,0:T(8,128)S(1)} %get-tuple-element.17), channel_id=1, source_target_pairs={{4,0},{12,1},{20,2},{28,3},{36,4},{44,5},{52,6},{60,7},{68,8},{76,... | collective-permute-start | bytes 12296 | tf_op jit(solution)/shard_map/ppermute | solution.py:339

commit v9 on v8

--- a/solution.py
+++ b/solution.py
@@ -197,7 +197,8 @@
 vmem = pl.BlockSpec(memory_space=pltpu.VMEM)
 anywhere = pl.BlockSpec(memory_space=pl.ANY)
 smem = pl.BlockSpec(memory_space=pltpu.SMEM)
-params = pltpu.CompilerParams(vmem_limit_bytes=58 * 2**20)
+wide = pltpu.CompilerParams(vmem_limit_bytes=58 * 2**20)
+narrow = pltpu.CompilerParams(vmem_limit_bytes=46 * 2**20)
 
 
 def pack(first, loadings, notional, strike, trade_slot, span_list, loss_local, devices, group_dates):
@@ -212,7 +213,7 @@
             pltpu.VMEM((group_dates, factors, trades), bf16),
             pltpu.SemaphoreType.DMA,
         ],
-        compiler_params=params,
+        compiler_params=wide,
     )(
         first,
         loadings,
@@ -244,7 +245,7 @@
             pltpu.SemaphoreType.DMA((shards,)),
             pltpu.SemaphoreType.DMA((shards,)),
         ],
-        compiler_params=params,
+        compiler_params=narrow,
         cost_estimate=pl.CostEstimate(
             flops=shards * trades * paths * 2 * 256 * 4,
             bytes_accessed=shards * trades * paths * 2,

time: 108 us -> 110 us (1.019)
  Pallas kernels: 56.5 us -> 60.6 us
  other arithmetic: 5.57 us -> 3.1 us
    pallas_call x1, Pallas kernels: 53.8 us -> 57.9 us  [price_and_adjoint(): pl.pallas_call(functools.partial(kernel, scale), out_shape=tuple((jax.Sha...]
    convert_element_type x1, other arithmetic: 2.11 us -> 0.92 us  [on_device(): loading_part = (own_part + passed.astype(f32)).astype(bf16)]
  transfers between devices with their start and end apart: 8 -> 8, of which waited for: 5 -> 5; matrix products, arithmetic and copies ran while one was open for 3% -> 2% of each run, Pallas kernels for 0% -> 0%
where the time goes in v9:
time: 110 us; the launch traced here: 109 us
  Pallas kernels  60.6 us (55%)
  starting transfers between devices  35.5 us (32%)
  waiting for transfers between devices  8.57 us (8%)
  other arithmetic  3.1 us (3%)
    pallas_call x1, Pallas kernels, price_and_adjoint(): pl.pallas_call(functools.partial(kernel, scale), out_shape=tuple((jax.Sha...  57.9 us
    all_to_all x1, starting transfers between devices, on_device(): lax.all_to_all(loading_part, 'trade', 0, 0, axis_index_groups=sides, tile...  7.71 us
    all_to_all x1, starting transfers between devices, on_device(): lax.all_to_all(sent, 'trade', 0, 0, axis_index_groups=sides, tiled=True)  7.49 us
    ppermute x1, starting transfers between devices, on_device(): second = lax.ppermute(second, ('path', 'trade'), routes[1])  6.49 us
    ppermute x1, starting transfers between devices, on_device(): first = lax.ppermute(first, ('path', 'trade'), routes[0])  5.77 us
    ppermute x1, starting transfers between devices, on_device(): second = lax.ppermute(second, ('path', 'trade'), back[1])  5.7 us
    pallas_call x1, Pallas kernels, pack(): pl.pallas_call(functools.partial(pack_kernel, slots), out_shape=jax.Shape...  2.67 us
    ppermute x1, waiting for transfers between devices, on_device(): lax.ppermute(jnp.where(odd_date, right, left), ('path', 'trade'), back[0])  2.54 us
  transfers between devices with their start and end apart: 8, of which 5 were waited for; matrix products, arithmetic and copies ran while one was open for 2% of the time, Pallas kernels for 0%

profile of v9, /device:TPU:1, one launch (start us, length us, event | category | flops | bytes accessed | tf_op | source)
XLA Modules:
  0.0 109.1 jit_solution(8655344479634644573)
XLA Ops:
  0.6 0.0 copy-start.1
  0.6 0.0 copy-start
  0.7 2.7 %shard_map.104 = bf16[8,8,5760]{2,1,0:T(8,128)(2,1)} custom-call(s32[1,1]{1,0:T(1,128)} %bitcast.1.first_ref, bf16[32,8,4096]{2,1,0:T(8,128)(2,1)} %loading_ref.1, f32[1,4096]{1,0:T(1,128)} %bitcast.18, f32[1,4096]{1,0:T(1,128)} %bitcast.19, s32[1,4096]{1,0:T(1,128)} %bitcast.20, s32[1,128]{1,0:T(1,128)} %bitcast.23, f32[1,128]{1,0:T(1,128)} %bitcast.24), custom_call_target="tpu_custom_call" | custom-call | tf_op jit(solution)/shard_map/pallas_call | solution.py:207
  3.3 7.5 %all-to-all-start = ((bf16[8,8,5760]{2,1,0:T(8,128)(2,1)}), bf16[8,8,5760]{2,1,0:T(8,128)(2,1)S(1)}, u32[]{:S(2)}, u32[]{:S(2)}) async-start(bf16[8,8,5760]{2,1,0:T(8,128)(2,1)} %shard_map.104), calls=%async_computation | async-start | bytes 1474560 | tf_op jit(solution)/shard_map/all_to_all | solution.py:309
  10.8 0.7 select_bitcast_fusion
  11.5 6.5 %collective-permute-start.1 = (bf16[8,128]{1,0:T(8,128)(2,1)S(1)}, bf16[8,128]{1,0:T(8,128)(2,1)S(1)}, u32[]{:S(2)}, u32[]{:S(2)}) collective-permute-start(bf16[8,128]{1,0:T(8,128)(2,1)S(1)} %get-tuple-element.18), channel_id=1, source_target_pairs={{0,4},{1,12},{2,20},{3,28},{4,36},{5,44},{6,52},{7,60},{8,68},{9,7... | collective-permute-start | bytes 6152 | tf_op jit(solution)/shard_map/ppermute | solution.py:308
  18.0 5.8 %collective-permute-start = (bf16[8,128]{1,0:T(8,128)(2,1)S(1)}, bf16[8,128]{1,0:T(8,128)(2,1)S(1)}, u32[]{:S(2)}, u32[]{:S(2)}) collective-permute-start(bf16[8,128]{1,0:T(8,128)(2,1)S(1)} %get-tuple-element.19), channel_id=1, source_target_pairs={{0,0},{1,8},{2,16},{3,24},{4,32},{5,40},{6,48},{7,56},{8,64},{9,72... | collective-permute-start | bytes 6152 | tf_op jit(solution)/shard_map/ppermute | solution.py:307
  23.8 0.0 collective-permute-done.1
  23.8 0.7 collective-permute-done
  24.5 0.0 all-to-all-done.own_in
  24.5 0.2 collective-permute-start.2
  24.7 0.0 copy-done.1
  24.7 0.6 dynamic_slice.6
  25.3 1.4 %collective-permute-done.2.other_in = bf16[8,8,5760]{2,1,0:T(8,128)(2,1)S(1)} collective-permute-done((bf16[8,8,5760]{2,1,0:T(8,128)(2,1)S(1)}, bf16[8,8,5760]{2,1,0:T(8,128)(2,1)S(1)}, u32[]{:S(2)}, u32[]{:S(2)}) %collective-permute-start.2) | collective-permute-done | bytes 737312 | tf_op jit(solution)/shard_map/ppermute | solution.py:311
  26.7 0.0 copy-done
  26.7 57.9 %shard_map.105 = (f32[8,8,4096]{2,1,0:T(8,128)S(1)}, bf16[8,8,4096]{2,1,0:T(8,128)(2,1)S(1)}, f32[8,256]{1,0:T(8,128)S(1)}) custom-call(f32[1,1]{1,0:T(1,128)} %bitcast.weight_ref, bf16[8,8,5760]{2,1,0:T(8,128)(2,1)S(1)} %all-to-all-done.own_in, bf16[8,8,5760]{2,1,0:T(8,128)(2,1)S(1)} %collective-permute-done.2.other_in, ...), custom_call_target="tpu_custom_call" | custom-call | flops 34359738368 | bytes 33554432 | tf_op jit(solution)/shard_map/pallas_call | solution.py:233
  84.7 0.3 collective-permute-start.3
  84.9 1.7 %collective-permute-done.3 = bf16[8,8,4096]{2,1,0:T(8,128)(2,1)S(1)} collective-permute-done((bf16[8,8,4096]{2,1,0:T(8,128)(2,1)S(1)}, bf16[8,8,4096]{2,1,0:T(8,128)(2,1)S(1)}, u32[]{:S(2)}, u32[]{:S(2)}) %collective-permute-start.3) | collective-permute-done | bytes 524320 | tf_op jit(solution)/shard_map/ppermute | solution.py:330
  86.7 0.9 add_convert_fusion
  87.6 7.7 %all-to-all-start.1 = ((bf16[8,8,4096]{2,1,0:T(8,128)(2,1)}), bf16[8,8,4096]{2,1,0:T(8,128)(2,1)S(1)}, u32[]{:S(2)}, u32[]{:S(2)}) async-start(bf16[8,8,4096]{2,1,0:T(8,128)(2,1)} %add_convert_fusion), calls=%async_computation.1 | async-start | bytes 1048576 | tf_op jit(solution)/shard_map/all_to_all | solution.py:336
  95.3 1.9 %collective-permute-start.5 = (f32[8,128]{1,0:T(8,128)S(1)}, f32[8,128]{1,0:T(8,128)S(1)}, u32[]{:S(2)}, u32[]{:S(2)}) collective-permute-start(f32[8,128]{1,0:T(8,128)S(1)} %get-tuple-element.20), channel_id=1, source_target_pairs={{0,0},{8,1},{16,2},{24,3},{32,4},{40,5},{48,6},{56,7},{64,8},{72,9... | collective-permute-start | bytes 12296 | tf_op jit(solution)/shard_map/ppermute | solution.py:334
  97.2 5.7 %collective-permute-start.4 = (f32[8,128]{1,0:T(8,128)S(1)}, f32[8,128]{1,0:T(8,128)S(1)}, u32[]{:S(2)}, u32[]{:S(2)}) collective-permute-start(f32[8,128]{1,0:T(8,128)S(1)} %get-tuple-element.17), channel_id=1, source_target_pairs={{4,0},{12,1},{20,2},{28,3},{36,4},{44,5},{52,6},{60,7},{68,8},{76,... | collective-permute-start | bytes 12296 | tf_op jit(solution)/shard_map/ppermute | solution.py:340
  102.9 2.5 %collective-permute-done.5 = f32[8,128]{1,0:T(8,128)S(1)} collective-permute-done((f32[8,128]{1,0:T(8,128)S(1)}, f32[8,128]{1,0:T(8,128)S(1)}, u32[]{:S(2)}, u32[]{:S(2)}) %collective-permute-start.5) | collective-permute-done | bytes 4128 | tf_op jit(solution)/shard_map/ppermute | solution.py:334
  105.4 2.2 %collective-permute-done.4 = f32[8,128]{1,0:T(8,128)S(1)} collective-permute-done((f32[8,128]{1,0:T(8,128)S(1)}, f32[8,128]{1,0:T(8,128)S(1)}, u32[]{:S(2)}, u32[]{:S(2)}) %collective-permute-start.4) | collective-permute-done | bytes 4128 | tf_op jit(solution)/shard_map/ppermute | solution.py:340
  107.6 0.6 maximum_select_fusion
  108.2 0.0 all-to-all-done.1
  108.2 0.9 convert_reduce_fusion
  (2 shorter events, 0.0 us)
Async XLA Ops:
  0.6 24.1 %copy-start.1 = (f32[32]{0:T(128)S(1)}, f32[32]{0:T(128)}, u32[]{:S(2)}) copy-start(f32[32]{0:T(128)} %param.13) | copy-start | bytes 388
  0.6 26.1 %copy-start = (f32[256]{0:T(256)S(1)}, f32[256]{0:T(256)}, u32[]{:S(2)}) copy-start(f32[256]{0:T(256)} %param.14) | copy-start | bytes 3076
  3.3 21.2 %all-to-all-start = ((bf16[8,8,5760]{2,1,0:T(8,128)(2,1)}), bf16[8,8,5760]{2,1,0:T(8,128)(2,1)S(1)}, u32[]{:S(2)}, u32[]{:S(2)}) async-start(bf16[8,8,5760]{2,1,0:T(8,128)(2,1)} %shard_map.104), calls=%async_computation | async-start | bytes 1474560 | tf_op jit(solution)/shard_map/all_to_all | solution.py:309
  11.5 12.3 %collective-permute-start.1 = (bf16[8,128]{1,0:T(8,128)(2,1)S(1)}, bf16[8,128]{1,0:T(8,128)(2,1)S(1)}, u32[]{:S(2)}, u32[]{:S(2)}) collective-permute-start(bf16[8,128]{1,0:T(8,128)(2,1)S(1)} %get-tuple-element.18), channel_id=1, source_target_pairs={{0,4},{1,12},{2,20},{3,28},{4,36},{5,44},{6,52},{7,60},{8,68},{9,7... | collective-permute-start | bytes 6152 | tf_op jit(solution)/shard_map/ppermute | solution.py:308
  18.0 6.5 %collective-permute-start = (bf16[8,128]{1,0:T(8,128)(2,1)S(1)}, bf16[8,128]{1,0:T(8,128)(2,1)S(1)}, u32[]{:S(2)}, u32[]{:S(2)}) collective-permute-start(bf16[8,128]{1,0:T(8,128)(2,1)S(1)} %get-tuple-element.19), channel_id=1, source_target_pairs={{0,0},{1,8},{2,16},{3,24},{4,32},{5,40},{6,48},{7,56},{8,64},{9,72... | collective-permute-start | bytes 6152 | tf_op jit(solution)/shard_map/ppermute | solution.py:307
  24.5 2.2 %collective-permute-start.2 = (bf16[8,8,5760]{2,1,0:T(8,128)(2,1)S(1)}, bf16[8,8,5760]{2,1,0:T(8,128)(2,1)S(1)}, u32[]{:S(2)}, u32[]{:S(2)}) collective-permute-start(bf16[8,8,5760]{2,1,0:T(8,128)(2,1)S(1)} %all-to-all-done.own_in), channel_id=1, source_target_pairs={{0,1},{1,0},{2,3},{3,2},{4,5},{5,4},{6,7},{7,6},{8,9},{9,8},{10,11... | collective-permute-start | bytes 2211848 | tf_op jit(solution)/shard_map/ppermute | solution.py:311
  84.7 2.0 %collective-permute-start.3 = (bf16[8,8,4096]{2,1,0:T(8,128)(2,1)S(1)}, bf16[8,8,4096]{2,1,0:T(8,128)(2,1)S(1)}, u32[]{:S(2)}, u32[]{:S(2)}) collective-permute-start(bf16[8,8,4096]{2,1,0:T(8,128)(2,1)S(1)} %get-tuple-element.14), channel_id=1, source_target_pairs={{0,1},{1,0},{2,3},{3,2},{4,5},{5,4},{6,7},{7,6},{8,9},{9,8},{10,11... | collective-permute-start | bytes 1572872 | tf_op jit(solution)/shard_map/ppermute | solution.py:330
  87.6 20.6 %all-to-all-start.1 = ((bf16[8,8,4096]{2,1,0:T(8,128)(2,1)}), bf16[8,8,4096]{2,1,0:T(8,128)(2,1)S(1)}, u32[]{:S(2)}, u32[]{:S(2)}) async-start(bf16[8,8,4096]{2,1,0:T(8,128)(2,1)} %add_convert_fusion), calls=%async_computation.1 | async-start | bytes 1048576 | tf_op jit(solution)/shard_map/all_to_all | solution.py:336
  95.3 10.2 %collective-permute-start.5 = (f32[8,128]{1,0:T(8,128)S(1)}, f32[8,128]{1,0:T(8,128)S(1)}, u32[]{:S(2)}, u32[]{:S(2)}) collective-permute-start(f32[8,128]{1,0:T(8,128)S(1)} %get-tuple-element.20), channel_id=1, source_target_pairs={{0,0},{8,1},{16,2},{24,3},{32,4},{40,5},{48,6},{56,7},{64,8},{72,9... | collective-permute-start | bytes 12296 | tf_op jit(solution)/shard_map/ppermute | solution.py:334
  97.2 10.4 %collective-permute-start.4 = (f32[8,128]{1,0:T(8,128)S(1)}, f32[8,128]{1,0:T(8,128)S(1)}, u32[]{:S(2)}, u32[]{:S(2)}) collective-permute-start(f32[8,128]{1,0:T(8,128)S(1)} %get-tuple-element.17), channel_id=1, source_target_pairs={{4,0},{12,1},{20,2},{28,3},{36,4},{44,5},{52,6},{60,7},{68,8},{76,... | collective-permute-start | bytes 12296 | tf_op jit(solution)/shard_map/ppermute | solution.py:340
